TPU v7x, 256 devices: a whole 4x4x8 slice. The times are simulated.
256 devices in a mesh: sub: 16 (over z, core), row: 16 (over y, x).
Axes of the slice: x: 4, y: 4, z: 8, core: 2. Of those that a mesh axis runs over, the one named last changes fastest.
Arguments:
- modes: float32 [196608, 64], P(('sub', 'row')), may hold values from -6 to 6
- search: float32 [196608, 64], P(('sub', 'row')), may hold values from -6 to 6
- precond: float32 [196608], P(('sub', 'row')), may hold values from 0.05 to 0.25
- in_row: int32 [16, 16, 96], P('sub', 'row'), may hold values from 0 to 11, as said below
- in_col: int32 [16, 16, 96], P('sub', 'row'), may hold values from 0 to 191, as said below
- in_val: bfloat16 [16, 16, 96, 64, 64], P('sub', 'row'), as said below
- bnd_rows: int32 [16, 16, 3], P('sub', 'row'), may hold values from 0 to 11, as said below
- if_row: int32 [16, 16, 12], P('sub', 'row'), may hold values from 0 to 11, as said below
- if_src: int32 [16, 16, 12], P('sub', 'row'), may hold values from 0 to 47, as said below
- if_val: bfloat16 [16, 16, 12, 64, 64], P('sub', 'row')
Outputs:
- modes_out: float32 [196608, 64], P(('sub', 'row'))
- search_out: float32 [196608, 64], P(('sub', 'row'))
Inputs may be any that keep to these rules, and one draw needn't show every extreme that they name: `in_row`: entry k < 12 is k; each later group of 12 entries names each of the device's block-rows once. `in_col`: entry k < 12 is r * 12 + k on device (s, r); in each later group of 12 entries the devices of a subdomain together name each of its 192 block-rows once, and no entry names its own block-row. `in_val`: the first 12 blocks of every device are symmetric; the operator A is symmetric positive definite. `bnd_rows`: distinct within a device. `if_row`: each of the device's 12 block-rows once. `if_src`: t * 3 + q with t never the device's own subdomain; among the devices with one index of row, each boundary slot of each subdomain is named exactly 4 times.
All inputs are finite; a program needn't handle non-finite values.
Results may differ from a plain program's by a relative error of at most 0.0006.
Values may be sent and summed in bfloat16 or wider, within the bound.
A program may use at most 128 MiB of HBM per device.

v0:
```python
import jax
import jax.numpy as jnp
from jax import lax
from jax.sharding import PartitionSpec as P

KB = 64
LB = 12
ITERS = 2
IFR = 3


precise_mode = lax.Precision.HIGHEST


def gram_product(left, right):
    return jnp.dot(left.T, right, precision=precise_mode, preferred_element_type=jnp.float32)


def full_dot(left, right):
    return jnp.dot(left, right, precision=precise_mode, preferred_element_type=jnp.float32)


def chol_solve(matrix, rhs):
    factor = jnp.linalg.cholesky(matrix)
    halfway = lax.linalg.triangular_solve(factor, rhs, left_side=True, lower=True)
    return lax.linalg.triangular_solve(
        factor, halfway, left_side=True, lower=True, transpose_a=True
    )


def rescale(factor, moved):
    return lax.linalg.triangular_solve(factor, moved, left_side=False, lower=True, transpose_a=True)


def project(current, image_x):
    return lax.psum(
        (gram_product(current, current), gram_product(current, image_x)), ("sub", "row")
    )


def apply_blocks(vector, blocks):
    rows_here, cols_here, vals_here, bnd_here, face_rows, face_src, face_vals = blocks
    width = vector.shape[1]
    mine = vector.reshape(LB, KB, width)
    local_ids = jnp.arange(LB, dtype=jnp.int32)
    position = lax.axis_index("row")
    group = lax.all_gather(vector, "row", axis=0, tiled=True).reshape(-1, KB, width)
    forward = jnp.einsum("kij,kjw->kiw", vals_here, group[cols_here], precision=precise_mode)
    select = (rows_here[:, None] == local_ids[None, :]).astype(jnp.float32)
    result = jnp.einsum("ka,kiw->aiw", select, forward, precision=precise_mode)
    backward = jnp.einsum("kji,kjw->kiw", vals_here, mine[rows_here], precision=precise_mode)
    keeper = (cols_here != position * LB + rows_here).astype(jnp.float32)
    backward = backward * keeper[:, None, None]
    wanted = jnp.arange(LB * KB * lax.axis_size("row") // KB, dtype=jnp.int32)
    chosen = (cols_here[None, :] == wanted[:, None]).astype(jnp.float32)
    returned = lax.psum_scatter(
        jnp.einsum("bk,kiw->biw", chosen, backward, precision=precise_mode).reshape(
            LB * KB * lax.axis_size("row"), width
        ),
        "row",
        scatter_dimension=0,
        tiled=True,
    )
    result = result + returned.reshape(LB, KB, width)
    boundary = mine[bnd_here].reshape(-1, width)
    remote = lax.all_gather(boundary, "sub", axis=0, tiled=True).reshape(-1, KB, width)
    forward = jnp.einsum("kij,kjw->kiw", face_vals, remote[face_src], precision=precise_mode)
    face_select = (face_rows[:, None] == local_ids[None, :]).astype(jnp.float32)
    result = result + jnp.einsum("ka,kiw->aiw", face_select, forward, precision=precise_mode)
    backward = jnp.einsum("kji,kjw->kiw", face_vals, mine[face_rows], precision=precise_mode)
    wanted = jnp.arange(IFR * KB * lax.axis_size("sub") // KB, dtype=jnp.int32)
    chosen = (face_src[None, :] == wanted[:, None]).astype(jnp.float32)
    landed = lax.psum_scatter(
        jnp.einsum("bk,kiw->biw", chosen, backward, precision=precise_mode).reshape(
            IFR * KB * lax.axis_size("sub"), width
        ),
        "sub",
        scatter_dimension=0,
        tiled=True,
    ).reshape(IFR, KB, width)
    placed = (bnd_here[:, None] == local_ids[None, :]).astype(jnp.float32)
    result = result + jnp.einsum("qa,qiw->aiw", placed, landed, precision=precise_mode)
    return result.reshape(LB * KB, width)


def local(modes, search, precond, in_row, in_col, in_val, bnd_rows, if_row, if_src, if_val):
    blocks = (
        in_row[0, 0],
        in_col[0, 0],
        in_val[0, 0].astype(jnp.float32),
        bnd_rows[0, 0],
        if_row[0, 0],
        if_src[0, 0],
        if_val[0, 0].astype(jnp.float32),
    )
    total_rows = modes.shape[0] * lax.axis_size("sub") * lax.axis_size("row")
    nmode = modes.shape[1]
    images = apply_blocks(jnp.concatenate([modes, search], 1), blocks)
    current, direction = (modes, search)
    image_x, image_p = (images[:, :nmode], images[:, nmode:])
    for sweep in range(ITERS):
        correlation, energy = project(current, image_x)
        ritz = chol_solve(correlation, energy)
        residue = image_x - full_dot(current, ritz)
        update = precond[:, None] * residue
        image_w = apply_blocks(update, blocks)
        basis = jnp.concatenate([update, direction], 1)
        image_b = jnp.concatenate([image_w, image_p], 1)
        coupled, driving = lax.psum(
            (gram_product(basis, image_b), gram_product(basis, image_x)), ("sub", "row")
        )
        coeffs = -chol_solve(coupled, driving)
        step_x = full_dot(basis, coeffs)
        step_a = full_dot(image_b, coeffs)
        moved = current + step_x
        moved_image = image_x + step_a
        lengths = lax.psum(gram_product(moved, moved), ("sub", "row"))
        factor = jnp.linalg.cholesky(lengths / total_rows)
        current = rescale(factor, moved)
        image_x = rescale(factor, moved_image)
        direction = rescale(factor, step_x)
        image_p = rescale(factor, step_a)
    return (current, direction)


def solution(mesh):
    return jax.shard_map(
        local,
        mesh=mesh,
        in_specs=(
            P(("sub", "row"), None),
            P(("sub", "row"), None),
            P(("sub", "row")),
            P("sub", "row", None),
            P("sub", "row", None),
            P("sub", "row", None, None, None),
            P("sub", "row", None),
            P("sub", "row", None),
            P("sub", "row", None),
            P("sub", "row", None, None, None),
        ),
        out_specs=(P(("sub", "row"), None), P(("sub", "row"), None)),
        check_vma=False,
    )
```

profile of v0, /device:TPU:1, one launch (start us, length us, event | category | flops | bytes accessed | tf_op | source)
XLA Modules:
  0.0 1590.2 jit_solution(9537704448237477838)
XLA Ops:
  19.6 2.8 copy.144
  22.4 3.7 multiply_bitcast_fusion.2
  26.2 4.6 fusion
  30.8 6.3 copy.146
  37.1 10.1 reduce-scatter.19.cloned.1.call-start
  47.2 3.3 copy.142
  51.6 3.5 all-gather.9.cloned.1.call-done
  57.4 53.9 %reduce-scatter.13.cloned.1.call-done = f32[192,128]{1,0:T(8,128)} async-done(((f32[3072,128]{1,0:T(8,128)}), f32[192,128]{1,0:T(8,128)}) %reduce-scatter.13.cloned.1.call-update) | async-done | bytes 98320 | tf_op jit(solution)/shard_map/reduce_scatter | solution.py:73
  112.7 68.9 %all-gather.7.cloned.1.call-done = f32[12288,128]{1,0:T(8,128)} async-done(((f32[768,128]{1,0:T(8,128)}), f32[12288,128]{1,0:T(8,128)}) %all-gather.7.cloned.1.call-update) | async-done | bytes 6291472 | tf_op jit(solution)/shard_map/all_gather | solution.py:47
  181.7 5.2 gather_fusion
  186.9 5.3 convolution_bitcast_fusion.2
  192.2 78.6 %reduce-scatter.11.cloned.1.call-done = f32[768,128]{1,0:T(8,128)} async-done(((f32[12288,128]{1,0:T(8,128)}), f32[768,128]{1,0:T(8,128)}) %reduce-scatter.11.cloned.1.call-update) | async-done | bytes 393232 | tf_op jit(solution)/shard_map/reduce_scatter | solution.py:56
  270.8 4.8 fusion.7
  277.3 76.9 %all-reduce.1 = (f32[64,64]{0,1:T(8,128)S(1)}, f32[64,64]{0,1:T(8,128)S(1)}) all-reduce(f32[64,64]{0,1:T(8,128)S(1)} %convolution_bitcast_fusion.16, f32[64,64]{0,1:T(8,128)} %fusion.130), channel_id=1, replica_groups=mesh['sub'=16,'row'=16] {'sub','row'}, use_global_device_ids=true, to_apply=%region_5.0 | all-reduce | flops 8192 | bytes 65536 | tf_op jit(solution)/shard_map/psum | solution.py:36
  354.3 5.8 cholesky.116
  361.5 4.9 custom-call.29
  371.9 2.7 fusion.15
  374.6 3.1 copy.246
  378.6 2.6 gather_fusion.6
  381.2 6.5 multiply_bitcast_fusion.1
  387.7 4.7 copy.164
  392.4 5.5 fusion.44
  397.9 6.3 copy.165
  404.2 5.9 reshape.293
  411.0 21.9 %all-gather = f32[16,192,64]{1,2,0:T(8,128)} all-gather(f32[1,192,64]{1,2,0:T(8,128)S(1)} %copy.168), channel_id=1, replica_groups=mesh['sub'=16,'row'=16] {'sub'}, dimensions={0}, use_global_device_ids=true | all-gather | bytes 835584 | tf_op jit(solution)/shard_map/all_gather | solution.py:66
  432.9 2.9 copy.234
  441.7 45.4 %all-gather.11.cloned.1.call-done = f32[12288,64]{0,1:T(8,128)} async-done(((f32[768,64]{0,1:T(8,128)}), f32[12288,64]{0,1:T(8,128)}) %all-gather.11.cloned.1.call-update) | async-done | bytes 3145744 | tf_op jit(solution)/shard_map/all_gather | solution.py:47
  487.1 5.8 copy.233
  492.8 5.3 gather_fusion.5
  498.1 6.2 convolution_bitcast_fusion.1
  504.3 4.7 copy.160
  509.0 60.1 %reduce-scatter.15.cloned.1.call-done = f32[768,64]{0,1:T(8,128)} async-done(((f32[12288,64]{0,1:T(8,128)}), f32[768,64]{0,1:T(8,128)}) %reduce-scatter.15.cloned.1.call-update) | async-done | bytes 196624 | tf_op jit(solution)/shard_map/reduce_scatter | solution.py:56
  573.2 4.3 convolution_add_fusion.4
  582.2 77.9 %psum.73 = f32[128,64]{0,1:T(8,128)S(1)} all-reduce(f32[128,64]{0,1:T(8,128)} %fusion.27), channel_id=1, replica_groups=mesh['sub'=16,'row'=16] {'sub','row'}, use_global_device_ids=true, to_apply=%region_11.16 | all-reduce | flops 8192 | bytes 65536 | tf_op jit(solution)/shard_map/psum | solution.py:109
  660.1 160.0 %all-reduce.5.cloned.1.call-done = f32[128,128]{0,1:T(8,128)} async-done(((f32[128,128]{0,1:T(8,128)}), f32[128,128]{0,1:T(8,128)}) %all-reduce.5.cloned.1.call-update) | async-done | bytes 65552 | tf_op jit(solution)/shard_map/psum | solution.py:109
  821.9 11.7 cholesky.127
  835.0 9.8 custom-call.31
  847.9 74.6 %psum.74 = f32[64,64]{0,1:T(8,128)S(1)} all-reduce(f32[64,64]{0,1:T(8,128)S(1)} %fusion.131), channel_id=1, replica_groups=mesh['sub'=16,'row'=16] {'sub','row'}, use_global_device_ids=true, to_apply=%region_12.19 | all-reduce | flops 4096 | bytes 32768 | tf_op jit(solution)/shard_map/psum | solution.py:117
  922.5 5.8 cholesky.138
  929.7 4.9 custom-call.32
  937.1 74.2 %all-reduce = (f32[64,64]{1,0:T(8,128)S(1)}, f32[64,64]{0,1:T(8,128)S(1)}) all-reduce(f32[64,64]{1,0:T(8,128)S(1)} %fusion.133, f32[64,64]{0,1:T(8,128)S(1)} %fusion.132), channel_id=1, replica_groups=mesh['sub'=16,'row'=16] {'sub','row'}, use_global_device_ids=true, to_apply=%region_14.22 | all-reduce | flops 8192 | bytes 65536 | tf_op jit(solution)/shard_map/psum | solution.py:36
  1011.3 5.8 cholesky.149
  1018.5 4.9 custom-call.35
  1027.7 3.1 copy.250
  1034.0 6.6 multiply_bitcast_fusion
  1040.6 4.7 copy.194
  1045.2 5.5 fusion.43
  1050.7 6.3 copy.195
  1057.0 5.9 reshape.302
  1063.8 19.7 %all-gather.1 = f32[16,192,64]{1,2,0:T(8,128)S(1)} all-gather(f32[1,192,64]{1,2,0:T(8,128)S(1)} %copy.198), channel_id=1, replica_groups=mesh['sub'=16,'row'=16] {'sub'}, dimensions={0}, use_global_device_ids=true | all-gather | bytes 835584 | tf_op jit(solution)/shard_map/all_gather | solution.py:66
  1091.1 47.1 %all-gather.13.cloned.1.call-done = f32[12288,64]{0,1:T(8,128)} async-done(((f32[768,64]{0,1:T(8,128)}), f32[12288,64]{0,1:T(8,128)}) %all-gather.13.cloned.1.call-update) | async-done | bytes 3145744 | tf_op jit(solution)/shard_map/all_gather | solution.py:47
  1138.2 5.8 copy.237
  1143.9 5.3 gather_fusion.10
  1149.2 6.2 convolution_bitcast_fusion
  1155.4 4.7 copy.190
  1160.1 60.5 %reduce-scatter.17.cloned.1.call-done = f32[768,64]{0,1:T(8,128)} async-done(((f32[12288,64]{0,1:T(8,128)}), f32[768,64]{0,1:T(8,128)}) %reduce-scatter.17.cloned.1.call-update) | async-done | bytes 196624 | tf_op jit(solution)/shard_map/reduce_scatter | solution.py:56
  1222.8 4.3 convolution_add_fusion.3
  1229.7 77.7 %psum.78 = f32[128,64]{0,1:T(8,128)S(1)} all-reduce(f32[128,64]{0,1:T(8,128)S(1)} %fusion.25), channel_id=1, replica_groups=mesh['sub'=16,'row'=16] {'sub','row'}, use_global_device_ids=true, to_apply=%region_18.26 | all-reduce | flops 8192 | bytes 65536 | tf_op jit(solution)/shard_map/psum | solution.py:109
  1307.4 161.1 %all-reduce.7.cloned.1.call-done = f32[128,128]{0,1:T(8,128)} async-done(((f32[128,128]{0,1:T(8,128)}), f32[128,128]{0,1:T(8,128)}) %all-reduce.7.cloned.1.call-update) | async-done | bytes 65552 | tf_op jit(solution)/shard_map/psum | solution.py:109
  1470.3 11.7 cholesky.160
  1483.4 9.8 custom-call.39
  1494.3 74.6 %psum.79 = f32[64,64]{0,1:T(8,128)S(1)} all-reduce(f32[64,64]{0,1:T(8,128)S(1)} %fusion.134), channel_id=1, replica_groups=mesh['sub'=16,'row'=16] {'sub','row'}, use_global_device_ids=true, to_apply=%region_19.27 | all-reduce | flops 4096 | bytes 32768 | tf_op jit(solution)/shard_map/psum | solution.py:117
  1569.0 5.8 cholesky.171
  1576.1 4.9 custom-call.40
  (205 shorter events, 81.2 us)
Async XLA Ops:
  7.2 5.7 copy-start
  7.2 6.1 copy-start.24
  7.2 47.9 %all-gather.9.cloned.1.call-start = ((), (), s32[]{:S(2)}) async-start(), calls=%async_computation.8 | async-start | bytes 1671168 | tf_op jit(solution)/shard_map/all_gather | solution.py:66
  10.1 5.7 copy-start.19
  10.3 5.5 copy-start.1
  11.5 99.8 %reduce-scatter.13.cloned.1.call-start = ((), (), s32[]{:S(2)}) async-start(), calls=%async_computation.9 | async-start | bytes 1671168 | tf_op jit(solution)/shard_map/reduce_scatter | solution.py:73
  12.3 3.6 copy-start.22
  13.2 3.8 copy-start.18
  15.8 1.2 copy-start.2
  15.9 165.8 %all-gather.7.cloned.1.call-start = ((), (), s32[]{:S(2)}) async-start(), calls=%async_computation.6 | async-start | bytes 6684672 | tf_op jit(solution)/shard_map/all_gather | solution.py:47
  16.6 254.2 %reduce-scatter.11.cloned.1.call-start = ((), (), s32[]{:S(2)}) async-start(), calls=%async_computation.7 | async-start | bytes 6684672 | tf_op jit(solution)/shard_map/reduce_scatter | solution.py:56
  17.1 2.5 copy-start.21
  17.1 2.5 copy-start.8
  17.1 5.3 copy-start.16
  37.1 13.5 copy-start.3
  37.1 74.2 %copy-start.29 = (s32[1,1,3]{2,1,0:T(1,128)S(1)}, s32[1,1,3]{2,1,0:T(1,128)}, u32[]{:S(2)}) copy-start(s32[1,1,3]{2,1,0:T(1,128)} %param.28) | copy-start | bytes 40
  37.1 402.3 %reduce-scatter.19.cloned.1.call-start = ((), (), s32[]{:S(2)}) async-start(), calls=%async_computation.16 | async-start | bytes 1671168 | tf_op jit(solution)/shard_map/reduce_scatter | solution.py:73
  50.6 136.3 %copy-start.20 = (s32[1024]{0:T(1024)}, s32[1024]{0:T(1024)S(1)}, u32[]{:S(2)}) copy-start(s32[1024]{0:T(1024)S(1)} %pad_clamp_fusion.4) | copy-start | bytes 12292
  50.6 4.4 copy-start.23
  192.2 83.4 %copy-start.26 = (s32[1,1,12]{2,1,0:T(1,128)S(1)}, s32[1,1,12]{2,1,0:T(1,128)}, u32[]{:S(2)}) copy-start(s32[1,1,12]{2,1,0:T(1,128)} %param.29) | copy-start | bytes 148
  275.6 92.0 %copy-start.17 = (f32[768]{0:T(1024)S(1)}, f32[768]{0:T(1024)}, u32[]{:S(2)}) copy-start(f32[768]{0:T(1024)} %param.24) | copy-start | bytes 9220
  367.6 10.2 copy-start.13
  368.8 9.0 copy-start.4
  377.8 109.3 %all-gather.11.cloned.1.call-start = ((), (), s32[]{:S(2)}) async-start(), calls=%async_computation.10 | async-start | bytes 3342336 | tf_op jit(solution)/shard_map/all_gather | solution.py:47
  378.4 190.8 %reduce-scatter.15.cloned.1.call-start = ((), (), s32[]{:S(2)}) async-start(), calls=%async_computation.11 | async-start | bytes 3342336 | tf_op jit(solution)/shard_map/reduce_scatter | solution.py:56
  410.2 410.0 %all-reduce.5.cloned.1.call-start = ((), (), s32[]{:S(2)}) async-start(), calls=%async_computation.12 | async-start | bytes 131072 | tf_op jit(solution)/shard_map/psum | solution.py:109
  509.0 68.4 %copy-start.27 = (s32[1,1,12]{2,1,0:T(1,128)S(1)}, s32[1,1,12]{2,1,0:T(1,128)}, u32[]{:S(2)}) copy-start(s32[1,1,12]{2,1,0:T(1,128)} %param.29) | copy-start | bytes 148
  573.2 6.0 copy-start.5
  573.2 6.0 copy-start.11
  580.8 508.1 %reduce-scatter.21.cloned.1.call-start = ((), (), s32[]{:S(2)}) async-start(), calls=%async_computation.17 | async-start | bytes 1671168 | tf_op jit(solution)/shard_map/reduce_scatter | solution.py:73
  847.6 178.0 %copy-start.25 = (s32[1,1,12]{2,1,0:T(1,128)S(1)}, s32[1,1,12]{2,1,0:T(1,128)}, u32[]{:S(2)}) copy-start(s32[1,1,12]{2,1,0:T(1,128)} %param.30) | copy-start | bytes 148
  936.4 87.8 %copy-start.9 = (f32[768,64]{0,1:T(8,128)}, f32[768,64]{0,1:T(8,128)S(1)}, u32[]{:S(2)}) copy-start(f32[768,64]{0,1:T(8,128)S(1)} %convolution_bitcast_fusion.13) | copy-start | bytes 589828
  1024.2 6.6 copy-start.6
  1030.8 107.3 %all-gather.13.cloned.1.call-start = ((), (), s32[]{:S(2)}) async-start(), calls=%async_computation.13 | async-start | bytes 3342336 | tf_op jit(solution)/shard_map/all_gather | solution.py:47
  1031.4 189.3 %reduce-scatter.17.cloned.1.call-start = ((), (), s32[]{:S(2)}) async-start(), calls=%async_computation.14 | async-start | bytes 3342336 | tf_op jit(solution)/shard_map/reduce_scatter | solution.py:56
  1063.0 405.5 %all-reduce.7.cloned.1.call-start = ((), (), s32[]{:S(2)}) async-start(), calls=%async_computation.15 | async-start | bytes 131072 | tf_op jit(solution)/shard_map/psum | solution.py:109
  1063.8 24.2 %copy-start.14 = (f32[768,64]{0,1:T(8,128)S(1)}, f32[768,64]{0,1:T(8,128)}, u32[]{:S(2)}) copy-start(f32[768,64]{0,1:T(8,128)} %fusion.42) | copy-start | bytes 589828
  1083.5 4.9 copy-start.15
  1083.5 5.4 copy-start.30
  1160.1 67.0 %copy-start.12 = (f32[12,64,64]{2,0,1:T(8,128)S(1)}, f32[12,64,64]{2,0,1:T(8,128)}, u32[]{:S(2)}) copy-start(f32[12,64,64]{2,0,1:T(8,128)} %fusion.36) | copy-start | bytes 589828
  1160.1 67.0 %copy-start.28 = (s32[1,1,12]{2,1,0:T(1,128)S(1)}, s32[1,1,12]{2,1,0:T(1,128)}, u32[]{:S(2)}) copy-start(s32[1,1,12]{2,1,0:T(1,128)} %param.29) | copy-start | bytes 148
  1222.8 5.2 copy-start.7
  1227.1 2.0 copy-start.10
Sparse Core Ops, SparseCore 0:
  11.7 43.3 all-gather.8
  57.6 53.6 reduce-scatter.12
  114.0 67.5 all-gather.6
  185.7 85.0 reduce-scatter.10
  377.9 52.2 reduce-scatter.18
  433.1 53.9 all-gather.10
  490.7 78.4 reduce-scatter.14
  580.9 239.2 all-reduce.4
  1030.9 50.4 reduce-scatter.20
  1084.0 54.0 all-gather.12
  1142.2 78.3 reduce-scatter.16
  1229.3 239.1 all-reduce.6
where the time goes:
time: 1590 us
  waiting for transfers between devices  741 us (47%)
  blocking collectives  497 us (31%)
  local copies, waits for them, and re-layouts  128 us (8%)
  matrix products  100 us (6%)
  other arithmetic  97.2 us (6%)
    psum x2, waiting for transfers between devices, local(): lax.psum((gram_product(basis, image_b), gram_product(basis, image_x)), ('...  321 us
    reduce_scatter x6, waiting for transfers between devices, apply_blocks(): lax.psum_scatter(jnp.einsum('bk,kiw->biw', chosen, backward, precision=pr...  253 us
    all_gather x3, waiting for transfers between devices, apply_blocks(): lax.all_gather(vector, 'row', axis=0, tiled=True).reshape(-1, KB, width)  161 us
    psum x2, blocking collectives, local(): lax.psum((gram_product(basis, image_b), gram_product(basis, image_x)), ('...  156 us
    psum x2, blocking collectives, project(): lax.psum((gram_product(current, current), gram_product(current, image_x))...  151 us
    psum x2, blocking collectives, local(): lengths = lax.psum(gram_product(moved, moved), ('sub', 'row'))  149 us
    all_gather x2, blocking collectives, apply_blocks(): lax.all_gather(boundary, 'sub', axis=0, tiled=True).reshape(-1, KB, width)  41.6 us
    another operation x12, other arithmetic, chol_solve(): factor = jnp.linalg.cholesky(matrix)  37.8 us
  transfers between devices with their start and end apart: 12, of which 10 were waited for; matrix products, arithmetic and copies ran while one was open for 11% of the time, Pallas kernels for 0%

commit v1 on v0

v1 whole, which is shorter than its diff:
```python
import functools

import jax
import jax.numpy as jnp
from jax import lax
from jax.experimental import pallas as pl
from jax.experimental.pallas import tpu as pltpu
from jax.sharding import PartitionSpec as P

KB = 64
LB = 12
IFR = 3
ITERS = 2
GROUPS = 8
LANES = 128
MESH = pl.DeviceIdType.MESH
F32, BF16 = jnp.float32, jnp.bfloat16
VMEM = pl.BlockSpec(memory_space=pltpu.VMEM)
SMEM = pl.BlockSpec(memory_space=pltpu.SMEM)
ANY = pl.BlockSpec(memory_space=pl.ANY)
LIMIT = 56 * 1024 * 1024


def hdot(a, b):
    return jnp.dot(a, b, precision=lax.Precision.HIGHEST, preferred_element_type=F32)


def swap(v):
    return pltpu.roll(v, LANES // 2, 1)


def is_left(shape):
    return lax.broadcasted_iota(jnp.int32, shape, 1) < LANES // 2


def split3(v):
    hi = v.astype(BF16).astype(F32)
    rest = v - hi
    mid = rest.astype(BF16).astype(F32)
    return hi, mid, (rest - mid).astype(BF16).astype(F32)


def pack(block):
    half = KB // 2
    left = is_left((half, LANES))
    return jnp.where(left, block[:half], swap(block[half:]))


def terms_of(block, width):
    hi, mid, lo = split3(block)
    if width == LANES:
        return jnp.concatenate([hi, mid, lo], 1).astype(BF16)
    left = is_left((KB, LANES))
    return jnp.concatenate(
        [jnp.where(left, hi, swap(mid)), jnp.where(left, lo, 0.0)], 1
    ).astype(BF16)


def sum_terms(total, width):
    if width == LANES:
        return total[:, :LANES] + (total[:, LANES : 2 * LANES] + total[:, 2 * LANES :])
    both = total[:, :LANES] + total[:, LANES:]
    return both + swap(both)


def store_terms(packed, ref, at, width):
    if width == LANES:
        ref[at] = terms_of(packed, width)
        return
    half = KB // 2
    hi, mid, lo = split3(packed)
    left = is_left((half, LANES))
    ref[at, :half, :LANES] = jnp.where(left, hi, swap(mid)).astype(BF16)
    ref[at, :half, LANES:] = jnp.where(left, lo, 0.0).astype(BF16)
    ref[at, half:, :LANES] = jnp.where(left, swap(hi), mid).astype(BF16)
    ref[at, half:, LANES:] = jnp.where(left, swap(lo), 0.0).astype(BF16)


def write_messages(width, basis, out, bnd, face_row, face_src, face_val):
    n_sub = out.shape[0]

    def block_at(row):
        return basis[pl.ds(pl.multiple_of(row * KB, KB), KB), :]

    def sent(block):
        return block if width == LANES else pack(block)

    rows = [sent(block_at(bnd[q])) for q in range(IFR)]

    @pl.loop(0, n_sub)
    def _(t):
        for q in range(IFR):
            out[t, q] = rows[q]
            out[t, IFR + q] = jnp.zeros_like(rows[q])

    @pl.loop(0, LB)
    def _(k):
        terms = terms_of(block_at(face_row[k]), width)
        total = lax.dot_general(
            face_val[k],
            terms,
            (((0,), (0,)), ((), ())),
            preferred_element_type=F32,
        )
        source = face_src[k]
        target, slot = source // IFR, IFR + source % IFR
        out[target, slot] = out[target, slot] + sent(sum_terms(total, width))


def start_kernel(bnd, face_row, face_src, basis, face_val, out):
    write_messages(LANES, basis, out, bnd, face_row, face_src, face_val)


def exchange_kernel(count, ny, nx, n_sub, *refs):
    shards, messages = refs[:count], refs[count]
    groups, received = refs[count + 1 : 2 * count + 1], refs[2 * count + 1]
    local_sem, sub_send, sub_recv, row_send, row_recv = refs[2 * count + 2 :]
    sub, row = lax.axis_index("sub"), lax.axis_index("row")
    y, x = row // nx, row % nx

    def at(dy, dx):
        return ((y + dy + ny) % ny) * nx + (x + dx + nx) % nx

    barrier = pltpu.get_barrier_semaphore()
    for d in range(1, nx):
        pl.semaphore_signal(barrier, inc=1, device_id={"row": at(0, d)}, device_id_type=MESH)
    for d in range(1, ny):
        pl.semaphore_signal(barrier, inc=1, device_id={"row": at(d, 0)}, device_id_type=MESH)
    for d in range(1, n_sub):
        pl.semaphore_signal(barrier, inc=1, device_id={"sub": (sub + d) % n_sub}, device_id_type=MESH)
    pl.semaphore_wait(barrier, nx - 1 + ny - 1 + n_sub - 1)

    own = [pltpu.make_async_copy(shards[i], groups[i].at[row], local_sem.at[i]) for i in range(count)]
    own.append(pltpu.make_async_copy(messages.at[sub], received.at[sub], local_sem.at[count]))

    def hop(i, half, holder, src, to, sem):
        size = shards[i].shape[0] // 2
        return pltpu.make_async_remote_copy(
            src_ref=src,
            dst_ref=groups[i].at[holder, pl.ds(half * size, size)],
            send_sem=row_send.at[i, half, sem],
            recv_sem=row_recv.at[i, half, sem],
            device_id={"row": to},
            device_id_type=MESH,
        )

    def half_of(i, half, holder=None):
        size = shards[i].shape[0] // 2
        part = pl.ds(half * size, size)
        return shards[i].at[part] if holder is None else groups[i].at[holder, part]

    counts = ((nx, ny), (ny, nx))

    def place(half, first, second):
        return at(second, first) if half == 0 else at(first, second)

    sends = []
    for i in range(count):
        for half in range(2):
            n1, n2 = counts[half]
            for first in range(1, n1):
                sends.append(hop(i, half, row, half_of(i, half), place(half, first, 0), first * n2))
                sends[-1].start()
        for half in range(2):
            n1, n2 = counts[half]
            for second in range(1, n2):
                sends.append(hop(i, half, row, half_of(i, half), place(half, 0, second), second))
                sends[-1].start()

    def message(d):
        t = (sub + d) % n_sub
        return pltpu.make_async_remote_copy(
            src_ref=messages.at[t],
            dst_ref=received.at[sub],
            send_sem=sub_send.at[d],
            recv_sem=sub_recv.at[d],
            device_id={"sub": t},
            device_id_type=MESH,
        )

    @pl.loop(1, n_sub)
    def _(d):
        message(d).start()

    for copy in own:
        copy.start()

    def arrived(i, half, holder, sem):
        here = half_of(i, half, holder)
        pltpu.make_async_copy(here, here, row_recv.at[i, half, sem]).wait()

    for i in range(count):
        for first in range(1, max(nx, ny)):
            for half in range(2):
                n1, n2 = counts[half]
                if first >= n1:
                    continue
                holder = place(half, -first, 0)
                arrived(i, half, holder, first * n2)
                for second in range(1, n2):
                    sends.append(
                        hop(i, half, holder, half_of(i, half, holder), place(half, 0, second), first * n2 + second)
                    )
                    sends[-1].start()
    for i in range(count):
        for half in range(2):
            n1, n2 = counts[half]
            for first in range(n1):
                for second in range(1, n2):
                    arrived(i, half, place(half, -first, -second), first * n2 + second)

    @pl.loop(1, n_sub)
    def _(d):
        source = (sub + n_sub - d) % n_sub
        here = received.at[source]
        pltpu.make_async_copy(here, here, sub_recv.at[d]).wait()
        message(d).wait_send()

    for copy in own:
        copy.wait()
    for copy in sends:
        copy.wait_send()


def exchange(collective_id, ny, nx, shards, messages):
    count, n_sub, n_row = len(shards), messages.shape[0], ny * nx
    return pl.pallas_call(
        functools.partial(exchange_kernel, count, ny, nx, n_sub),
        name=f"exchange_{collective_id}",
        out_shape=[jax.ShapeDtypeStruct((n_row, *a.shape), a.dtype) for a in shards]
        + [jax.ShapeDtypeStruct(messages.shape, F32)],
        in_specs=[ANY] * (count + 1),
        out_specs=[ANY] * (count + 1),
        scratch_shapes=[
            pltpu.SemaphoreType.DMA((count + 1,)),
            pltpu.SemaphoreType.DMA((n_sub,)),
            pltpu.SemaphoreType.DMA((n_sub,)),
            pltpu.SemaphoreType.DMA((count, 2, n_row)),
            pltpu.SemaphoreType.DMA((count, 2, n_row)),
        ],
        compiler_params=pltpu.CompilerParams(collective_id=collective_id, has_side_effects=True),
    )(*shards, messages)


def sum_kernel(n_sub, n_row, parts, out, by_row, by_sub, own_sem, send, recv):
    sub, row = lax.axis_index("sub"), lax.axis_index("row")
    barrier = pltpu.get_barrier_semaphore()

    @pl.loop(1, n_row)
    def _(d):
        pl.semaphore_signal(barrier, inc=1, device_id={"row": (row + d) % n_row}, device_id_type=MESH)

    @pl.loop(1, n_sub)
    def _(d):
        pl.semaphore_signal(barrier, inc=1, device_id={"sub": (sub + d) % n_sub}, device_id_type=MESH)

    pl.semaphore_wait(barrier, n_row - 1 + n_sub - 1)

    def phase(index, axis, mine, n, source, target):
        def to(d):
            t = (mine + d) % n
            return pltpu.make_async_remote_copy(
                src_ref=source(t),
                dst_ref=target(mine),
                send_sem=send.at[index, d],
                recv_sem=recv.at[index, d],
                device_id={axis: t},
                device_id_type=MESH,
            )

        own = pltpu.make_async_copy(source(mine), target(mine), own_sem.at[index])

        @pl.loop(1, n)
        def _(d):
            to(d).start()

        own.start()

        @pl.loop(1, n)
        def _(d):
            here = target((mine + n - d) % n)
            pltpu.make_async_copy(here, here, recv.at[index, d]).wait()
            to(d).wait_send()

        own.wait()

    def summed(buffer, n):
        total = buffer[0]
        for t in range(1, n):
            total = total + buffer[t]
        return total

    phase(0, "row", row, n_row, lambda t: parts.at[t], lambda t: by_row.at[t])
    by_row[n_row] = summed(by_row, n_row)
    phase(1, "sub", sub, n_sub, lambda t: by_row.at[n_row], lambda t: by_sub.at[t])
    by_sub[n_sub] = summed(by_sub, n_sub)
    phase(2, "row", row, n_row, lambda t: by_sub.at[n_sub], lambda t: out.at[t])


def sum_all(collective_id, n_sub, n_row, part):
    rows = part.shape[0] // n_row
    most = max(n_sub, n_row)
    shape = (n_row, rows, LANES)
    total = pl.pallas_call(
        functools.partial(sum_kernel, n_sub, n_row),
        name=f"sum_{collective_id}",
        out_shape=jax.ShapeDtypeStruct(shape, F32),
        in_specs=[VMEM],
        out_specs=VMEM,
        scratch_shapes=[
            pltpu.VMEM((n_row + 1, rows, LANES), F32),
            pltpu.VMEM((n_sub + 1, rows, LANES), F32),
            pltpu.SemaphoreType.DMA((3,)),
            pltpu.SemaphoreType.DMA((3, most)),
            pltpu.SemaphoreType.DMA((3, most)),
        ],
        compiler_params=pltpu.CompilerParams(collective_id=collective_id, has_side_effects=True),
    )(part.reshape(shape))
    return total.reshape(part.shape)


def build_kernel(own_at, back_at, face_at, own_val, all_val, face_val, rows_ref):
    half = KB // 2
    left = is_left((half, LANES))

    def pair(one, two):
        top = jnp.where(left, one, swap(two))
        low = jnp.where(left, swap(one), two)
        return jnp.concatenate([top, low], 0)

    def put(a, slot, value):
        rows_ref[a, :, slot * LANES : (slot + 1) * LANES] = value.astype(BF16)

    @pl.loop(0, LB)
    def _(a):
        for g in range(0, GROUPS, 2):
            one, two = (own_val[own_at[a * GROUPS + g + i]].astype(F32) for i in range(2))
            put(a, g // 2, pair(one, two))
        back = [all_val[back_at[a * (GROUPS - 1) + g]].astype(F32) for g in range(GROUPS - 1)]
        turned = jnp.concatenate([pair(back[0], back[2]), pair(back[1], back[3])], 0).T
        put(a, 4, turned[:KB])
        put(a, 5, turned[KB:])
        turned = jnp.concatenate([pair(back[4], back[6]), pair(back[5], back[5])], 0).T
        put(a, 6, turned[:KB])
        face = face_val[face_at[a]].astype(F32)
        put(a, 7, jnp.where(is_left((KB, LANES)), turned[KB:], jnp.concatenate([face, face], 1)))


def apply_operator(width, col_at, bnd, rows_ref, group, received, terms, put_row):
    n_group, n_sub = group.shape[0], received.shape[0]

    @pl.loop(0, n_group)
    def _(j):
        store_terms(group[j], terms, j, width)

    @pl.loop(0, n_sub)
    def _(t):
        for q in range(IFR):
            store_terms(received[t, q], terms, n_group + t * IFR + q, width)

    step = 4
    slots = 2 * GROUPS

    @pl.loop(0, LB)
    def _(a):
        total = None
        for c in range(slots // step):
            stack = jnp.concatenate([terms[col_at[a * slots + c * step + i]] for i in range(step)], 0)
            part = jnp.dot(
                rows_ref[a, :, c * step * KB : (c + 1) * step * KB], stack, preferred_element_type=F32
            )
            total = part if total is None else total + part
        put_row(a, sum_terms(total, width))


def landed_block(width, received, q):
    n_sub = received.shape[0]
    total = received[0, IFR + q]
    for t in range(1, n_sub):
        total = total + received[t, IFR + q]
    if width == LANES:
        return total
    left = is_left(total.shape)
    other = swap(total)
    return jnp.concatenate([jnp.where(left, total, other), jnp.where(left, other, total)], 0)


def first_apply_kernel(col_at, bnd, rows_ref, group, received, basis, image, gram, terms):
    def put_row(a, block):
        image[pl.ds(pl.multiple_of(a * KB, KB), KB), :] = block

    apply_operator(LANES, col_at, bnd, rows_ref, group, received, terms, put_row)
    for q in range(IFR):
        at = pl.ds(pl.multiple_of(bnd[q] * KB, KB), KB)
        image[at, :] = image[at, :] + landed_block(LANES, received, q)
    both = basis[...]
    left = is_left(both.shape)
    gram[...] = hdot(both.T, jnp.where(left, both, swap(image[...])))


def apply_kernel(col_at, bnd, rows_ref, group, received, current, image_x, basis, image_b, gram, terms):
    left_block = is_left((KB, LANES))

    def put_row(a, block):
        at = pl.ds(pl.multiple_of(a * KB, KB), KB)
        image_b[at, :] = jnp.where(left_block, block, image_x[at, :])

    apply_operator(KB, col_at, bnd, rows_ref, group, received, terms, put_row)
    for q in range(IFR):
        at = pl.ds(pl.multiple_of(bnd[q] * KB, KB), KB)
        block = landed_block(KB, received, q)
        image_b[at, :] = image_b[at, :] + jnp.where(left_block, block, 0.0)
    y = basis[...]
    turned = y.T
    left = is_left(y.shape)
    gram[0:LANES] = hdot(turned, image_b[...])
    gram[LANES : 2 * LANES] = hdot(turned, jnp.where(left, image_x[...], swap(current[...])))
    gram[2 * LANES :] = hdot(turned, y)


def eliminate(work, n, full):
    shape = (n, LANES)
    lane = lax.broadcasted_iota(jnp.int32, shape, 1)
    line = lax.broadcasted_iota(jnp.int32, (n, 1), 0)
    lane1 = lax.broadcasted_iota(jnp.int32, (1, LANES), 1)

    def step(j, pivots):
        row = work[pl.ds(j, 1), :]
        pivot = jnp.sum(jnp.where(lane1 == j, row[:, :LANES], 0.0), axis=1, keepdims=True)
        whole = work[...]
        column = jnp.sum(jnp.where(lane == j, whole[:, :LANES], 0.0), axis=1, keepdims=True)
        scaled = row * (1.0 / pivot)
        if full:
            work[...] = jnp.where(line == j, scaled, whole - column * scaled)
        else:
            work[...] = whole - jnp.where(line > j, column, 0.0) * scaled
        return jnp.where(line == j, pivot, pivots)

    return lax.fori_loop(0, n, step, jnp.zeros((n, 1), F32))


def rest_of(shape):
    return is_left(shape)


def padded(top):
    return jnp.concatenate([top, jnp.zeros_like(top)], 0)


def identity_right():
    line = lax.broadcasted_iota(jnp.int32, (KB, LANES), 0)
    lane = lax.broadcasted_iota(jnp.int32, (KB, LANES), 1)
    return (lane == line + KB).astype(F32)


def identity_left():
    line = lax.broadcasted_iota(jnp.int32, (KB, LANES), 0)
    lane = lax.broadcasted_iota(jnp.int32, (KB, LANES), 1)
    return (lane == line).astype(F32)


CHUNK = 256


def chunks(body):
    @pl.loop(0, LB * KB // CHUNK)
    def _(c):
        body(pl.ds(pl.multiple_of(c * CHUNK, CHUNK), CHUNK))


def new_basis(ritz, precond, current, image_x, basis, update, at):
    here = current[at, :]
    left = is_left(here.shape)
    residue = jnp.where(left, image_x[at, :], 0.0) - hdot(here, ritz)
    fresh = precond[at, :] * residue
    update[at, :] = fresh
    basis[at, :] = jnp.where(left, fresh, here)


def send_basis(update, packed, messages, bnd, face_row, face_src, face_val):
    @pl.loop(0, LB)
    def _(a):
        packed[a] = pack(update[pl.ds(pl.multiple_of(a * KB, KB), KB), :])

    write_messages(KB, update, messages, bnd, face_row, face_src, face_val)


def first_ritz_kernel(
    bnd, face_row, face_src, gram, face_val, precond, current, image_x, basis, packed, messages, update, work
):
    work[...] = gram[:KB]
    eliminate(work, KB, True)
    left = is_left((KB, LANES))
    ritz = padded(jnp.where(left, swap(work[...]), 0.0))
    chunks(lambda at: new_basis(ritz, precond, current, image_x, basis, update, at))
    send_basis(update, packed, messages, bnd, face_row, face_src, face_val)


def combine(total_rows, gram, metric, wide, narrow):
    wide[:, :LANES] = gram[0:LANES]
    right = gram[LANES : 2 * LANES]
    wide[:, LANES:] = right
    eliminate(wide, LANES, True)
    left_all = is_left((LANES, LANES))
    left = is_left((KB, LANES))
    z = jnp.where(left_all, -wide[:, LANES:], 0.0)
    cross = hdot(right.T, z)
    against = jnp.where(left_all, swap(right), 0.0) + hdot(gram[2 * LANES :], z)
    square = hdot(z.T, against)[:KB]
    lengths = jnp.where(left, metric[...], 0.0) + cross[KB:] + square
    narrow[...] = lengths * (1.0 / total_rows) + identity_right()
    pivots = eliminate(narrow, KB, False)
    root = 1.0 / jnp.sqrt(pivots)
    inverse = padded(jnp.where(left, swap(narrow[...]), 0.0) * root)
    turned = inverse.T
    half = hdot(z, turned)
    energy = jnp.where(left, swap(metric[...]), 0.0) + cross[:KB]
    energy = hdot(hdot(inverse, padded(energy)), turned)
    return turned, jnp.where(left_all, half, swap(half)), energy


def step_kernel(
    total_rows,
    bnd,
    face_row,
    face_src,
    gram,
    metric,
    face_val,
    precond,
    current,
    image_x,
    basis,
    image_b,
    next_metric,
    next_current,
    next_image,
    next_basis,
    packed,
    messages,
    update,
    wide,
    narrow,
):
    turned, moves, energy = combine(total_rows, gram, metric, wide, narrow)
    next_metric[...] = identity_left() * total_rows + swap(energy[:KB])
    ritz = energy * (1.0 / total_rows)

    def body(at):
        next_current[at, :] = hdot(current[at, :], turned) + hdot(basis[at, :], moves)
        next_image[at, :] = hdot(image_x[at, :], turned) + hdot(image_b[at, :], moves)
        new_basis(ritz, precond, next_current, next_image, next_basis, update, at)

    chunks(body)
    send_basis(update, packed, messages, bnd, face_row, face_src, face_val)


def last_kernel(total_rows, gram, metric, current, basis, modes, search, wide, narrow):
    turned, moves, _ = combine(total_rows, gram, metric, wide, narrow)

    def body(at):
        both = hdot(current[at, :], turned) + hdot(basis[at, :], moves)
        modes[at, :] = both[:, :KB]
        search[at, :] = swap(both)[:, :KB]

    chunks(body)


def plain(kernel, name, specs, outs, scratch, *args):
    return pl.pallas_call(
        kernel,
        name=name,
        out_shape=outs,
        in_specs=specs,
        out_specs=[VMEM] * len(outs),
        scratch_shapes=scratch,
        compiler_params=pltpu.CompilerParams(vmem_limit_bytes=LIMIT),
    )(*args)


def shape(*dims):
    return jax.ShapeDtypeStruct(dims, F32)


def tables(n_row, in_row, in_col, if_row, if_src):
    row = lax.axis_index("row")
    everyone = lax.all_gather(jnp.stack([in_row, in_col]), "row")
    own_ids = jnp.arange(LB, dtype=jnp.int32)
    k_ids = jnp.arange(GROUPS * LB, dtype=jnp.int32).reshape(GROUPS, LB)
    hit = in_row.reshape(GROUPS, LB)[None] == own_ids[:, None, None]
    own_at = jnp.sum(jnp.where(hit, k_ids[None], 0), 2)
    own_col = jnp.sum(jnp.where(hit, in_col.reshape(GROUPS, LB)[None], 0), 2)
    rows_all = everyone[:, 0, LB:].reshape(n_row, GROUPS - 1, LB)
    cols_all = everyone[:, 1, LB:].reshape(n_row, GROUPS - 1, LB)
    r_ids = jnp.arange(n_row, dtype=jnp.int32)[:, None, None]
    back_hit = cols_all[None] == (row * LB + own_ids)[:, None, None, None]
    back_k = r_ids * ((GROUPS - 1) * LB) + (k_ids[1:] - LB)[None]
    back_at = jnp.sum(jnp.where(back_hit, back_k[None], 0), (1, 3))
    back_col = jnp.sum(jnp.where(back_hit, (r_ids * LB + rows_all)[None], 0), (1, 3))
    face_hit = if_row[None] == own_ids[:, None]
    face_at = jnp.sum(jnp.where(face_hit, own_ids[None], 0), 1)
    face_col = n_row * LB + jnp.sum(jnp.where(face_hit, if_src[None], 0), 1)
    col_at = jnp.concatenate([own_col, back_col, face_col[:, None]], 1)
    return own_at.reshape(-1), back_at.reshape(-1), face_at, col_at.reshape(-1)


def local(grid, modes, search, precond, in_row, in_col, in_val, bnd_rows, if_row, if_src, if_val):
    n_sub, ny, nx = grid
    n_row = ny * nx
    rows_here = LB * KB
    total_rows = float(rows_here * n_sub * n_row)
    bnd, face_row, face_src, face_val = bnd_rows[0, 0], if_row[0, 0], if_src[0, 0], if_val[0, 0]
    own_at, back_at, face_at, col_at = tables(n_row, in_row[0, 0], in_col[0, 0], face_row, face_src)
    vals = in_val[0, 0]
    half = KB // 2
    own_val = jnp.concatenate([vals[:, :half], vals[:, half:]], 2)
    weights = jnp.broadcast_to(precond[:, None], (rows_here, LANES))
    current = jnp.concatenate([modes, search], 1)

    (messages,) = plain(
        start_kernel,
        "start",
        [SMEM] * 3 + [VMEM] * 2,
        [shape(n_sub, 2 * IFR, KB, LANES)],
        [],
        bnd,
        face_row,
        face_src,
        current,
        face_val,
    )
    group, all_val, received = exchange(
        0, ny, nx, [current, own_val[LB:].reshape(-1, LANES)], messages
    )
    block_rows = pl.pallas_call(
        build_kernel,
        name="build",
        out_shape=jax.ShapeDtypeStruct((LB, KB, 2 * GROUPS * KB), BF16),
        in_specs=[SMEM] * 3 + [VMEM] * 3,
        out_specs=VMEM,
        compiler_params=pltpu.CompilerParams(vmem_limit_bytes=LIMIT),
    )(own_at, back_at, face_at, own_val, all_val.reshape(-1, half, LANES), face_val)
    blocks_all = n_row * LB + n_sub * IFR
    image_x, gram = plain(
        first_apply_kernel,
        "first_apply",
        [SMEM] * 2 + [VMEM] * 4,
        [shape(rows_here, LANES), shape(LANES, LANES)],
        [pltpu.VMEM((blocks_all, KB, 3 * LANES), BF16)],
        col_at,
        bnd,
        block_rows,
        group.reshape(-1, KB, LANES),
        received,
        current,
    )
    metric = sum_all(1, n_sub, n_row, gram)
    sent = [shape(rows_here, LANES), shape(LB, half, LANES), shape(n_sub, 2 * IFR, half, LANES)]
    basis, packed, messages = plain(
        first_ritz_kernel,
        "first_ritz",
        [SMEM] * 3 + [VMEM] * 5,
        sent,
        [pltpu.VMEM((rows_here, LANES), F32), pltpu.VMEM((KB, LANES), F32)],
        bnd,
        face_row,
        face_src,
        metric,
        face_val,
        weights,
        current,
        image_x,
    )
    metric = metric[:KB]
    for sweep in range(ITERS):
        group, received = exchange(2 + 2 * sweep, ny, nx, [packed.reshape(-1, LANES)], messages)
        image_b, gram = plain(
            apply_kernel,
            "apply",
            [SMEM] * 2 + [VMEM] * 6,
            [shape(rows_here, LANES), shape(3 * LANES, LANES)],
            [pltpu.VMEM((blocks_all, KB, 2 * LANES), BF16)],
            col_at,
            bnd,
            block_rows,
            group.reshape(-1, half, LANES),
            received,
            current,
            image_x,
            basis,
        )
        gram = sum_all(3 + 2 * sweep, n_sub, n_row, gram)
        solver = [pltpu.VMEM((LANES, 2 * LANES), F32), pltpu.VMEM((KB, LANES), F32)]
        if sweep < ITERS - 1:
            metric, current, image_x, basis, packed, messages = plain(
                functools.partial(step_kernel, total_rows),
                "step",
                [SMEM] * 3 + [VMEM] * 8,
                [shape(KB, LANES), shape(rows_here, LANES), shape(rows_here, LANES), *sent],
                [pltpu.VMEM((rows_here, LANES), F32), *solver],
                bnd,
                face_row,
                face_src,
                gram,
                metric,
                face_val,
                weights,
                current,
                image_x,
                basis,
                image_b,
            )
    return plain(
        functools.partial(last_kernel, total_rows),
        "last",
        [VMEM] * 4,
        [shape(rows_here, KB), shape(rows_here, KB)],
        solver,
        gram,
        metric,
        current,
        basis,
    )


def solution(mesh):
    n_sub, n_row = mesh.shape["sub"], mesh.shape["row"]
    ny = 4 if n_row == 16 else 2
    return jax.shard_map(
        functools.partial(local, (n_sub, ny, n_row // ny)),
        mesh=mesh,
        in_specs=(
            P(("sub", "row"), None),
            P(("sub", "row"), None),
            P(("sub", "row")),
            P("sub", "row", None),
            P("sub", "row", None),
            P("sub", "row", None, None, None),
            P("sub", "row", None),
            P("sub", "row", None),
            P("sub", "row", None),
            P("sub", "row", None, None, None),
        ),
        out_specs=(P(("sub", "row"), None), P(("sub", "row"), None)),
        check_vma=False,
    )
```

time: 1590 us -> 470 us (0.30)
  waiting for transfers between devices: 741 us -> 0 us
  blocking collectives: 497 us -> 18.9 us
  Pallas kernels: 0 us -> 428 us
  local copies, waits for them, and re-layouts: 128 us -> 12.3 us
  matrix products: 100 us -> 0 us
  other arithmetic: 97.2 us -> 9.48 us
    psum x6 -> x0, blocking collectives: 456 us -> none  [the longest x2 156 us: local(): lax.psum((gram_product(basis, image_b), gram_product(basis, image_x)), ('...]
    pallas_call x0 -> x14, Pallas kernels: none -> 428 us  [the longest x3 216 us: exchange(): pl.pallas_call(functools.partial(exchange_kernel, count, ny, nx, n_sub),...]
    psum x2 -> x0, waiting for transfers between devices: 321 us -> none  [local(): lax.psum((gram_product(basis, image_b), gram_product(basis, image_x)), ('...]
    reduce_scatter x6 -> x0, waiting for transfers between devices: 253 us -> none  [apply_blocks(): lax.psum_scatter(jnp.einsum('bk,kiw->biw', chosen, backward, precision=pr...]
    all_gather x4 -> x0, waiting for transfers between devices: 165 us -> none  [the longest x3 161 us: apply_blocks(): lax.all_gather(vector, 'row', axis=0, tiled=True).reshape(-1, KB, width)]
    another operation x30 -> x1, other arithmetic: 93.9 us -> 0.01 us  [tables(): own_at = jnp.sum(jnp.where(hit, k_ids[None], 0), 2)]
    dot_general x40 -> x0, matrix products: 82.1 us -> none  [the longest x3 17.8 us: apply_blocks(): jnp.einsum('kij,kjw->kiw', vals_here, group[cols_here], precision=precise...]
    gather x15 -> x0, local copies, waits for them, and re-layouts: 34.8 us -> none  [the longest x3 15.8 us: apply_blocks(): group[cols_here]]
  transfers between devices with their start and end apart: 12 -> 0, of which waited for: 10 -> 0; matrix products, arithmetic and copies ran while one was open for 11% -> 0% of each run, Pallas kernels for 0% -> 0%
where the time goes in v1:
time: 470 us
  Pallas kernels  428 us (91%)
  blocking collectives  18.9 us (4%)
  local copies, waits for them, and re-layouts  12.3 us (3%)
  other arithmetic  9.48 us (2%)
    pallas_call x3, Pallas kernels, exchange(): pl.pallas_call(functools.partial(exchange_kernel, count, ny, nx, n_sub),...  216 us
    pallas_call x7, Pallas kernels, plain(): pl.pallas_call(kernel, name=name, out_shape=outs, in_specs=specs, out_spe...  137 us
    pallas_call x3, Pallas kernels, sum_all(): pl.pallas_call(functools.partial(sum_kernel, n_sub, n_row), name=f'sum_{c...  66.6 us
    all_gather x1, blocking collectives, tables(): everyone = lax.all_gather(jnp.stack([in_row, in_col]), 'row')  18.9 us

profile of v1, /device:TPU:1, one launch (start us, length us, event | category | flops | bytes accessed | tf_op | source)
XLA Modules:
  0.0 469.8 jit_solution(6405486886737007461)
XLA Ops:
  0.6 1.3 select_reduce_fusion.2
  1.9 0.1 copy.32
  2.0 0.1 copy.33
  2.1 0.1 broadcast_add_fusion.1
  2.2 0.7 add_bitcast_fusion
  2.9 18.9 %all-gather.1 = s32[16,2,96]{2,1,0:T(2,128)S(1)} all-gather(s32[1,2,96]{2,1,0:T(2,128)S(1)} %add_bitcast_fusion), channel_id=2, replica_groups=mesh['sub'=16,'row'=16] {'row'}, dimensions={0}, use_global_device_ids=true | all-gather | bytes 13056 | tf_op jit(solution)/shard_map/all_gather | solution.py:587
  21.8 0.1 slice_reduce_fusion.1
  21.9 0.1 eq.49
  22.0 0.1 copy.30
  22.2 0.1 reshape_squeeze.3
  22.3 0.1 broadcast_add_fusion
  22.3 0.1 copy.31
  22.5 0.6 fusion.2
  23.1 0.5 broadcast.76
  23.6 1.3 reduce.15
  24.9 0.1 eq.45
  25.0 1.3 reduce.14
  26.3 0.1 broadcast_in_dim.73
  26.4 0.5 select_reduce_fusion
  26.9 0.1 pad_add_fusion
  26.9 0.6 reshape.100.col_at
  27.6 0.6 reshape.101.own_at
  28.2 0.6 reshape.102.back_at
  28.8 3.3 copy.34
  32.1 0.3 fusion.3
  32.4 0.0 copy-start.1
  32.4 0.0 copy-start.2
  32.4 1.3 pad_maximum_fusion.own_val
  33.7 0.0 copy-done.1
  33.7 0.2 copy.36
  33.9 0.0 copy-done.2
  33.9 0.2 copy.35
  34.1 1.0 pad_maximum_fusion.1.basis.refs_0_.current
  35.0 1.2 fusion
  36.3 5.2 %start.1.refs_2_ = f32[16,6,64,128]{3,2,1,0:T(8,128)} custom-call(s32[3]{0:T(128)} %bitcast.44, s32[12]{0:T(128)} %bitcast.51, s32[12]{0:T(128)} %bitcast.55, f32[768,128]{1,0:T(8,128)} %pad_maximum_fusion.1.basis.refs_0_.current, bf16[12,64,64]{2,1,0:T(8,128)(2,1)} %bitcast.29), custom_call_target="tpu_custom_call" | custom-call | tf_op jit(solution)/shard_map/start/pallas_call | solution.py:570
  41.5 133.3 %exchange_0.1 = (f32[16,768,128]{2,1,0:T(8,128)}, bf16[16,2688,128]{2,1,0:T(8,128)(2,1)}, f32[16,6,64,128]{3,2,1,0:T(8,128)}) custom-call(f32[768,128]{1,0:T(8,128)} %pad_maximum_fusion.1.basis.refs_0_.current, bf16[2688,128]{1,0:T(8,128)(2,1)} %bitcast.35, f32[16,6,64,128]{3,2,1,0:T(8,128)} %start.1.refs_2_), custom_call_target="tpu_custom_call" | custom-call | tf_op jit(solution)/shard_map/exchange_0/pallas_call | solution.py:227
  174.8 8.1 %build.1.rows_ref = bf16[12,64,1024]{2,1,0:T(8,128)(2,1)} custom-call(s32[96]{0:T(128)} %reshape.101.own_at, s32[84]{0:T(128)} %reshape.102.back_at, s32[12]{0:T(128)} %get-tuple-element.58.face_at, bf16[96,32,128]{2,1,0:T(8,128)(2,1)} %pad_maximum_fusion.own_val, bf16[1344,32,128]{2,1,0:T(8,128)(2,1)} %bitcast.26, bf16[12,64,64]{2,1,0:T(8,128)(2,1)} %bitcast.30), custom_call_target="tpu_custom_call" | custom-call | tf_op jit(solution)/shard_map/build/pallas_call | solution.py:635
  182.9 0.0 copy-start.3
  182.9 11.4 %first_apply.1 = (f32[768,128]{1,0:T(8,128)}, f32[128,128]{1,0:T(8,128)}) custom-call(s32[192]{0:T(256)} %reshape.100.col_at, s32[3]{0:T(128)} %bitcast.45, bf16[12,64,1024]{2,1,0:T(8,128)(2,1)} %build.1.rows_ref, f32[192,64,128]{2,1,0:T(8,128)} %bitcast.27, f32[16,6,64,128]{3,2,1,0:T(8,128)} %get-tuple-element.25.received, ...), custom_call_target="tpu_custom_call" | custom-call | tf_op jit(solution)/shard_map/first_apply/pallas_call | solution.py:570
  194.3 19.9 %sum_1.1 = f32[16,8,128]{2,1,0:T(8,128)} custom-call(f32[16,8,128]{2,1,0:T(8,128)} %bitcast.43), custom_call_target="tpu_custom_call" | custom-call | tf_op jit(solution)/shard_map/sum_1/pallas_call | solution.py:304
  214.2 0.0 copy-done.3
  214.2 0.9 broadcast_in_dim.84.precond
  215.1 14.5 %first_ritz.1 = (f32[768,128]{1,0:T(8,128)}, f32[12,32,128]{2,1,0:T(8,128)}, f32[16,6,32,128]{3,2,1,0:T(8,128)}) custom-call(s32[3]{0:T(128)} %bitcast.46, s32[12]{0:T(128)} %bitcast.52, s32[12]{0:T(128)} %bitcast.56, f32[128,128]{1,0:T(8,128)} %bitcast.38, bf16[12,64,64]{2,1,0:T(8,128)(2,1)} %bitcast.31, f32[768,128]{1,0:T(8,128)} %broadcast_in_dim.84.precond, ...), custom_call_target="tpu_custom_call" | custom-call | tf_op jit(solution)/shard_map/first_ritz/pallas_call | solution.py:570
  229.6 40.8 %exchange_2.1 = (f32[16,384,128]{2,1,0:T(8,128)}, f32[16,6,32,128]{3,2,1,0:T(8,128)}) custom-call(f32[384,128]{1,0:T(8,128)} %bitcast.40, f32[16,6,32,128]{3,2,1,0:T(8,128)} %get-tuple-element.29.refs_1_), custom_call_target="tpu_custom_call" | custom-call | tf_op jit(solution)/shard_map/exchange_2/pallas_call | solution.py:227
  270.4 0.0 copy-start
  270.4 25.6 %apply.2 = (f32[768,128]{1,0:T(8,128)}, f32[384,128]{1,0:T(8,128)}) custom-call(s32[192]{0:T(256)} %reshape.100.col_at, s32[3]{0:T(128)} %bitcast.47, bf16[12,64,1024]{2,1,0:T(8,128)(2,1)} %build.1.rows_ref, f32[192,32,128]{2,1,0:T(8,128)} %bitcast.34, f32[16,6,32,128]{3,2,1,0:T(8,128)} %get-tuple-element.31.received, ...), custom_call_target="tpu_custom_call" | custom-call | tf_op jit(solution)/shard_map/apply/pallas_call | solution.py:570
  296.0 23.1 %sum_3.1 = f32[16,24,128]{2,1,0:T(8,128)} custom-call(f32[16,24,128]{2,1,0:T(8,128)} %bitcast.42), custom_call_target="tpu_custom_call" | custom-call | tf_op jit(solution)/shard_map/sum_3/pallas_call | solution.py:304
  319.1 0.0 copy-done
  319.1 0.6 slice_bitcast_fusion.metric
  319.7 31.1 %step.1 = (f32[64,128]{1,0:T(8,128)}, f32[768,128]{1,0:T(8,128)}, f32[768,128]{1,0:T(8,128)}, f32[768,128]{1,0:T(8,128)}, f32[12,32,128]{2,1,0:T(8,128)}, /*index=5*/f32[16,6,32,128]{3,2,1,0:T(8,128)}) custom-call(s32[3]{0:T(128)} %bitcast.48, s32[12]{0:T(128)} %bitcast.53, s32[12]{0:T(128)} %bitcast.57, f32[384,128]{1,0:T(8,128)} %bitcast.36, ...), custom_call_target="tpu_custom_call" | custom-call | tf_op jit(solution)/shard_map/step/pallas_call | solution.py:570
  350.8 42.2 %exchange_4.1 = (f32[16,384,128]{2,1,0:T(8,128)}, f32[16,6,32,128]{3,2,1,0:T(8,128)}) custom-call(f32[384,128]{1,0:T(8,128)} %bitcast.39, f32[16,6,32,128]{3,2,1,0:T(8,128)} %get-tuple-element.36.refs_1_), custom_call_target="tpu_custom_call" | custom-call | tf_op jit(solution)/shard_map/exchange_4/pallas_call | solution.py:227
  393.0 25.7 %apply.3 = (f32[768,128]{1,0:T(8,128)}, f32[384,128]{1,0:T(8,128)}) custom-call(s32[192]{0:T(256)} %reshape.100.col_at, s32[3]{0:T(128)} %bitcast.49, bf16[12,64,1024]{2,1,0:T(8,128)(2,1)} %build.1.rows_ref, f32[192,32,128]{2,1,0:T(8,128)} %bitcast.33, f32[16,6,32,128]{3,2,1,0:T(8,128)} %get-tuple-element.38.received, f32[768,128]{1,0:T(8,128)} %get-tuple-element.39.current, ...), custom_call_target="tpu_custom_call" | custom-call | tf_op jit(solution)/shard_map/apply/pallas_call | solution.py:570
  418.7 23.6 %sum_5.1 = f32[16,24,128]{2,1,0:T(8,128)} custom-call(f32[16,24,128]{2,1,0:T(8,128)} %bitcast.41), custom_call_target="tpu_custom_call" | custom-call | tf_op jit(solution)/shard_map/sum_5/pallas_call | solution.py:304
  442.3 23.9 %last.1 = (f32[768,64]{1,0:T(8,128)}, f32[768,64]{1,0:T(8,128)}) custom-call(f32[384,128]{1,0:T(8,128)} %bitcast.37, f32[64,128]{1,0:T(8,128)} %get-tuple-element.43.metric, f32[768,128]{1,0:T(8,128)} %get-tuple-element.39.current, f32[768,128]{1,0:T(8,128)} %get-tuple-element.41.basis), custom_call_target="tpu_custom_call" | custom-call | tf_op jit(solution)/shard_map/last/pallas_call | solution.py:570
  466.2 1.8 copy.37
  468.0 1.8 copy.38
  (6 shorter events, 0.0 us)
Async XLA Ops:
  32.4 1.4 copy-start.1
  32.4 1.5 copy-start.2
  182.9 31.3 %copy-start.3 = (f32[768]{0:T(1024)S(1)}, f32[768]{0:T(1024)}, u32[]{:S(2)}) copy-start(f32[768]{0:T(1024)} %param.12) | copy-start | bytes 9220
  270.4 48.7 %copy-start = (f32[16,8,128]{2,1,0:T(8,128)S(1)}, f32[16,8,128]{2,1,0:T(8,128)}, u32[]{:S(2)}) copy-start(f32[16,8,128]{2,1,0:T(8,128)} %sum_1.1) | copy-start | bytes 196612

commit v2 on v1

v2 whole, which is shorter than its diff:
```python
import functools

import jax
import jax.numpy as jnp
from jax import lax
from jax.experimental import pallas as pl
from jax.experimental.pallas import tpu as pltpu
from jax.sharding import PartitionSpec as P

KB = 64
LB = 12
IFR = 3
ITERS = 2
GROUPS = 8
HALF = KB // 2
SLOTS = 2 * GROUPS
LANES = 128
MESH = pl.DeviceIdType.MESH
F32, BF16 = jnp.float32, jnp.bfloat16
VMEM = pl.BlockSpec(memory_space=pltpu.VMEM)
SMEM = pl.BlockSpec(memory_space=pltpu.SMEM)
ANY = pl.BlockSpec(memory_space=pl.ANY)
LIMIT = 40 * 1024 * 1024
EARLY = 4 * LB


def hdot(a, b):
    return jnp.dot(a, b, precision=lax.Precision.HIGHEST, preferred_element_type=F32)


def swap(v):
    return pltpu.roll(v, LANES // 2, 1)


def is_left(shape):
    return lax.broadcasted_iota(jnp.int32, shape, 1) < LANES // 2


def pack(block):
    left = is_left((HALF, LANES))
    return jnp.where(left, block[:HALF], swap(block[HALF:]))


def two_terms(v):
    hi = v.astype(BF16)
    return hi, (v - hi.astype(F32)).astype(BF16)


def write_messages(many, shard, bnd_out, parts, bnd, face_row, face_src, face_val):
    for q in range(IFR):
        bnd_out[q] = shard[bnd[0, 0, q]]
    parts[...] = jnp.zeros_like(parts)
    left = is_left((HALF, LANES))
    products = []
    for k in range(LB):
        block = shard[face_row[0, 0, k]]
        face = face_val[0, 0, k]
        terms = []
        for v in range(many):
            terms.extend(two_terms(block[v * HALF : (v + 1) * HALF]))
        terms = jnp.concatenate(terms, 1)
        one, two = (
            lax.dot_general(half, terms, (((0,), (0,)), ((), ())), preferred_element_type=F32)
            for half in (face[:HALF], face[HALF:])
        )
        sums = []
        for v in range(many):
            at = 2 * v * LANES
            first = one[:, at : at + LANES] + one[:, at + LANES : at + 2 * LANES]
            second = two[:, at : at + LANES] + two[:, at + LANES : at + 2 * LANES]
            sums.append(
                jnp.where(left, first[:HALF] + swap(second[:HALF]), swap(first[HALF:]) + second[HALF:])
            )
        products.append(jnp.concatenate(sums, 0) if many > 1 else sums[0])
    for k in range(LB):
        source = face_src[0, 0, k]
        target, slot = source // IFR, source % IFR
        core, z = target % 2, target // 2
        parts[core, z, slot] = parts[core, z, slot] + products[k]


def start_kernel(bnd, face_row, face_src, modes, search, precond, face_val, current, shard, bnd_out, parts, weights):
    current[...] = jnp.concatenate([modes[...], search[...]], 0).T
    for a in range(LB):
        block = current[a * KB : (a + 1) * KB]
        shard[a, :HALF] = pack(block)
        shard[a, HALF:] = pack(swap(block))
    for c in range(LB * KB // LANES):
        weights[c * LANES : (c + 1) * LANES] = jnp.broadcast_to(precond[c : c + 1], (LANES, LANES)).T
    write_messages(2, shard, bnd_out, parts, bnd, face_row, face_src, face_val)


def exchange_kernel(count, rings, ny, nx, n_sub, *refs):
    arrays = count + 2 * rings
    shards, bnd, parts = refs[:arrays], refs[arrays], refs[arrays + 1]
    groups, bnd_all, landed = refs[arrays + 2 : 2 * arrays + 2], refs[2 * arrays + 2], refs[2 * arrays + 3]
    theirs, ours, sub_send, sub_recv, row_send, row_recv, ring_send, ring_recv = refs[2 * arrays + 4 :]
    sub, row = lax.axis_index("sub"), lax.axis_index("row")
    y, x = row // nx, row % nx
    nz = n_sub // 2
    z, core = sub // 2, sub % 2
    sibling = z * 2 + 1 - core

    def at(dy, dx):
        return ((y + dy + ny) % ny) * nx + (x + dx + nx) % nx

    def along(d):
        return ((z + d + nz) % nz) * 2 + core

    barrier = pltpu.get_barrier_semaphore()
    for d in range(1, nx):
        pl.semaphore_signal(barrier, inc=1, device_id={"row": at(0, d)}, device_id_type=MESH)
    for d in range(1, ny):
        pl.semaphore_signal(barrier, inc=1, device_id={"row": at(d, 0)}, device_id_type=MESH)
    for d in range(1, nz):
        pl.semaphore_signal(barrier, inc=1, device_id={"sub": along(d)}, device_id_type=MESH)
    pl.semaphore_signal(barrier, inc=1, device_id={"sub": sibling}, device_id_type=MESH)
    pl.semaphore_wait(barrier, nx - 1 + ny - 1 + nz)

    def to_sub(src, dst, kind, d, target):
        return pltpu.make_async_remote_copy(
            src_ref=src,
            dst_ref=dst,
            send_sem=sub_send.at[kind, d],
            recv_sem=sub_recv.at[kind, d],
            device_id={"sub": target},
            device_id_type=MESH,
        )

    def landed_at(ref, sem):
        pltpu.make_async_copy(ref, ref, sem).wait()

    def hop(i, half, holder, src, to, sem):
        size = shards[i].shape[0] // 2
        return pltpu.make_async_remote_copy(
            src_ref=src,
            dst_ref=groups[i].at[holder, pl.ds(half * size, size)],
            send_sem=row_send.at[i, half, sem],
            recv_sem=row_recv.at[i, half, sem],
            device_id={"row": to},
            device_id_type=MESH,
        )

    def half_of(i, half, holder=None):
        size = shards[i].shape[0] // 2
        part = pl.ds(half * size, size)
        return shards[i].at[part] if holder is None else groups[i].at[holder, part]

    counts = ((nx, ny), (ny, nx))

    def place(half, first, second):
        return at(second, first) if half == 0 else at(first, second)

    sends = []

    def send(copy):
        copy.start()
        sends.append(copy)

    send(to_sub(parts.at[1 - core], theirs, 3, 0, sibling))
    for i in range(count):
        for half in range(2):
            n1, n2 = counts[half]
            for first in range(1, n1):
                send(hop(i, half, row, half_of(i, half), place(half, first, 0), first * n2))
        if i == 0:
            for d in range(1, nz):
                send(to_sub(bnd, bnd_all.at[sub], 0, d, along(d)))
            send(to_sub(bnd, bnd_all.at[sub], 1, 0, sibling))
        for half in range(2):
            n1, n2 = counts[half]
            for second in range(1, n2):
                send(hop(i, half, row, half_of(i, half), place(half, 0, second), second))

    for axis in range(2 * rings):
        mine = (x, y)[axis]
        for d in range(1, counts[axis][0]):
            send(
                pltpu.make_async_remote_copy(
                    src_ref=shards[count + axis],
                    dst_ref=groups[count + axis].at[mine],
                    send_sem=ring_send.at[axis, d],
                    recv_sem=ring_recv.at[axis, d],
                    device_id={"row": place(axis, d, 0)},
                    device_id_type=MESH,
                )
            )

    landed_at(theirs, sub_recv.at[3, 0])
    ours[...] = theirs[...] + parts[core]
    for d in range(1, nz):
        send(to_sub(ours.at[(z + d) % nz], landed.at[z], 2, d, along(d)))
    landed[z] = ours[z]

    for i in range(count):
        for first in range(1, max(nx, ny)):
            for half in range(2):
                n1, n2 = counts[half]
                if first >= n1:
                    continue
                holder = place(half, -first, 0)
                landed_at(half_of(i, half, holder), row_recv.at[i, half, first * n2])
                for second in range(1, n2):
                    send(hop(i, half, holder, half_of(i, half, holder), place(half, 0, second), first * n2 + second))
        if i == 0:
            for d in range(1, nz):
                here = bnd_all.at[along(-d)]
                landed_at(here, sub_recv.at[0, d])
                send(to_sub(here, here, 1, d, sibling))
    for d in range(1, nz):
        landed_at(landed.at[(z + nz - d) % nz], sub_recv.at[2, d])
    for d in range(nz):
        landed_at(bnd_all.at[((z + nz - d) % nz) * 2 + 1 - core], sub_recv.at[1, d])
    for i in range(count):
        for half in range(2):
            n1, n2 = counts[half]
            for first in range(n1):
                for second in range(1, n2):
                    landed_at(half_of(i, half, place(half, -first, -second)), row_recv.at[i, half, first * n2 + second])
    for axis in range(2 * rings):
        mine, n = (x, y)[axis], counts[axis][0]
        for d in range(1, n):
            landed_at(groups[count + axis].at[(mine + n - d) % n], ring_recv.at[axis, d])
    for copy in sends:
        copy.wait_send()


def exchange(collective_id, ny, nx, shards, rings, bnd, parts):
    count, n_row = len(shards), ny * nx
    nz = parts.shape[1]
    n_sub = 2 * nz
    most = max(nz, 2)
    gathered = [jax.ShapeDtypeStruct((n_row, *a.shape), a.dtype) for a in shards]
    gathered += [jax.ShapeDtypeStruct((n, *a.shape), a.dtype) for n, a in zip((nx, ny), rings)]
    return pl.pallas_call(
        functools.partial(exchange_kernel, count, bool(rings), ny, nx, n_sub),
        name=f"exchange_{collective_id}",
        out_shape=gathered
        + [jax.ShapeDtypeStruct((n_sub, *bnd.shape), F32), jax.ShapeDtypeStruct(parts.shape[1:], F32)],
        in_specs=[VMEM] * (len(gathered) + 2),
        out_specs=[VMEM] * (len(gathered) + 2),
        scratch_shapes=[
            pltpu.VMEM(parts.shape[1:], F32),
            pltpu.VMEM(parts.shape[1:], F32),
            pltpu.SemaphoreType.DMA((4, most)),
            pltpu.SemaphoreType.DMA((4, most)),
            pltpu.SemaphoreType.DMA((count, 2, n_row)),
            pltpu.SemaphoreType.DMA((count, 2, n_row)),
            pltpu.SemaphoreType.DMA((2, max(nx, ny))),
            pltpu.SemaphoreType.DMA((2, max(nx, ny))),
        ],
        compiler_params=pltpu.CompilerParams(
            collective_id=collective_id, has_side_effects=True, vmem_limit_bytes=LIMIT
        ),
    )(*shards, *rings, bnd, parts)


def hand_on_kernel(ny, nx, to_y, to_x, from_y, from_x, send, recv):
    row = lax.axis_index("row")
    y, x = row // nx, row % nx
    axes = ((ny, y, lambda t: t * nx + x, to_y, from_y), (nx, x, lambda t: y * nx + t, to_x, from_x))
    barrier = pltpu.get_barrier_semaphore()
    for n, mine, name, _, _ in axes:
        for d in range(1, n):
            pl.semaphore_signal(barrier, inc=1, device_id={"row": name((mine + d) % n)}, device_id_type=MESH)
    pl.semaphore_wait(barrier, ny - 1 + nx - 1)
    sends = []
    for i, (n, mine, name, src, dst) in enumerate(axes):
        for d in range(1, n):
            t = (mine + d) % n
            copy = pltpu.make_async_remote_copy(
                src_ref=src.at[t],
                dst_ref=dst.at[mine],
                send_sem=send.at[i, d],
                recv_sem=recv.at[i, d],
                device_id={"row": name(t)},
                device_id_type=MESH,
            )
            copy.start()
            sends.append(copy)
    for i, (n, mine, _, _, dst) in enumerate(axes):
        for d in range(1, n):
            here = dst.at[(mine + n - d) % n]
            pltpu.make_async_copy(here, here, recv.at[i, d]).wait()
    for copy in sends:
        copy.wait_send()


def hand_on(collective_id, ny, nx, to_y, to_x):
    return pl.pallas_call(
        functools.partial(hand_on_kernel, ny, nx),
        name=f"hand_on_{collective_id}",
        out_shape=[
            jax.ShapeDtypeStruct((ny, *to_y.shape[1:]), BF16),
            jax.ShapeDtypeStruct((nx, *to_x.shape[1:]), BF16),
        ],
        in_specs=[VMEM] * 2,
        out_specs=[VMEM] * 2,
        scratch_shapes=[pltpu.SemaphoreType.DMA((2, max(nx, ny)))] * 2,
        compiler_params=pltpu.CompilerParams(
            collective_id=collective_id, has_side_effects=True, vmem_limit_bytes=LIMIT
        ),
    )(to_y, to_x)


def sum_kernel(n_sub, n_row, parts, out, by_row, by_sub, own_sem, send, recv):
    sub, row = lax.axis_index("sub"), lax.axis_index("row")
    barrier = pltpu.get_barrier_semaphore()

    @pl.loop(1, n_row)
    def _(d):
        pl.semaphore_signal(barrier, inc=1, device_id={"row": (row + d) % n_row}, device_id_type=MESH)

    @pl.loop(1, n_sub)
    def _(d):
        pl.semaphore_signal(barrier, inc=1, device_id={"sub": (sub + d) % n_sub}, device_id_type=MESH)

    pl.semaphore_wait(barrier, n_row - 1 + n_sub - 1)

    def phase(index, axis, mine, n, source, target):
        def to(d):
            t = (mine + d) % n
            return pltpu.make_async_remote_copy(
                src_ref=source(t),
                dst_ref=target(mine),
                send_sem=send.at[index, d],
                recv_sem=recv.at[index, d],
                device_id={axis: t},
                device_id_type=MESH,
            )

        own = pltpu.make_async_copy(source(mine), target(mine), own_sem.at[index])

        @pl.loop(1, n)
        def _(d):
            to(d).start()

        own.start()

        @pl.loop(1, n)
        def _(d):
            here = target((mine + n - d) % n)
            pltpu.make_async_copy(here, here, recv.at[index, d]).wait()
            to(d).wait_send()

        own.wait()

    def summed(buffer, n):
        total = buffer[0]
        for t in range(1, n):
            total = total + buffer[t]
        return total

    phase(0, "row", row, n_row, lambda t: parts.at[t], lambda t: by_row.at[t])
    by_row[n_row] = summed(by_row, n_row)
    phase(1, "sub", sub, n_sub, lambda t: by_row.at[n_row], lambda t: by_sub.at[t])
    by_sub[n_sub] = summed(by_sub, n_sub)
    phase(2, "row", row, n_row, lambda t: by_sub.at[n_sub], lambda t: out.at[t])


def sum_all(collective_id, n_sub, n_row, part):
    rows = part.shape[0] // n_row
    most = max(n_sub, n_row)
    shape = (n_row, rows, LANES)
    total = pl.pallas_call(
        functools.partial(sum_kernel, n_sub, n_row),
        name=f"sum_{collective_id}",
        out_shape=jax.ShapeDtypeStruct(shape, F32),
        in_specs=[VMEM],
        out_specs=VMEM,
        scratch_shapes=[
            pltpu.VMEM((n_row + 1, rows, LANES), F32),
            pltpu.VMEM((n_sub + 1, rows, LANES), F32),
            pltpu.SemaphoreType.DMA((3,)),
            pltpu.SemaphoreType.DMA((3, most)),
            pltpu.SemaphoreType.DMA((3, most)),
        ],
        compiler_params=pltpu.CompilerParams(collective_id=collective_id, has_side_effects=True),
    )(part.reshape(shape))
    return total.reshape(part.shape)


def select_kernel(ny, nx, code_at, codes, own_val, ring_x, ring_y, to_y, to_x, back_at):
    row = lax.axis_index("row")
    y, x = row // nx, row % nx

    def scatter(device, source, start, size, out, n, mine_of, place_of, mine):
        @pl.loop(0, size // LB)
        def _(g):
            for b in range(LB):
                k = g * LB + b
                code = code_at[device, start + k]
                owner = code // 256
                slot = g * LB + code // 16 % 16
                out[jnp.where(mine_of(owner) == mine, place_of(owner), n), slot] = source(k)

    late = LB * GROUPS - LB - EARLY

    def by_x(device, source):
        scatter(device, source, LB, EARLY, to_y, ny, lambda o: o % nx, lambda o: o // nx, x)

    def by_y(device, source):
        scatter(device, source, LB + EARLY, late, to_x, nx, lambda o: o // nx, lambda o: o % nx, y)

    by_x(row, lambda k: own_val[LB + k])
    by_y(row, lambda k: own_val[LB + EARLY + k])

    @pl.loop(1, nx)
    def _(d):
        t = (x + d) % nx
        by_x(y * nx + t, lambda k: ring_x[t, k])

    @pl.loop(1, ny)
    def _(d):
        t = (y + d) % ny
        by_y(t * nx + x, lambda k: ring_y[t, k])

    code = codes[...]
    lane = lax.broadcasted_iota(jnp.int32, code.shape, 1)
    device = lax.broadcasted_iota(jnp.int32, code.shape, 0)
    ours = (code // 256 == row) & (lane >= LB) & (lane < GROUPS * LB)
    value = device * 16 + code % 16
    place = code // 16 % 16
    lines = [jnp.sum(jnp.where(ours & (place == a), value, 0), axis=0, keepdims=True) for a in range(LB)]
    lines += [jnp.zeros_like(lines[0])] * (16 - LB)
    k = lax.broadcasted_iota(jnp.int32, (LANES, LANES), 0)
    g = lax.broadcasted_iota(jnp.int32, (LANES, LANES), 1)
    member = ((k >= g * LB) & (k < g * LB + LB)).astype(F32)
    back_at[...] = hdot(jnp.concatenate(lines, 0).astype(F32), member).astype(jnp.int32)


def build_kernel(
    ny, nx, in_row, in_col, back_at, face_row, face_src, own_val, to_y, to_x, from_y, from_x, face_val, rows_ref, col_at,
    own_at, face_at
):
    n_row = ny * nx
    row = lax.axis_index("row")
    y, x = row // nx, row % nx

    @pl.loop(0, GROUPS)
    def _(g):
        for b in range(LB):
            k = g * LB + b
            own_at[g * LB + in_row[0, 0, k]] = k

    for k in range(LB):
        face_at[face_row[0, 0, k]] = k

    quarter = lax.broadcasted_iota(jnp.int32, (KB, LANES), 1) % KB < HALF
    left = is_left((HALF, LANES))

    def pair(one, two):
        top = jnp.where(left, one, swap(two))
        low = jnp.where(left, swap(one), two)
        return jnp.concatenate([top, low], 0)

    @pl.loop(0, LB)
    def _(a):
        def put(slot, ij, kl):
            lanes = slice(slot * LANES, (slot + 1) * LANES)
            rows_ref[a, :KB, lanes] = jnp.where(quarter, ij, pltpu.roll(kl, HALF, 1)).astype(BF16)
            rows_ref[a, KB:, lanes] = jnp.where(quarter, pltpu.roll(ij, LANES - HALF, 1), kl).astype(BF16)

        own = []
        for g in range(GROUPS):
            k = own_at[g * LB + a]
            col_at[a * SLOTS + g] = in_col[0, 0, k]
            own.append(own_val[k].astype(F32))
        put(0, pair(own[0], own[2]), pair(own[1], own[3]))
        put(1, pair(own[4], own[6]), pair(own[5], own[7]))
        back = []
        for g in range(GROUPS - 1):
            code = back_at[a, g + 1]
            device = code // 16
            col_at[a * SLOTS + GROUPS + g] = device * LB + code % 16
            if (g + 1) * LB <= EARLY:
                slot, t, mine, kept, got = g * LB + a, device // nx, y, to_y, from_y
            else:
                slot, t, mine, kept, got = g * LB - EARLY + a, device % nx, x, to_x, from_x
            back.append(jnp.where(t == mine, kept[mine, slot].astype(F32), got[t, slot].astype(F32)))
        turned = jnp.concatenate([pair(back[0], back[1]), pair(back[2], back[3])], 0).T
        put(2, turned[:KB], turned[KB:])
        turned = jnp.concatenate([pair(back[4], back[5]), pair(back[6], back[6])], 0).T
        k = face_at[a]
        col_at[a * SLOTS + SLOTS - 1] = n_row * LB + face_src[0, 0, k]
        face = face_val[0, 0, k].astype(F32)
        put(3, turned[:KB], jnp.where(is_left((KB, LANES)), turned[KB:], jnp.concatenate([face, face], 1)))


def apply_operator(many, col_at, rows_ref, own, group, bnd_all, terms, put_row):
    n_row, n_sub = group.shape[0], bnd_all.shape[0]

    def split(values, at, size):
        for v in range(many):
            hi, mid = two_terms(values[:, v * HALF : (v + 1) * HALF])
            lane = 2 * v * LANES
            terms[pl.ds(at, size), :, lane : lane + LANES] = hi
            terms[pl.ds(at, size), :, lane + LANES : lane + 2 * LANES] = mid

    @pl.loop(0, n_row)
    def _(r):
        split(group[r], r * LB, LB)

    split(own[...], lax.axis_index("row") * LB, LB)

    @pl.loop(0, n_sub)
    def _(t):
        split(bnd_all[t], n_row * LB + t * IFR, IFR)

    together = 3

    @pl.loop(0, LB // together)
    def _(c):
        for i in range(together):
            a = c * together + i
            total = None
            for part in range(2):
                here = range(part * GROUPS, (part + 1) * GROUPS)
                stack = jnp.concatenate([terms[col_at[a * SLOTS + t]] for t in here], 0)
                lhs = rows_ref[a, :, part * GROUPS * HALF : (part + 1) * GROUPS * HALF]
                product = jnp.dot(lhs, stack, preferred_element_type=F32)
                total = product if total is None else total + product
            blocks = []
            for v in range(many):
                lane = 2 * v * LANES
                both = total[:, lane : lane + LANES] + total[:, lane + LANES : lane + 2 * LANES]
                blocks.append(both[:KB] + swap(both[KB:]))
            put_row(a, blocks)


def landed_blocks(many, landed, q):
    total = landed[0, q]
    for t in range(1, landed.shape[0]):
        total = total + landed[t, q]
    parts = [total[v * HALF : (v + 1) * HALF] for v in range(many)]
    return [jnp.concatenate([part, swap(part)], 0) for part in parts]


def block_at(a):
    return pl.ds(pl.multiple_of(a * KB, KB), KB)


def first_apply_kernel(col_at, bnd, rows_ref, own, group, bnd_all, landed, basis, image, gram, terms):
    left_block = is_left((KB, LANES))

    def put_row(a, blocks):
        image[block_at(a), :] = jnp.where(left_block, blocks[0], swap(blocks[1]))

    apply_operator(2, col_at, rows_ref, own, group, bnd_all, terms, put_row)
    for q in range(IFR):
        one, two = landed_blocks(2, landed, q)
        at = block_at(bnd[0, 0, q])
        image[at, :] = image[at, :] + jnp.where(left_block, one, swap(two))
    both = basis[...]
    left = is_left(both.shape)
    gram[...] = hdot(both.T, jnp.where(left, both, swap(image[...])))


def apply_kernel(col_at, bnd, rows_ref, own, group, bnd_all, landed, current, image_x, basis, image_b, gram, terms):
    left_block = is_left((KB, LANES))

    def put_row(a, blocks):
        at = block_at(a)
        image_b[at, :] = jnp.where(left_block, blocks[0], image_x[at, :])

    apply_operator(1, col_at, rows_ref, own, group, bnd_all, terms, put_row)
    for q in range(IFR):
        at = block_at(bnd[0, 0, q])
        image_b[at, :] = image_b[at, :] + jnp.where(left_block, landed_blocks(1, landed, q)[0], 0.0)
    y = basis[...]
    turned = y.T
    left = is_left(y.shape)
    gram[0:LANES] = hdot(turned, image_b[...])
    gram[LANES : 2 * LANES] = hdot(turned, jnp.where(left, image_x[...], swap(current[...])))
    gram[2 * LANES :] = hdot(turned, y)


def eliminate(work, n, full):
    lane = lax.broadcasted_iota(jnp.int32, (n, LANES), 1)
    line = lax.broadcasted_iota(jnp.int32, (n, 1), 0)
    lane1 = lax.broadcasted_iota(jnp.int32, (1, LANES), 1)

    def step(t, pivots):
        j = 2 * t
        k = j + 1
        row0, row1 = work[pl.ds(j, 1), :], work[pl.ds(k, 1), :]
        whole = work[...]

        def entry(row, at):
            return jnp.sum(jnp.where(lane1 == at, row[:, :LANES], 0.0), axis=1, keepdims=True)

        def column(at):
            return jnp.sum(jnp.where(lane == at, whole[:, :LANES], 0.0), axis=1, keepdims=True)

        a, b, c, d = entry(row0, j), entry(row0, k), entry(row1, j), entry(row1, k)
        col0, col1 = column(j), column(k)
        inverse = 1.0 / a
        ratio = b * inverse
        below = row1 - (c * inverse) * row0
        second = d - c * ratio
        unit1 = below * (1.0 / second)
        unit0 = row0 * inverse - ratio * unit1
        moved = whole - (col0 * unit0 + col1 * unit1)
        if full:
            work[...] = jnp.where(line == j, unit0, jnp.where(line == k, unit1, moved))
        else:
            work[...] = jnp.where(line > k, moved, jnp.where(line == k, below, whole))
        return jnp.where(line == j, a, jnp.where(line == k, second, pivots))

    return lax.fori_loop(0, n // 2, step, jnp.zeros((n, 1), F32))


def padded(top):
    return jnp.concatenate([top, jnp.zeros_like(top)], 0)


def identity_right():
    line = lax.broadcasted_iota(jnp.int32, (KB, LANES), 0)
    lane = lax.broadcasted_iota(jnp.int32, (KB, LANES), 1)
    return (lane == line + KB).astype(F32)


def identity_left():
    line = lax.broadcasted_iota(jnp.int32, (KB, LANES), 0)
    lane = lax.broadcasted_iota(jnp.int32, (KB, LANES), 1)
    return (lane == line).astype(F32)


CHUNK = 256


def chunks(body):
    @pl.loop(0, LB * KB // CHUNK)
    def _(c):
        body(pl.ds(pl.multiple_of(c * CHUNK, CHUNK), CHUNK))


def new_basis(ritz, precond, current, image_x, basis, update, at):
    here = current[at, :]
    left = is_left(here.shape)
    residue = jnp.where(left, image_x[at, :], 0.0) - hdot(here, ritz)
    fresh = precond[at, :] * residue
    update[at, :] = fresh
    basis[at, :] = jnp.where(left, fresh, here)


def send_basis(update, packed, bnd_out, parts, bnd, face_row, face_src, face_val):
    for a in range(LB):
        packed[a] = pack(update[a * KB : (a + 1) * KB, :])
    write_messages(1, packed, bnd_out, parts, bnd, face_row, face_src, face_val)


def first_ritz_kernel(
    bnd, face_row, face_src, gram, face_val, precond, current, image_x, basis, packed, bnd_out, parts, update, work
):
    work[...] = gram[:KB]
    eliminate(work, KB, True)
    left = is_left((KB, LANES))
    ritz = padded(jnp.where(left, swap(work[...]), 0.0))
    chunks(lambda at: new_basis(ritz, precond, current, image_x, basis, update, at))
    send_basis(update, packed, bnd_out, parts, bnd, face_row, face_src, face_val)


def combine(total_rows, gram, metric, wide, narrow):
    wide[:, :LANES] = gram[0:LANES]
    right = gram[LANES : 2 * LANES]
    wide[:, LANES:] = right
    eliminate(wide, LANES, True)
    left_all = is_left((LANES, LANES))
    left = is_left((KB, LANES))
    z = jnp.where(left_all, -wide[:, LANES:], 0.0)
    cross = hdot(right.T, z)
    against = jnp.where(left_all, swap(right), 0.0) + hdot(gram[2 * LANES :], z)
    square = hdot(z.T, against)[:KB]
    lengths = jnp.where(left, metric[...], 0.0) + cross[KB:] + square
    narrow[...] = lengths * (1.0 / total_rows) + identity_right()
    pivots = eliminate(narrow, KB, False)
    root = 1.0 / jnp.sqrt(pivots)
    inverse = padded(jnp.where(left, swap(narrow[...]), 0.0) * root)
    turned = inverse.T
    half = hdot(z, turned)
    energy = jnp.where(left, swap(metric[...]), 0.0) + cross[:KB]
    energy = hdot(hdot(inverse, padded(energy)), turned)
    return turned, jnp.where(left_all, half, swap(half)), energy


def step_kernel(
    total_rows,
    bnd,
    face_row,
    face_src,
    gram,
    metric,
    face_val,
    precond,
    current,
    image_x,
    basis,
    image_b,
    next_metric,
    next_current,
    next_image,
    next_basis,
    packed,
    bnd_out,
    parts,
    update,
    wide,
    narrow,
):
    turned, moves, energy = combine(total_rows, gram, metric, wide, narrow)
    next_metric[...] = identity_left() * total_rows + swap(energy[:KB])
    ritz = energy * (1.0 / total_rows)

    def body(at):
        next_current[at, :] = hdot(current[at, :], turned) + hdot(basis[at, :], moves)
        next_image[at, :] = hdot(image_x[at, :], turned) + hdot(image_b[at, :], moves)
        new_basis(ritz, precond, next_current, next_image, next_basis, update, at)

    chunks(body)
    send_basis(update, packed, bnd_out, parts, bnd, face_row, face_src, face_val)


def last_kernel(total_rows, gram, metric, current, basis, modes, search, both, wide, narrow):
    turned, moves, _ = combine(total_rows, gram, metric, wide, narrow)

    def body(at):
        both[at, :] = hdot(current[at, :], turned) + hdot(basis[at, :], moves)

    chunks(body)
    whole = both[...].T
    modes[...] = whole[:KB]
    search[...] = whole[KB:]


def plain(kernel, name, specs, outs, scratch, *args):
    return pl.pallas_call(
        kernel,
        name=name,
        out_shape=outs,
        in_specs=specs,
        out_specs=[VMEM] * len(outs),
        scratch_shapes=scratch,
        compiler_params=pltpu.CompilerParams(vmem_limit_bytes=LIMIT),
    )(*args)


def shape(*dims):
    return jax.ShapeDtypeStruct(dims, F32)


def local(grid, modes, search, precond, in_row, in_col, in_val, bnd_rows, if_row, if_src, if_val):
    n_sub, ny, nx = grid
    n_row = ny * nx
    rows_here = LB * KB
    total_rows = float(rows_here * n_sub * n_row)
    vals = in_val[0, 0]
    own_val = jnp.concatenate([vals[:, :HALF], vals[:, HALF:]], 2)
    faces = (bnd_rows, if_row, if_src)

    def sent(many):
        return [
            shape(LB, many * HALF, LANES),
            shape(IFR, many * HALF, LANES),
            shape(2, n_sub // 2, IFR, many * HALF, LANES),
        ]

    current, shard, bnd, parts, weights = plain(
        start_kernel,
        "start",
        [SMEM] * 3 + [VMEM] * 4,
        [shape(rows_here, LANES), *sent(2), shape(rows_here, LANES)],
        [],
        *faces,
        modes.T,
        search.T,
        precond.reshape(-1, LANES),
        if_val,
    )
    cols = in_col[0]
    codes = cols // LB * 256 + cols % LB * 16 + in_row[0]
    codes = jnp.pad(codes, ((0, 15), (0, LANES - GROUPS * LB)))
    early = own_val[LB : LB + EARLY].reshape(-1, LANES)
    late = own_val[LB + EARLY :].reshape(-1, LANES)
    group, codes_all, ring_x, ring_y, bnd_all, landed = exchange(
        0, ny, nx, [shard.reshape(-1, LANES), codes], [early, late], bnd, parts
    )
    codes_all = lax.dynamic_update_slice(codes_all[:, 0], codes[:1], (lax.axis_index("row"), 0))
    in_early, in_late = EARLY, GROUPS * LB - LB - EARLY

    def blocks(n, count):
        return jax.ShapeDtypeStruct((n, count, HALF, LANES), BF16)

    to_y, to_x, back_at = plain(
        functools.partial(select_kernel, ny, nx),
        "select",
        [SMEM] + [VMEM] * 4,
        [blocks(ny + 1, in_early), blocks(nx + 1, in_late), jax.ShapeDtypeStruct((16, LANES), jnp.int32)],
        [],
        codes_all,
        codes_all,
        own_val,
        ring_x.reshape(nx, in_early, HALF, LANES),
        ring_y.reshape(ny, in_late, HALF, LANES),
    )
    from_y, from_x = hand_on(6, ny, nx, to_y, to_x)
    block_rows, col_at = pl.pallas_call(
        functools.partial(build_kernel, ny, nx),
        name="build",
        out_shape=[
            jax.ShapeDtypeStruct((LB, 2 * KB, SLOTS * HALF), BF16),
            jax.ShapeDtypeStruct((LB * SLOTS,), jnp.int32),
        ],
        in_specs=[SMEM] * 5 + [VMEM] * 6,
        out_specs=[VMEM, SMEM],
        scratch_shapes=[pltpu.SMEM((GROUPS * LB,), jnp.int32), pltpu.SMEM((LB,), jnp.int32)],
        compiler_params=pltpu.CompilerParams(vmem_limit_bytes=LIMIT),
    )(in_row, in_col, back_at, if_row, if_src, own_val, to_y, to_x, from_y, from_x, if_val)
    blocks_all = n_row * LB + n_sub * IFR
    image_x, gram = plain(
        first_apply_kernel,
        "first_apply",
        [SMEM] * 2 + [VMEM] * 6,
        [shape(rows_here, LANES), shape(LANES, LANES)],
        [pltpu.VMEM((blocks_all, HALF, 4 * LANES), BF16)],
        col_at,
        bnd_rows,
        block_rows,
        shard,
        group.reshape(n_row, LB, 2 * HALF, LANES),
        bnd_all,
        landed,
        current,
    )
    metric = sum_all(1, n_sub, n_row, gram)
    basis, packed, bnd, parts = plain(
        first_ritz_kernel,
        "first_ritz",
        [SMEM] * 3 + [VMEM] * 5,
        [shape(rows_here, LANES), *sent(1)],
        [pltpu.VMEM((rows_here, LANES), F32), pltpu.VMEM((KB, LANES), F32)],
        *faces,
        metric,
        if_val,
        weights,
        current,
        image_x,
    )
    metric = metric[:KB]
    solver = [pltpu.VMEM((rows_here, LANES), F32), pltpu.VMEM((LANES, 2 * LANES), F32), pltpu.VMEM((KB, LANES), F32)]
    for sweep in range(ITERS):
        group, bnd_all, landed = exchange(2 + 2 * sweep, ny, nx, [packed.reshape(-1, LANES)], [], bnd, parts)
        image_b, gram = plain(
            apply_kernel,
            "apply",
            [SMEM] * 2 + [VMEM] * 8,
            [shape(rows_here, LANES), shape(3 * LANES, LANES)],
            [pltpu.VMEM((blocks_all, HALF, 2 * LANES), BF16)],
            col_at,
            bnd_rows,
            block_rows,
            packed,
            group.reshape(n_row, LB, HALF, LANES),
            bnd_all,
            landed,
            current,
            image_x,
            basis,
        )
        gram = sum_all(3 + 2 * sweep, n_sub, n_row, gram)
        if sweep < ITERS - 1:
            metric, current, image_x, basis, packed, bnd, parts = plain(
                functools.partial(step_kernel, total_rows),
                "step",
                [SMEM] * 3 + [VMEM] * 8,
                [shape(KB, LANES), shape(rows_here, LANES), shape(rows_here, LANES), shape(rows_here, LANES), *sent(1)],
                solver,
                *faces,
                gram,
                metric,
                if_val,
                weights,
                current,
                image_x,
                basis,
                image_b,
            )
    modes, search = plain(
        functools.partial(last_kernel, total_rows),
        "last",
        [VMEM] * 4,
        [shape(KB, rows_here), shape(KB, rows_here)],
        solver,
        gram,
        metric,
        current,
        basis,
    )
    return modes.T, search.T


def solution(mesh):
    n_sub, n_row = mesh.shape["sub"], mesh.shape["row"]
    ny = 4 if n_row == 16 else 2
    return jax.shard_map(
        functools.partial(local, (n_sub, ny, n_row // ny)),
        mesh=mesh,
        in_specs=(
            P(("sub", "row"), None),
            P(("sub", "row"), None),
            P(("sub", "row")),
            P("sub", "row", None),
            P("sub", "row", None),
            P("sub", "row", None, None, None),
            P("sub", "row", None),
            P("sub", "row", None),
            P("sub", "row", None),
            P("sub", "row", None, None, None),
        ),
        out_specs=(P(("sub", "row"), None), P(("sub", "row"), None)),
        check_vma=False,
    )
```

time: 470 us -> 305 us (0.65)
  Pallas kernels: 428 us -> 281 us
  blocking collectives: 18.9 us -> 0 us
  local copies, waits for them, and re-layouts: 12.3 us -> 21.5 us
  other arithmetic: 9.48 us -> 1.51 us
    pallas_call x7 -> x8, Pallas kernels: 137 us -> 59.3 us  [plain(): pl.pallas_call(kernel, name=name, out_shape=outs, in_specs=specs, out_spe...]
    pallas_call x4 -> x5, Pallas kernels: 224 us -> 153 us  [the longest x3 127 us: exchange(): pl.pallas_call(functools.partial(exchange_kernel, count, bool(rings), ny,...]
    all_gather x1 -> x0, blocking collectives: 18.9 us -> none  [tables(): everyone = lax.all_gather(jnp.stack([in_row, in_col]), 'row')]
    unnamed x12 -> x63, local copies, waits for them, and re-layouts: 4.16 us -> 20.2 us
where the time goes in v2:
time: 305 us
  Pallas kernels  281 us (92%)
  local copies, waits for them, and re-layouts  21.5 us (7%)
    pallas_call x3, Pallas kernels, exchange(): pl.pallas_call(functools.partial(exchange_kernel, count, bool(rings), ny,...  127 us
    pallas_call x3, Pallas kernels, sum_all(): pl.pallas_call(functools.partial(sum_kernel, n_sub, n_row), name=f'sum_{c...  68.5 us
    pallas_call x8, Pallas kernels, plain(): pl.pallas_call(kernel, name=name, out_shape=outs, in_specs=specs, out_spe...  59.3 us
    pallas_call x1, Pallas kernels, hand_on(): pl.pallas_call(functools.partial(hand_on_kernel, ny, nx), name=f'hand_on_...  20.4 us
    unnamed x63, local copies, waits for them, and re-layouts  20.2 us

profile of v2, /device:TPU:1, one launch (start us, length us, event | category | flops | bytes accessed | tf_op | source)
XLA Modules:
  0.0 304.8 jit_solution(9876059813106860848)
XLA Ops:
  0.6 0.7 fusion.5
  1.3 3.3 %copy.12 = bf16[1,1,96,64,64]{4,3,2,1,0:T(8,128)(2,1)S(1)} copy(bf16[1,1,96,64,64]{2,4,3,1,0:T(8,128)(2,1)} %param.15) | data formatting | bytes 1572864 | tf_op args[5]
  4.7 0.3 fusion.6
  4.9 0.2 fusion.1
  5.1 0.2 fusion
  5.4 0.0 copy-start.2
  5.4 0.0 copy-start.22
  5.4 0.0 copy-start.23
  5.4 0.0 copy-start.25
  5.4 0.0 copy-start.26
  5.4 0.0 copy-start.27
  5.4 0.0 copy-start.28
  5.4 0.4 pad_maximum_fusion.own_val
  5.9 0.4 copy-done.2
  6.3 0.1 copy-done.22
  6.4 0.1 copy-done.23
  6.5 0.0 copy-done.25
  6.5 0.0 copy-done.26
  6.5 0.0 copy-done.27
  6.5 0.0 copy-done.28
  6.5 1.7 start.1
  8.2 0.0 copy-start.3
  8.3 0.8 copy-done.3
  9.0 72.7 %exchange_0.1 = (f32[16,768,128]{2,1,0:T(8,128)S(1)}, s32[16,16,128]{2,1,0:T(8,128)S(1)}, bf16[4,1536,128]{2,1,0:T(8,128)(2,1)S(1)}, bf16[4,1152,128]{2,1,0:T(8,...) custom-call(f32[768,128]{1,0:T(8,128)S(1)} %bitcast.46, s32[16,128]{1,0:T(8,128)S(1)} %pad.4.refs_1_, ...), custom_call_target="tpu_custom_call" | custom-call | tf_op jit(solution)/shard_map/exchange_0/pallas_call | solution.py:235
  81.7 0.0 copy-start
  81.7 2.7 copy-done
  84.4 1.2 copy-done.5
  85.5 1.1 copy-done.11
  86.7 0.9 copy-done.13
  87.6 0.2 dynamic_update_slice.3.code_at.codes
  87.8 0.0 copy-start.12
  87.8 1.3 copy-done.12
  89.1 7.3 %select.2 = (bf16[5,48,32,128]{3,2,1,0:T(8,128)(2,1)S(1)}, bf16[5,36,32,128]{3,2,1,0:T(8,128)(2,1)S(1)}, s32[16,128]{1,0:T(8,128)S(1)}) custom-call(s32[16,128]{1,0:T(8,128)S(1)} %dynamic_update_slice.3.code_at.codes, s32[16,128]{1,0:T(8,128)S(1)} %dynamic_update_slice.3.code_at.codes, bf16[96,32,128]{2,1,0:T(8,128)(2,1)S(1)} %pad_maximum_fusion.own_val, ...), custom_call_target="tpu_custom_call" | custom-call | tf_op jit(solution)/shard_map/select/pallas_call | solution.py:737
  96.3 0.0 copy-start.30
  96.4 0.0 copy-start.6
  96.4 20.4 %hand_on_6.1 = (bf16[4,48,32,128]{3,2,1,0:T(8,128)(2,1)S(1)}, bf16[4,36,32,128]{3,2,1,0:T(8,128)(2,1)S(1)}) custom-call(bf16[5,48,32,128]{3,2,1,0:T(8,128)(2,1)S(1)} %get-tuple-element.51.to_y, bf16[5,36,32,128]{3,2,1,0:T(8,128)(2,1)S(1)} %get-tuple-element.52.to_x), custom_call_target="tpu_custom_call" | custom-call | tf_op jit(solution)/shard_map/hand_on_6/pallas_call | solution.py:290
  116.8 0.0 copy-done.29
  116.8 5.3 %build.1 = (bf16[12,128,512]{2,1,0:T(8,128)(2,1)S(1)}, s32[192]{0:T(256)S(1)}) custom-call(s32[1,1,96]{2,1,0:T(1,128)S(1)} %copy-done.29, s32[1,1,96]{2,1,0:T(1,128)S(1)} %copy-done.30, s32[16,128]{1,0:T(8,128)S(1)} %get-tuple-element.50.back_at, s32[1,1,12]{2,1,0:T(1,128)S(1)} %copy-done.26, s32[1,1,12]{2,1,0:T(1,128)S(1)} %copy-done.27, ...), custom_call_target="tpu_custom_call" | custom-call | tf_op jit(solution)/shard_map/build/pallas_call | solution.py:807
  122.2 4.9 %first_apply.1 = (f32[768,128]{1,0:T(8,128)S(1)}, f32[128,128]{1,0:T(8,128)S(1)}) custom-call(s32[192]{0:T(256)S(1)} %get-tuple-element.55.col_at, s32[1,1,3]{2,1,0:T(1,128)S(1)} %copy-done.25, bf16[12,128,512]{2,1,0:T(8,128)(2,1)S(1)} %get-tuple-element.56.rows_ref, f32[12,64,128]{2,1,0:T(8,128)S(1)} %get-tuple-element.44.own, ...), custom_call_target="tpu_custom_call" | custom-call | tf_op jit(solution)/shard_map/first_apply/pallas_call | solution.py:737
  127.1 0.0 copy-start.24
  127.1 0.6 copy-done.24
  127.7 21.1 %sum_1.1 = f32[16,8,128]{2,1,0:T(8,128)} custom-call(f32[16,8,128]{2,1,0:T(8,128)} %bitcast.60), custom_call_target="tpu_custom_call" | custom-call | tf_op jit(solution)/shard_map/sum_1/pallas_call | solution.py:365
  148.8 0.8 slice_bitcast_fusion.metric
  149.5 0.8 copy-done.17
  150.4 5.4 %first_ritz.1 = (f32[768,128]{1,0:T(8,128)S(1)}, f32[12,32,128]{2,1,0:T(8,128)S(1)}, f32[3,32,128]{2,1,0:T(8,128)S(1)}, f32[2,8,3,32,128]{4,3,2,1,0:T(8,128)S(1)}) custom-call(s32[1,1,3]{2,1,0:T(1,128)S(1)} %copy-done.25, s32[1,1,12]{2,1,0:T(1,128)S(1)} %copy-done.26, s32[1,1,12]{2,1,0:T(1,128)S(1)} %copy-done.27, f32[128,128]{1,0:T(8,128)S(1)} %bitcast.55, ...), custom_call_target="tpu_custom_call" | custom-call | tf_op jit(solution)/shard_map/first_ritz/pallas_call | solution.py:737
  155.8 26.5 %exchange_2.1 = (f32[16,384,128]{2,1,0:T(8,128)S(1)}, f32[16,3,32,128]{3,2,1,0:T(8,128)S(1)}, f32[8,3,32,128]{3,2,1,0:T(8,128)S(1)}) custom-call(f32[384,128]{1,0:T(8,128)S(1)} %bitcast.54, f32[3,32,128]{2,1,0:T(8,128)S(1)} %get-tuple-element.65.refs_1_, f32[2,8,3,32,128]{4,3,2,1,0:T(8,128)S(1)} %get-tuple-element.66.refs_2_), custom_call_target="tpu_custom_call" | custom-call | tf_op jit(solution)/shard_map/exchange_2/pallas_call | solution.py:235
  182.3 4.0 %apply.2 = (f32[768,128]{1,0:T(8,128)S(1)}, f32[384,128]{1,0:T(8,128)S(1)}) custom-call(s32[192]{0:T(256)S(1)} %get-tuple-element.55.col_at, s32[1,1,3]{2,1,0:T(1,128)S(1)} %copy-done.25, bf16[12,128,512]{2,1,0:T(8,128)(2,1)S(1)} %get-tuple-element.56.rows_ref, f32[12,32,128]{2,1,0:T(8,128)S(1)} %get-tuple-element.64.own, f32[16,12,32,128]{3,2,1,0:T(8,128)S(1)} %bitcast.45, ...), custom_call_target="tpu_custom_call" | custom-call | tf_op jit(solution)/shard_map/apply/pallas_call | solution.py:737
  186.3 0.7 copy-done.18
  187.0 0.7 copy-done.21
  187.7 24.0 %sum_3.1 = f32[16,24,128]{2,1,0:T(8,128)} custom-call(f32[16,24,128]{2,1,0:T(8,128)} %bitcast.57), custom_call_target="tpu_custom_call" | custom-call | tf_op jit(solution)/shard_map/sum_3/pallas_call | solution.py:365
  211.7 0.9 copy-done.15
  212.6 1.0 copy-done.19
  213.6 16.6 %step.1 = (f32[64,128]{1,0:T(8,128)S(1)}, f32[768,128]{1,0:T(8,128)S(1)}, f32[768,128]{1,0:T(8,128)S(1)}, f32[768,128]{1,0:T(8,128)S(1)}, f32[12,32,128]{2,1,0:T...) custom-call(s32[1,1,3]{2,1,0:T(1,128)S(1)} %copy-done.25, s32[1,1,12]{2,1,0:T(1,128)S(1)} %copy-done.26, ...), custom_call_target="tpu_custom_call" | custom-call | tf_op jit(solution)/shard_map/step/pallas_call | solution.py:737
  230.2 0.0 copy-start.7
  230.2 0.0 copy-start.9
  230.2 28.0 %exchange_4.1 = (f32[16,384,128]{2,1,0:T(8,128)S(1)}, f32[16,3,32,128]{3,2,1,0:T(8,128)S(1)}, f32[8,3,32,128]{3,2,1,0:T(8,128)S(1)}) custom-call(f32[384,128]{1,0:T(8,128)S(1)} %bitcast.53, f32[3,32,128]{2,1,0:T(8,128)S(1)} %get-tuple-element.74.refs_1_, f32[2,8,3,32,128]{4,3,2,1,0:T(8,128)S(1)} %get-tuple-element.75.refs_2_), custom_call_target="tpu_custom_call" | custom-call | tf_op jit(solution)/shard_map/exchange_4/pallas_call | solution.py:235
  258.2 4.4 %apply.3 = (f32[768,128]{1,0:T(8,128)}, f32[384,128]{1,0:T(8,128)S(1)}) custom-call(s32[192]{0:T(256)S(1)} %get-tuple-element.55.col_at, s32[1,1,3]{2,1,0:T(1,128)S(1)} %copy-done.25, bf16[12,128,512]{2,1,0:T(8,128)(2,1)S(1)} %get-tuple-element.56.rows_ref, f32[12,32,128]{2,1,0:T(8,128)S(1)} %get-tuple-element.73.own, f32[16,12,32,128]{3,2,1,0:T(8,128)S(1)} %bitcast.44, ...), custom_call_target="tpu_custom_call" | custom-call | tf_op jit(solution)/shard_map/apply/pallas_call | solution.py:737
  262.7 0.0 copy-done.9
  262.7 0.7 copy-done.20
  263.4 23.5 %sum_5.1 = f32[16,24,128]{2,1,0:T(8,128)} custom-call(f32[16,24,128]{2,1,0:T(8,128)} %bitcast.56), custom_call_target="tpu_custom_call" | custom-call | tf_op jit(solution)/shard_map/sum_5/pallas_call | solution.py:365
  286.9 1.0 copy-done.8
  287.9 1.0 copy-done.10
  288.9 0.9 copy-done.16
  289.8 15.0 %last.1 = (f32[64,768]{1,0:T(8,128)}, f32[64,768]{1,0:T(8,128)}) custom-call(f32[384,128]{1,0:T(8,128)S(1)} %bitcast.52, f32[64,128]{1,0:T(8,128)S(1)} %get-tuple-element.83.metric, f32[768,128]{1,0:T(8,128)S(1)} %copy-done.8, f32[768,128]{1,0:T(8,128)S(1)} %copy-done.10), custom_call_target="tpu_custom_call" | custom-call | tf_op jit(solution)/shard_map/last/pallas_call | solution.py:737
  (26 shorter events, 0.1 us)
Async XLA Ops:
  5.4 0.9 copy-start.2
  5.4 1.0 copy-start.22
  5.4 1.1 copy-start.23
  5.4 1.1 copy-start.25
  5.4 1.1 copy-start.26
  5.4 1.1 copy-start.27
  5.4 1.1 copy-start.28
  8.2 0.8 copy-start.3
  81.7 2.7 copy-start
  84.4 1.2 copy-start.5
  85.5 1.1 copy-start.11
  86.7 0.9 copy-start.13
  87.8 1.3 copy-start.12
  96.3 20.4 %copy-start.29 = (s32[1,1,96]{2,1,0:T(1,128)S(1)}, s32[1,1,96]{2,1,0:T(1,128)}, u32[]{:S(2)}) copy-start(s32[1,1,96]{2,1,0:T(1,128)} %in_row.1) | copy-start | bytes 1156
  96.3 20.4 %copy-start.30 = (s32[1,1,96]{2,1,0:T(1,128)S(1)}, s32[1,1,96]{2,1,0:T(1,128)}, u32[]{:S(2)}) copy-start(s32[1,1,96]{2,1,0:T(1,128)} %in_col.1) | copy-start | bytes 1156
  96.4 25.7 %copy-start.6 = (f32[16,3,64,128]{3,2,1,0:T(8,128)S(1)}, f32[16,3,64,128]{3,2,1,0:T(8,128)}, u32[]{:S(2)}) copy-start(f32[16,3,64,128]{3,2,1,0:T(8,128)} %copy-done.5) | copy-start | bytes 4718596
  116.8 5.3 %copy-start.1 = (f32[16,768,128]{2,1,0:T(8,128)S(1)}, f32[16,768,128]{2,1,0:T(8,128)}, u32[]{:S(2)}) copy-start(f32[16,768,128]{2,1,0:T(8,128)} %copy-done) | copy-start | bytes 18874372
  116.8 5.3 %copy-start.14 = (f32[8,3,64,128]{3,2,1,0:T(8,128)S(1)}, f32[8,3,64,128]{3,2,1,0:T(8,128)}, u32[]{:S(2)}) copy-start(f32[8,3,64,128]{3,2,1,0:T(8,128)} %copy-done.13) | copy-start | bytes 2359300
  122.1 27.4 %copy-start.4 = (f32[768,128]{1,0:T(8,128)S(1)}, f32[768,128]{1,0:T(8,128)}, u32[]{:S(2)}) copy-start(f32[768,128]{1,0:T(8,128)} %copy-done.3) | copy-start | bytes 1179652
  127.1 0.6 copy-start.24
  149.5 0.8 copy-start.17
  186.3 0.7 copy-start.18
  187.0 0.7 copy-start.21
  211.7 0.9 copy-start.15
  212.6 1.0 copy-start.19
  230.2 32.5 %copy-start.7 = (f32[768,128]{1,0:T(8,128)}, f32[768,128]{1,0:T(8,128)S(1)}, u32[]{:S(2)}) copy-start(f32[768,128]{1,0:T(8,128)S(1)} %get-tuple-element.79.current) | copy-start | bytes 1179652
  230.2 32.5 %copy-start.9 = (f32[768,128]{1,0:T(8,128)}, f32[768,128]{1,0:T(8,128)S(1)}, u32[]{:S(2)}) copy-start(f32[768,128]{1,0:T(8,128)S(1)} %get-tuple-element.81.basis) | copy-start | bytes 1179652
  262.7 0.7 copy-start.20
  286.9 1.0 copy-start.8
  287.9 1.0 copy-start.10
  288.9 0.9 copy-start.16

commit v3 on v2

--- a/solution.py
+++ b/solution.py
@@ -20,7 +20,8 @@
 VMEM = pl.BlockSpec(memory_space=pltpu.VMEM)
 SMEM = pl.BlockSpec(memory_space=pltpu.SMEM)
 ANY = pl.BlockSpec(memory_space=pl.ANY)
-LIMIT = 40 * 1024 * 1024
+LIMIT = 12 * 1024 * 1024
+SMALL = 4 * 1024 * 1024
 EARLY = 4 * LB
 
 
@@ -46,7 +47,14 @@
     return hi, (v - hi.astype(F32)).astype(BF16)
 
 
-def write_messages(many, shard, bnd_out, parts, bnd, face_row, face_src, face_val):
+def add_terms(coarse, product, v):
+    if coarse:
+        return product
+    at = 2 * v * LANES
+    return product[:, at : at + LANES] + product[:, at + LANES : at + 2 * LANES]
+
+
+def write_messages(many, coarse, shard, bnd_out, parts, bnd, face_row, face_src, face_val):
     for q in range(IFR):
         bnd_out[q] = shard[bnd[0, 0, q]]
     parts[...] = jnp.zeros_like(parts)
@@ -55,19 +63,17 @@
     for k in range(LB):
         block = shard[face_row[0, 0, k]]
         face = face_val[0, 0, k]
-        terms = []
-        for v in range(many):
-            terms.extend(two_terms(block[v * HALF : (v + 1) * HALF]))
-        terms = jnp.concatenate(terms, 1)
+        if coarse:
+            terms = block
+        else:
+            terms = jnp.concatenate([t for v in range(many) for t in two_terms(block[v * HALF : (v + 1) * HALF])], 1)
         one, two = (
             lax.dot_general(half, terms, (((0,), (0,)), ((), ())), preferred_element_type=F32)
             for half in (face[:HALF], face[HALF:])
         )
         sums = []
         for v in range(many):
-            at = 2 * v * LANES
-            first = one[:, at : at + LANES] + one[:, at + LANES : at + 2 * LANES]
-            second = two[:, at : at + LANES] + two[:, at + LANES : at + 2 * LANES]
+            first, second = add_terms(coarse, one, v), add_terms(coarse, two, v)
             sums.append(
                 jnp.where(left, first[:HALF] + swap(second[:HALF]), swap(first[HALF:]) + second[HALF:])
             )
@@ -87,11 +93,11 @@
         shard[a, HALF:] = pack(swap(block))
     for c in range(LB * KB // LANES):
         weights[c * LANES : (c + 1) * LANES] = jnp.broadcast_to(precond[c : c + 1], (LANES, LANES)).T
-    write_messages(2, shard, bnd_out, parts, bnd, face_row, face_src, face_val)
-
-
-def exchange_kernel(count, rings, ny, nx, n_sub, *refs):
-    arrays = count + 2 * rings
+    write_messages(2, False, shard, bnd_out, parts, bnd, face_row, face_src, face_val)
+
+
+def exchange_kernel(count, handing, ny, nx, n_sub, *refs):
+    arrays = count + 2 * handing
     shards, bnd, parts = refs[:arrays], refs[arrays], refs[arrays + 1]
     groups, bnd_all, landed = refs[arrays + 2 : 2 * arrays + 2], refs[2 * arrays + 2], refs[2 * arrays + 3]
     theirs, ours, sub_send, sub_recv, row_send, row_recv, ring_send, ring_recv = refs[2 * arrays + 4 :]
@@ -172,16 +178,17 @@
             for second in range(1, n2):
                 send(hop(i, half, row, half_of(i, half), place(half, 0, second), second))
 
-    for axis in range(2 * rings):
-        mine = (x, y)[axis]
-        for d in range(1, counts[axis][0]):
+    for axis in range(2 * handing):
+        mine, n = (y, x)[axis], (ny, nx)[axis]
+        for d in range(1, n):
+            t = (mine + d) % n
             send(
                 pltpu.make_async_remote_copy(
-                    src_ref=shards[count + axis],
+                    src_ref=shards[count + axis].at[t],
                     dst_ref=groups[count + axis].at[mine],
                     send_sem=ring_send.at[axis, d],
                     recv_sem=ring_recv.at[axis, d],
-                    device_id={"row": place(axis, d, 0)},
+                    device_id={"row": (t * nx + x, y * nx + t)[axis]},
                     device_id_type=MESH,
                 )
             )
@@ -217,26 +224,26 @@
             for first in range(n1):
                 for second in range(1, n2):
                     landed_at(half_of(i, half, place(half, -first, -second)), row_recv.at[i, half, first * n2 + second])
-    for axis in range(2 * rings):
-        mine, n = (x, y)[axis], counts[axis][0]
+    for axis in range(2 * handing):
+        mine, n = (y, x)[axis], (ny, nx)[axis]
         for d in range(1, n):
             landed_at(groups[count + axis].at[(mine + n - d) % n], ring_recv.at[axis, d])
     for copy in sends:
         copy.wait_send()
 
 
-def exchange(collective_id, ny, nx, shards, rings, bnd, parts):
+def exchange(collective_id, ny, nx, shards, handed, bnd, parts):
     count, n_row = len(shards), ny * nx
     nz = parts.shape[1]
     n_sub = 2 * nz
     most = max(nz, 2)
     gathered = [jax.ShapeDtypeStruct((n_row, *a.shape), a.dtype) for a in shards]
-    gathered += [jax.ShapeDtypeStruct((n, *a.shape), a.dtype) for n, a in zip((nx, ny), rings)]
+    gathered += [jax.ShapeDtypeStruct((n, *a.shape[1:]), a.dtype) for n, a in zip((ny, nx), handed)]
     return pl.pallas_call(
-        functools.partial(exchange_kernel, count, bool(rings), ny, nx, n_sub),
+        functools.partial(exchange_kernel, count, bool(handed), ny, nx, n_sub),
         name=f"exchange_{collective_id}",
         out_shape=gathered
-        + [jax.ShapeDtypeStruct((n_sub, *bnd.shape), F32), jax.ShapeDtypeStruct(parts.shape[1:], F32)],
+        + [jax.ShapeDtypeStruct((n_sub, *bnd.shape), bnd.dtype), jax.ShapeDtypeStruct(parts.shape[1:], F32)],
         in_specs=[VMEM] * (len(gathered) + 2),
         out_specs=[VMEM] * (len(gathered) + 2),
         scratch_shapes=[
@@ -250,35 +257,39 @@
             pltpu.SemaphoreType.DMA((2, max(nx, ny))),
         ],
         compiler_params=pltpu.CompilerParams(
-            collective_id=collective_id, has_side_effects=True, vmem_limit_bytes=LIMIT
+            collective_id=collective_id, has_side_effects=True, vmem_limit_bytes=SMALL
         ),
-    )(*shards, *rings, bnd, parts)
-
-
-def hand_on_kernel(ny, nx, to_y, to_x, from_y, from_x, send, recv):
+    )(*shards, *handed, bnd, parts)
+
+
+def rings_kernel(ny, nx, codes, early, late, codes_all, ring_x, ring_y, send, recv):
     row = lax.axis_index("row")
     y, x = row // nx, row % nx
-    axes = ((ny, y, lambda t: t * nx + x, to_y, from_y), (nx, x, lambda t: y * nx + t, to_x, from_x))
+    n_row = ny * nx
     barrier = pltpu.get_barrier_semaphore()
-    for n, mine, name, _, _ in axes:
+    for d in range(1, n_row):
+        pl.semaphore_signal(barrier, inc=1, device_id={"row": (row + d) % n_row}, device_id_type=MESH)
+    pl.semaphore_wait(barrier, n_row - 1)
+    rings = (
+        (nx, x, lambda t: y * nx + t, early, ring_x),
+        (ny, y, lambda t: t * nx + x, late, ring_y),
+        (n_row, row, lambda t: t, codes, codes_all),
+    )
+    sends = []
+    for i, (n, mine, name, src, dst) in enumerate(rings):
         for d in range(1, n):
-            pl.semaphore_signal(barrier, inc=1, device_id={"row": name((mine + d) % n)}, device_id_type=MESH)
-    pl.semaphore_wait(barrier, ny - 1 + nx - 1)
-    sends = []
-    for i, (n, mine, name, src, dst) in enumerate(axes):
-        for d in range(1, n):
-            t = (mine + d) % n
             copy = pltpu.make_async_remote_copy(
-                src_ref=src.at[t],
+                src_ref=src,
                 dst_ref=dst.at[mine],
                 send_sem=send.at[i, d],
                 recv_sem=recv.at[i, d],
-                device_id={"row": name(t)},
+                device_id={"row": name((mine + d) % n)},
                 device_id_type=MESH,
             )
             copy.start()
             sends.append(copy)
-    for i, (n, mine, _, _, dst) in enumerate(axes):
+    codes_all[row] = codes[...]
+    for i, (n, mine, _, _, dst) in enumerate(rings):
         for d in range(1, n):
             here = dst.at[(mine + n - d) % n]
             pltpu.make_async_copy(here, here, recv.at[i, d]).wait()
@@ -286,21 +297,20 @@
         copy.wait_send()
 
 
-def hand_on(collective_id, ny, nx, to_y, to_x):
+def ring_gather(collective_id, ny, nx, codes, early, late):
     return pl.pallas_call(
-        functools.partial(hand_on_kernel, ny, nx),
-        name=f"hand_on_{collective_id}",
+        functools.partial(rings_kernel, ny, nx),
+        name=f"rings_{collective_id}",
         out_shape=[
-            jax.ShapeDtypeStruct((ny, *to_y.shape[1:]), BF16),
-            jax.ShapeDtypeStruct((nx, *to_x.shape[1:]), BF16),
+            jax.ShapeDtypeStruct((n, *a.shape), a.dtype) for n, a in ((ny * nx, codes), (nx, early), (ny, late))
         ],
-        in_specs=[VMEM] * 2,
-        out_specs=[VMEM] * 2,
-        scratch_shapes=[pltpu.SemaphoreType.DMA((2, max(nx, ny)))] * 2,
+        in_specs=[VMEM] * 3,
+        out_specs=[VMEM] * 3,
+        scratch_shapes=[pltpu.SemaphoreType.DMA((3, ny * nx))] * 2,
         compiler_params=pltpu.CompilerParams(
-            collective_id=collective_id, has_side_effects=True, vmem_limit_bytes=LIMIT
+            collective_id=collective_id, has_side_effects=True, vmem_limit_bytes=SMALL
         ),
-    )(to_y, to_x)
+    )(codes, early, late)
 
 
 def sum_kernel(n_sub, n_row, parts, out, by_row, by_sub, own_sem, send, recv):
@@ -375,47 +385,52 @@
             pltpu.SemaphoreType.DMA((3, most)),
             pltpu.SemaphoreType.DMA((3, most)),
         ],
-        compiler_params=pltpu.CompilerParams(collective_id=collective_id, has_side_effects=True),
+        compiler_params=pltpu.CompilerParams(
+            collective_id=collective_id, has_side_effects=True, vmem_limit_bytes=SMALL
+        ),
     )(part.reshape(shape))
     return total.reshape(part.shape)
 
 
-def select_kernel(ny, nx, code_at, codes, own_val, ring_x, ring_y, to_y, to_x, back_at):
+def select_kernel(ny, nx, codes, own_val, ring_x, ring_y, to_y, to_x, back_at, flat, goes, goes_at, sem):
     row = lax.axis_index("row")
     y, x = row // nx, row % nx
-
-    def scatter(device, source, start, size, out, n, mine_of, place_of, mine):
+    late = LB * GROUPS - LB - EARLY
+    flat[...] = codes[:, 0, :]
+    value = flat[...]
+    owner, within = value // 256, value // 16 % 16
+    at = lax.broadcasted_iota(jnp.int32, value.shape, 1)
+    member = jnp.zeros_like(at)
+    for g in range(1, GROUPS):
+        member = member + jnp.where(at >= g * LB, LB, 0)
+    by_x = jnp.where(owner % nx == x, owner // nx, ny) * EARLY + member - LB + within
+    by_y = jnp.where(owner // nx == y, owner % nx, nx) * late + member - LB - EARLY + within
+    goes[...] = jnp.where(at < LB + EARLY, by_x, by_y)
+    copy = pltpu.make_async_copy(goes, goes_at, sem)
+    copy.start()
+    copy.wait()
+
+    def scatter(device, source, start, size, out):
         @pl.loop(0, size // LB)
         def _(g):
             for b in range(LB):
                 k = g * LB + b
-                code = code_at[device, start + k]
-                owner = code // 256
-                slot = g * LB + code // 16 % 16
-                out[jnp.where(mine_of(owner) == mine, place_of(owner), n), slot] = source(k)
-
-    late = LB * GROUPS - LB - EARLY
-
-    def by_x(device, source):
-        scatter(device, source, LB, EARLY, to_y, ny, lambda o: o % nx, lambda o: o // nx, x)
-
-    def by_y(device, source):
-        scatter(device, source, LB + EARLY, late, to_x, nx, lambda o: o // nx, lambda o: o % nx, y)
-
-    by_x(row, lambda k: own_val[LB + k])
-    by_y(row, lambda k: own_val[LB + EARLY + k])
+                out[goes_at[device, start + k]] = source(k)
+
+    scatter(row, lambda k: own_val[LB + k], LB, EARLY, to_y)
+    scatter(row, lambda k: own_val[LB + EARLY + k], LB + EARLY, late, to_x)
 
     @pl.loop(1, nx)
     def _(d):
         t = (x + d) % nx
-        by_x(y * nx + t, lambda k: ring_x[t, k])
+        scatter(y * nx + t, lambda k: ring_x[t, k], LB, EARLY, to_y)
 
     @pl.loop(1, ny)
     def _(d):
         t = (y + d) % ny
-        by_y(t * nx + x, lambda k: ring_y[t, k])
-
-    code = codes[...]
+        scatter(t * nx + x, lambda k: ring_y[t, k], LB + EARLY, late, to_x)
+
+    code = flat[...]
     lane = lax.broadcasted_iota(jnp.int32, code.shape, 1)
     device = lax.broadcasted_iota(jnp.int32, code.shape, 0)
     ours = (code // 256 == row) & (lane >= LB) & (lane < GROUPS * LB)
@@ -487,10 +502,13 @@
         put(3, turned[:KB], jnp.where(is_left((KB, LANES)), turned[KB:], jnp.concatenate([face, face], 1)))
 
 
-def apply_operator(many, col_at, rows_ref, own, group, bnd_all, terms, put_row):
+def apply_operator(many, coarse, col_at, rows_ref, own, group, bnd_all, terms, put_row):
     n_row, n_sub = group.shape[0], bnd_all.shape[0]
 
     def split(values, at, size):
+        if coarse:
+            terms[pl.ds(at, size)] = values
+            return
         for v in range(many):
             hi, mid = two_terms(values[:, v * HALF : (v + 1) * HALF])
             lane = 2 * v * LANES
@@ -516,14 +534,16 @@
             total = None
             for part in range(2):
                 here = range(part * GROUPS, (part + 1) * GROUPS)
-                stack = jnp.concatenate([terms[col_at[a * SLOTS + t]] for t in here], 0)
+                pieces = [terms[col_at[a * SLOTS + t]] for t in here]
+                if coarse and part == 0:
+                    pieces[0] = jnp.zeros_like(pieces[0])
+                stack = jnp.concatenate(pieces, 0)
                 lhs = rows_ref[a, :, part * GROUPS * HALF : (part + 1) * GROUPS * HALF]
                 product = jnp.dot(lhs, stack, preferred_element_type=F32)
                 total = product if total is None else total + product
             blocks = []
             for v in range(many):
-                lane = 2 * v * LANES
-                both = total[:, lane : lane + LANES] + total[:, lane + LANES : lane + 2 * LANES]
+                both = add_terms(coarse, total, v)
                 blocks.append(both[:KB] + swap(both[KB:]))
             put_row(a, blocks)
 
@@ -546,7 +566,7 @@
     def put_row(a, blocks):
         image[block_at(a), :] = jnp.where(left_block, blocks[0], swap(blocks[1]))
 
-    apply_operator(2, col_at, rows_ref, own, group, bnd_all, terms, put_row)
+    apply_operator(2, False, col_at, rows_ref, own, group, bnd_all, terms, put_row)
     for q in range(IFR):
         one, two = landed_blocks(2, landed, q)
         at = block_at(bnd[0, 0, q])
@@ -556,21 +576,34 @@
     gram[...] = hdot(both.T, jnp.where(left, both, swap(image[...])))
 
 
-def apply_kernel(col_at, bnd, rows_ref, own, group, bnd_all, landed, current, image_x, basis, image_b, gram, terms):
+def apply_kernel(
+    coarse, col_at, bnd, rows_ref, own, group, bnd_all, landed, current, image_x, basis, image_b, gram, terms, diagonal
+):
     left_block = is_left((KB, LANES))
 
     def put_row(a, blocks):
         at = block_at(a)
         image_b[at, :] = jnp.where(left_block, blocks[0], image_x[at, :])
 
-    apply_operator(1, col_at, rows_ref, own, group, bnd_all, terms, put_row)
+    apply_operator(1, coarse, col_at, rows_ref, own, group, bnd_all, terms, put_row)
     for q in range(IFR):
         at = block_at(bnd[0, 0, q])
         image_b[at, :] = image_b[at, :] + jnp.where(left_block, landed_blocks(1, landed, q)[0], 0.0)
     y = basis[...]
     turned = y.T
     left = is_left(y.shape)
-    gram[0:LANES] = hdot(turned, image_b[...])
+    if coarse:
+        for a in range(LB):
+            own_terms = jnp.concatenate(two_terms(pack(y[a * KB : (a + 1) * KB])), 1)
+            product = jnp.dot(rows_ref[a, :, :HALF], own_terms, preferred_element_type=F32)
+            both = add_terms(False, product, 0)
+            diagonal[a * KB : (a + 1) * KB] = both[:KB] + swap(both[KB:])
+        twice = jnp.where(left, y + (y - y.astype(BF16).astype(F32)), 0.0)
+        gram[0:LANES] = hdot(turned, jnp.where(left, diagonal[...], image_x[...])) + hdot(
+            twice.T, jnp.where(left, image_b[...], 0.0)
+        )
+    else:
+        gram[0:LANES] = hdot(turned, image_b[...])
     gram[LANES : 2 * LANES] = hdot(turned, jnp.where(left, image_x[...], swap(current[...])))
     gram[2 * LANES :] = hdot(turned, y)
 
@@ -644,10 +677,10 @@
     basis[at, :] = jnp.where(left, fresh, here)
 
 
-def send_basis(update, packed, bnd_out, parts, bnd, face_row, face_src, face_val):
+def send_basis(coarse, update, packed, bnd_out, parts, bnd, face_row, face_src, face_val):
     for a in range(LB):
-        packed[a] = pack(update[a * KB : (a + 1) * KB, :])
-    write_messages(1, packed, bnd_out, parts, bnd, face_row, face_src, face_val)
+        packed[a] = pack(update[a * KB : (a + 1) * KB, :]).astype(packed.dtype)
+    write_messages(1, coarse, packed, bnd_out, parts, bnd, face_row, face_src, face_val)
 
 
 def first_ritz_kernel(
@@ -658,11 +691,16 @@
     left = is_left((KB, LANES))
     ritz = padded(jnp.where(left, swap(work[...]), 0.0))
     chunks(lambda at: new_basis(ritz, precond, current, image_x, basis, update, at))
-    send_basis(update, packed, bnd_out, parts, bnd, face_row, face_src, face_val)
+    send_basis(False, update, packed, bnd_out, parts, bnd, face_row, face_src, face_val)
 
 
 def combine(total_rows, gram, metric, wide, narrow):
-    wide[:, :LANES] = gram[0:LANES]
+    energy = gram[0:LANES]
+    turned = energy.T
+    upper = lax.broadcasted_iota(jnp.int32, (LANES, LANES), 0) < KB
+    right_half = lax.broadcasted_iota(jnp.int32, (LANES, LANES), 1) >= KB
+    crossed = jnp.where(upper, energy, turned)
+    wide[:, :LANES] = jnp.where(upper == right_half, crossed, 0.5 * (energy + turned))
     right = gram[LANES : 2 * LANES]
     wide[:, LANES:] = right
     eliminate(wide, LANES, True)
@@ -718,7 +756,7 @@
         new_basis(ritz, precond, next_current, next_image, next_basis, update, at)
 
     chunks(body)
-    send_basis(update, packed, bnd_out, parts, bnd, face_row, face_src, face_val)
+    send_basis(True, update, packed, bnd_out, parts, bnd, face_row, face_src, face_val)
 
 
 def last_kernel(total_rows, gram, metric, current, basis, modes, search, both, wide, narrow):
@@ -758,10 +796,10 @@
     own_val = jnp.concatenate([vals[:, :HALF], vals[:, HALF:]], 2)
     faces = (bnd_rows, if_row, if_src)
 
-    def sent(many):
+    def sent(many, kind=F32):
         return [
-            shape(LB, many * HALF, LANES),
-            shape(IFR, many * HALF, LANES),
+            jax.ShapeDtypeStruct((LB, many * HALF, LANES), kind),
+            jax.ShapeDtypeStruct((IFR, many * HALF, LANES), kind),
             shape(2, n_sub // 2, IFR, many * HALF, LANES),
         ]
 
@@ -779,31 +817,32 @@
     )
     cols = in_col[0]
     codes = cols // LB * 256 + cols % LB * 16 + in_row[0]
-    codes = jnp.pad(codes, ((0, 15), (0, LANES - GROUPS * LB)))
+    codes = jnp.pad(codes, ((0, 7), (0, LANES - GROUPS * LB)))
     early = own_val[LB : LB + EARLY].reshape(-1, LANES)
     late = own_val[LB + EARLY :].reshape(-1, LANES)
-    group, codes_all, ring_x, ring_y, bnd_all, landed = exchange(
-        0, ny, nx, [shard.reshape(-1, LANES), codes], [early, late], bnd, parts
-    )
-    codes_all = lax.dynamic_update_slice(codes_all[:, 0], codes[:1], (lax.axis_index("row"), 0))
+    codes_all, ring_x, ring_y = ring_gather(6, ny, nx, codes, early, late)
     in_early, in_late = EARLY, GROUPS * LB - LB - EARLY
 
-    def blocks(n, count):
-        return jax.ShapeDtypeStruct((n, count, HALF, LANES), BF16)
+    def blocks(count):
+        return jax.ShapeDtypeStruct((count, HALF, LANES), BF16)
 
     to_y, to_x, back_at = plain(
         functools.partial(select_kernel, ny, nx),
         "select",
-        [SMEM] + [VMEM] * 4,
-        [blocks(ny + 1, in_early), blocks(nx + 1, in_late), jax.ShapeDtypeStruct((16, LANES), jnp.int32)],
-        [],
-        codes_all,
+        [VMEM] * 4,
+        [blocks((ny + 1) * in_early), blocks((nx + 1) * in_late), jax.ShapeDtypeStruct((16, LANES), jnp.int32)],
+        [pltpu.VMEM((n_row, LANES), jnp.int32)] * 2
+        + [pltpu.SMEM((n_row, LANES), jnp.int32), pltpu.SemaphoreType.DMA],
         codes_all,
         own_val,
         ring_x.reshape(nx, in_early, HALF, LANES),
         ring_y.reshape(ny, in_late, HALF, LANES),
     )
-    from_y, from_x = hand_on(6, ny, nx, to_y, to_x)
+    to_y = to_y.reshape(ny + 1, in_early, HALF, LANES)
+    to_x = to_x.reshape(nx + 1, in_late, HALF, LANES)
+    group, from_y, from_x, bnd_all, landed = exchange(
+        0, ny, nx, [shard.reshape(-1, LANES)], [to_y, to_x], bnd, parts
+    )
     block_rows, col_at = pl.pallas_call(
         functools.partial(build_kernel, ny, nx),
         name="build",
@@ -850,12 +889,16 @@
     solver = [pltpu.VMEM((rows_here, LANES), F32), pltpu.VMEM((LANES, 2 * LANES), F32), pltpu.VMEM((KB, LANES), F32)]
     for sweep in range(ITERS):
         group, bnd_all, landed = exchange(2 + 2 * sweep, ny, nx, [packed.reshape(-1, LANES)], [], bnd, parts)
+        coarse = sweep == ITERS - 1
         image_b, gram = plain(
-            apply_kernel,
-            "apply",
+            functools.partial(apply_kernel, coarse),
+            f"apply_{sweep}",
             [SMEM] * 2 + [VMEM] * 8,
             [shape(rows_here, LANES), shape(3 * LANES, LANES)],
-            [pltpu.VMEM((blocks_all, HALF, 2 * LANES), BF16)],
+            [
+                pltpu.VMEM((blocks_all, HALF, LANES if coarse else 2 * LANES), BF16),
+                pltpu.VMEM((rows_here, LANES), F32),
+            ],
             col_at,
             bnd_rows,
             block_rows,
@@ -873,7 +916,7 @@
                 functools.partial(step_kernel, total_rows),
                 "step",
                 [SMEM] * 3 + [VMEM] * 8,
-                [shape(KB, LANES), shape(rows_here, LANES), shape(rows_here, LANES), shape(rows_here, LANES), *sent(1)],
+                [shape(KB, LANES), shape(rows_here, LANES), shape(rows_here, LANES), shape(rows_here, LANES), *sent(1, BF16)],
                 solver,
                 *faces,
                 gram,

time: 305 us -> 273 us (0.90)
  local copies, waits for them, and re-layouts: 21.5 us -> 3.6 us
  Pallas kernels: 281 us -> 267 us
    unnamed x63 -> x19, local copies, waits for them, and re-layouts: 20.2 us -> 3.31 us
    pallas_call x4, Pallas kernels: 148 us -> 141 us  [the longest x3 115 us: exchange(): pl.pallas_call(functools.partial(exchange_kernel, count, bool(handed), ny...]
    pallas_call x8, Pallas kernels: 59.3 us -> 54.2 us  [plain(): pl.pallas_call(kernel, name=name, out_shape=outs, in_specs=specs, out_spe...]
where the time goes in v3:
time: 273 us
  Pallas kernels  267 us (98%)
  local copies, waits for them, and re-layouts  3.6 us (1%)
    pallas_call x3, Pallas kernels, exchange(): pl.pallas_call(functools.partial(exchange_kernel, count, bool(handed), ny...  115 us
    pallas_call x3, Pallas kernels, sum_all(): pl.pallas_call(functools.partial(sum_kernel, n_sub, n_row), name=f'sum_{c...  67.2 us
    pallas_call x8, Pallas kernels, plain(): pl.pallas_call(kernel, name=name, out_shape=outs, in_specs=specs, out_spe...  54.2 us
    pallas_call x1, Pallas kernels, ring_gather(): pl.pallas_call(functools.partial(rings_kernel, ny, nx), name=f'rings_{col...  26 us

profile of v3, /device:TPU:1, one launch (start us, length us, event | category | flops | bytes accessed | tf_op | source)
XLA Modules:
  0.0 273.3 jit_solution(4923148231014848641)
XLA Ops:
  0.6 0.7 fusion.5
  1.3 3.3 %copy.12 = bf16[1,1,96,64,64]{4,3,2,1,0:T(8,128)(2,1)S(1)} copy(bf16[1,1,96,64,64]{2,4,3,1,0:T(8,128)(2,1)} %param.15) | data formatting | bytes 1572864 | tf_op args[5]
  4.6 0.3 fusion.6
  4.9 0.2 fusion.1
  5.1 0.2 fusion
  5.3 0.4 pad_maximum_fusion.own_val
  5.7 26.0 %rings_6.1 = (s32[16,8,128]{2,1,0:T(8,128)S(1)}, bf16[4,1536,128]{2,1,0:T(8,128)(2,1)S(1)}, bf16[4,1152,128]{2,1,0:T(8,128)(2,1)S(1)}) custom-call(s32[8,128]{1,0:T(8,128)S(1)} %pad.4.codes, bf16[1536,128]{1,0:T(8,128)(2,1)S(1)} %bitcast.52, bf16[1152,128]{1,0:T(8,128)(2,1)S(1)} %bitcast.54), custom_call_target="tpu_custom_call" | custom-call | tf_op jit(solution)/shard_map/rings_6/pallas_call | solution.py:301
  31.7 0.0 copy-start
  31.7 0.0 copy-start.1
  31.7 0.0 copy-start.2
  31.8 0.0 copy-start.3
  31.8 0.0 copy-start.4
  31.8 0.0 copy-start.5
  31.8 0.0 copy-start.6
  31.8 2.0 select.2
  33.8 0.0 copy-done
  33.8 0.0 copy-done.1
  33.8 0.0 copy-done.2
  33.8 0.0 copy-done.3
  33.8 0.0 copy-done.4
  33.8 0.0 copy-done.5
  33.9 0.0 copy-done.6
  33.9 1.7 start.1
  35.6 0.0 copy-start.7
  35.6 0.0 copy-start.8
  35.6 68.1 %exchange_0.1 = (f32[16,768,128]{2,1,0:T(8,128)S(1)}, bf16[4,48,32,128]{3,2,1,0:T(8,128)(2,1)S(1)}, bf16[4,36,32,128]{3,2,1,0:T(8,128)(2,1)S(1)}, f32[16,3,64,128]{3,2,1,0:T(8,128)S(1)}, f32[8,3,64,128]{3,2,1,0:T(8,128)S(1)}) custom-call(f32[768,128]{1,0:T(8,128)S(1)} %bitcast.50, bf16[5,48,32,128]{3,2,1,0:T(8,128)(2,1)S(1)} %bitcast.43, ...), custom_call_target="tpu_custom_call" | custom-call | tf_op jit(solution)/shard_map/exchange_0/pallas_call | solution.py:242
  103.7 0.0 copy-done.7
  103.7 0.0 copy-done.8
  103.7 5.3 %build.1 = (bf16[12,128,512]{2,1,0:T(8,128)(2,1)S(1)}, s32[192]{0:T(256)S(1)}) custom-call(s32[1,1,96]{2,1,0:T(1,128)S(1)} %copy-done.7, s32[1,1,96]{2,1,0:T(1,128)S(1)} %copy-done.8, s32[16,128]{1,0:T(8,128)S(1)} %get-tuple-element.47.back_at, s32[1,1,12]{2,1,0:T(1,128)S(1)} %copy-done.4, s32[1,1,12]{2,1,0:T(1,128)S(1)} %copy-done.5, ...), custom_call_target="tpu_custom_call" | custom-call | tf_op jit(solution)/shard_map/build/pallas_call | solution.py:846
  109.0 4.9 %first_apply.1 = (f32[768,128]{1,0:T(8,128)S(1)}, f32[128,128]{1,0:T(8,128)S(1)}) custom-call(s32[192]{0:T(256)S(1)} %get-tuple-element.55.col_at, s32[1,1,3]{2,1,0:T(1,128)S(1)} %copy-done.3, bf16[12,128,512]{2,1,0:T(8,128)(2,1)S(1)} %get-tuple-element.56.rows_ref, f32[12,64,128]{2,1,0:T(8,128)S(1)} %get-tuple-element.50.own, ...), custom_call_target="tpu_custom_call" | custom-call | tf_op jit(solution)/shard_map/first_apply/pallas_call | solution.py:775
  113.9 22.2 %sum_1.1 = f32[16,8,128]{2,1,0:T(8,128)S(1)} custom-call(f32[16,8,128]{2,1,0:T(8,128)S(1)} %bitcast.64), custom_call_target="tpu_custom_call" | custom-call | tf_op jit(solution)/shard_map/sum_1/pallas_call | solution.py:375
  136.1 5.4 %first_ritz.1 = (f32[768,128]{1,0:T(8,128)S(1)}, f32[12,32,128]{2,1,0:T(8,128)S(1)}, f32[3,32,128]{2,1,0:T(8,128)S(1)}, f32[2,8,3,32,128]{4,3,2,1,0:T(8,128)S(1)}) custom-call(s32[1,1,3]{2,1,0:T(1,128)S(1)} %copy-done.3, s32[1,1,12]{2,1,0:T(1,128)S(1)} %copy-done.4, s32[1,1,12]{2,1,0:T(1,128)S(1)} %copy-done.5, f32[128,128]{1,0:T(8,128)S(1)} %bitcast.58, ...), custom_call_target="tpu_custom_call" | custom-call | tf_op jit(solution)/shard_map/first_ritz/pallas_call | solution.py:775
  141.5 27.3 %exchange_2.1 = (f32[16,384,128]{2,1,0:T(8,128)S(1)}, f32[16,3,32,128]{3,2,1,0:T(8,128)S(1)}, f32[8,3,32,128]{3,2,1,0:T(8,128)S(1)}) custom-call(f32[384,128]{1,0:T(8,128)S(1)} %bitcast.57, f32[3,32,128]{2,1,0:T(8,128)S(1)} %get-tuple-element.65.refs_1_, f32[2,8,3,32,128]{4,3,2,1,0:T(8,128)S(1)} %get-tuple-element.66.refs_2_), custom_call_target="tpu_custom_call" | custom-call | tf_op jit(solution)/shard_map/exchange_2/pallas_call | solution.py:242
  168.8 4.0 %apply_0.1 = (f32[768,128]{1,0:T(8,128)S(1)}, f32[384,128]{1,0:T(8,128)S(1)}) custom-call(s32[192]{0:T(256)S(1)} %get-tuple-element.55.col_at, s32[1,1,3]{2,1,0:T(1,128)S(1)} %copy-done.3, bf16[12,128,512]{2,1,0:T(8,128)(2,1)S(1)} %get-tuple-element.56.rows_ref, f32[12,32,128]{2,1,0:T(8,128)S(1)} %get-tuple-element.64.own, f32[16,12,32,128]{3,2,1,0:T(8,128)S(1)} %bitcast.48, ...), custom_call_target="tpu_custom_call" | custom-call | tf_op jit(solution)/shard_map/apply_0/pallas_call | solution.py:775
  172.8 22.2 %sum_3.1 = f32[16,24,128]{2,1,0:T(8,128)S(1)} custom-call(f32[16,24,128]{2,1,0:T(8,128)S(1)} %bitcast.61), custom_call_target="tpu_custom_call" | custom-call | tf_op jit(solution)/shard_map/sum_3/pallas_call | solution.py:375
  195.1 16.8 %step.1 = (f32[64,128]{1,0:T(8,128)S(1)}, f32[768,128]{1,0:T(8,128)S(1)}, f32[768,128]{1,0:T(8,128)S(1)}, f32[768,128]{1,0:T(8,128)S(1)}, bf16[12,32,128]{2,1,0:...) custom-call(s32[1,1,3]{2,1,0:T(1,128)S(1)} %copy-done.3, ...), custom_call_target="tpu_custom_call" | custom-call | tf_op jit(solution)/shard_map/step/pallas_call | solution.py:775
  211.9 19.2 %exchange_4.1 = (bf16[16,384,128]{2,1,0:T(8,128)(2,1)S(1)}, bf16[16,3,32,128]{3,2,1,0:T(8,128)(2,1)S(1)}, f32[8,3,32,128]{3,2,1,0:T(8,128)S(1)}) custom-call(bf16[384,128]{1,0:T(8,128)(2,1)S(1)} %bitcast.59, bf16[3,32,128]{2,1,0:T(8,128)(2,1)S(1)} %get-tuple-element.74.refs_1_, f32[2,8,3,32,128]{4,3,2,1,0:T(8,128)S(1)} %get-tuple-element.75.refs_2_), custom_call_target="tpu_custom_call" | custom-call | tf_op jit(solution)/shard_map/exchange_4/pallas_call | solution.py:242
  231.1 4.4 %apply_1.1 = (f32[768,128]{1,0:T(8,128)}, f32[384,128]{1,0:T(8,128)S(1)}) custom-call(s32[192]{0:T(256)S(1)} %get-tuple-element.55.col_at, s32[1,1,3]{2,1,0:T(1,128)S(1)} %copy-done.3, bf16[12,128,512]{2,1,0:T(8,128)(2,1)S(1)} %get-tuple-element.56.rows_ref, bf16[12,32,128]{2,1,0:T(8,128)(2,1)S(1)} %get-tuple-element.73.own, ...), custom_call_target="tpu_custom_call" | custom-call | tf_op jit(solution)/shard_map/apply_1/pallas_call | solution.py:775
  235.5 22.8 %sum_5.1 = f32[16,24,128]{2,1,0:T(8,128)S(1)} custom-call(f32[16,24,128]{2,1,0:T(8,128)S(1)} %bitcast.60), custom_call_target="tpu_custom_call" | custom-call | tf_op jit(solution)/shard_map/sum_5/pallas_call | solution.py:375
  258.3 15.1 %last.1 = (f32[64,768]{1,0:T(8,128)}, f32[64,768]{1,0:T(8,128)}) custom-call(f32[384,128]{1,0:T(8,128)S(1)} %bitcast.56, f32[64,128]{1,0:T(8,128)S(1)} %get-tuple-element.83.metric, f32[768,128]{1,0:T(8,128)S(1)} %get-tuple-element.79.current, f32[768,128]{1,0:T(8,128)S(1)} %get-tuple-element.81.basis), custom_call_target="tpu_custom_call" | custom-call | tf_op jit(solution)/shard_map/last/pallas_call | solution.py:775
  (2 shorter events, 0.0 us)
Async XLA Ops:
  31.7 2.1 copy-start
  31.7 2.1 copy-start.1
  31.7 2.1 copy-start.2
  31.8 2.1 copy-start.3
  31.8 2.1 copy-start.4
  31.8 2.1 copy-start.5
  31.8 2.1 copy-start.6
  35.6 68.1 %copy-start.7 = (s32[1,1,96]{2,1,0:T(1,128)S(1)}, s32[1,1,96]{2,1,0:T(1,128)}, u32[]{:S(2)}) copy-start(s32[1,1,96]{2,1,0:T(1,128)} %in_row.1) | copy-start | bytes 1156
  35.6 68.1 %copy-start.8 = (s32[1,1,96]{2,1,0:T(1,128)S(1)}, s32[1,1,96]{2,1,0:T(1,128)}, u32[]{:S(2)}) copy-start(s32[1,1,96]{2,1,0:T(1,128)} %in_col.1) | copy-start | bytes 1156

commit v4 on v3

--- a/solution.py
+++ b/solution.py
@@ -85,18 +85,20 @@
         parts[core, z, slot] = parts[core, z, slot] + products[k]
 
 
-def start_kernel(bnd, face_row, face_src, modes, search, precond, face_val, current, shard, bnd_out, parts, weights):
+def start_kernel(bnd, face_row, face_src, modes, search, precond, face_val, current, *refs):
+    first, second, weights = refs[:3], refs[3:6], refs[6]
     current[...] = jnp.concatenate([modes[...], search[...]], 0).T
     for a in range(LB):
         block = current[a * KB : (a + 1) * KB]
-        shard[a, :HALF] = pack(block)
-        shard[a, HALF:] = pack(swap(block))
+        first[0][a] = pack(block)
+        second[0][a] = pack(swap(block))
     for c in range(LB * KB // LANES):
         weights[c * LANES : (c + 1) * LANES] = jnp.broadcast_to(precond[c : c + 1], (LANES, LANES)).T
-    write_messages(2, False, shard, bnd_out, parts, bnd, face_row, face_src, face_val)
-
-
-def exchange_kernel(count, handing, ny, nx, n_sub, *refs):
+    write_messages(1, False, *first, bnd, face_row, face_src, face_val)
+    write_messages(1, False, *second, bnd, face_row, face_src, face_val)
+
+
+def exchange_steps(greet, count, handing, ny, nx, n_sub, *refs):
     arrays = count + 2 * handing
     shards, bnd, parts = refs[:arrays], refs[arrays], refs[arrays + 1]
     groups, bnd_all, landed = refs[arrays + 2 : 2 * arrays + 2], refs[2 * arrays + 2], refs[2 * arrays + 3]
@@ -113,15 +115,16 @@
     def along(d):
         return ((z + d + nz) % nz) * 2 + core
 
-    barrier = pltpu.get_barrier_semaphore()
-    for d in range(1, nx):
-        pl.semaphore_signal(barrier, inc=1, device_id={"row": at(0, d)}, device_id_type=MESH)
-    for d in range(1, ny):
-        pl.semaphore_signal(barrier, inc=1, device_id={"row": at(d, 0)}, device_id_type=MESH)
-    for d in range(1, nz):
-        pl.semaphore_signal(barrier, inc=1, device_id={"sub": along(d)}, device_id_type=MESH)
-    pl.semaphore_signal(barrier, inc=1, device_id={"sub": sibling}, device_id_type=MESH)
-    pl.semaphore_wait(barrier, nx - 1 + ny - 1 + nz)
+    if greet:
+        barrier = pltpu.get_barrier_semaphore()
+        for d in range(1, nx):
+            pl.semaphore_signal(barrier, inc=1, device_id={"row": at(0, d)}, device_id_type=MESH)
+        for d in range(1, ny):
+            pl.semaphore_signal(barrier, inc=1, device_id={"row": at(d, 0)}, device_id_type=MESH)
+        for d in range(1, nz):
+            pl.semaphore_signal(barrier, inc=1, device_id={"sub": along(d)}, device_id_type=MESH)
+        pl.semaphore_signal(barrier, inc=1, device_id={"sub": sibling}, device_id_type=MESH)
+        pl.semaphore_wait(barrier, nx - 1 + ny - 1 + nz)
 
     def to_sub(src, dst, kind, d, target):
         return pltpu.make_async_remote_copy(
@@ -193,6 +196,7 @@
                 )
             )
 
+    yield
     landed_at(theirs, sub_recv.at[3, 0])
     ours[...] = theirs[...] + parts[core]
     for d in range(1, nz):
@@ -214,6 +218,7 @@
                 here = bnd_all.at[along(-d)]
                 landed_at(here, sub_recv.at[0, d])
                 send(to_sub(here, here, 1, d, sibling))
+    yield
     for d in range(1, nz):
         landed_at(landed.at[(z + nz - d) % nz], sub_recv.at[2, d])
     for d in range(nz):
@@ -232,11 +237,29 @@
         copy.wait_send()
 
 
+def exchange_kernel(*args):
+    for _ in exchange_steps(True, *args):
+        pass
+
+
+def exchange_scratch(count, ny, nx, parts):
+    most, n_row = max(parts.shape[1], 2), ny * nx
+    return [
+        pltpu.VMEM(parts.shape[1:], F32),
+        pltpu.VMEM(parts.shape[1:], F32),
+        pltpu.SemaphoreType.DMA((4, most)),
+        pltpu.SemaphoreType.DMA((4, most)),
+        pltpu.SemaphoreType.DMA((count, 2, n_row)),
+        pltpu.SemaphoreType.DMA((count, 2, n_row)),
+        pltpu.SemaphoreType.DMA((2, max(nx, ny))),
+        pltpu.SemaphoreType.DMA((2, max(nx, ny))),
+    ]
+
+
 def exchange(collective_id, ny, nx, shards, handed, bnd, parts):
     count, n_row = len(shards), ny * nx
     nz = parts.shape[1]
     n_sub = 2 * nz
-    most = max(nz, 2)
     gathered = [jax.ShapeDtypeStruct((n_row, *a.shape), a.dtype) for a in shards]
     gathered += [jax.ShapeDtypeStruct((n, *a.shape[1:]), a.dtype) for n, a in zip((ny, nx), handed)]
     return pl.pallas_call(
@@ -246,16 +269,7 @@
         + [jax.ShapeDtypeStruct((n_sub, *bnd.shape), bnd.dtype), jax.ShapeDtypeStruct(parts.shape[1:], F32)],
         in_specs=[VMEM] * (len(gathered) + 2),
         out_specs=[VMEM] * (len(gathered) + 2),
-        scratch_shapes=[
-            pltpu.VMEM(parts.shape[1:], F32),
-            pltpu.VMEM(parts.shape[1:], F32),
-            pltpu.SemaphoreType.DMA((4, most)),
-            pltpu.SemaphoreType.DMA((4, most)),
-            pltpu.SemaphoreType.DMA((count, 2, n_row)),
-            pltpu.SemaphoreType.DMA((count, 2, n_row)),
-            pltpu.SemaphoreType.DMA((2, max(nx, ny))),
-            pltpu.SemaphoreType.DMA((2, max(nx, ny))),
-        ],
+        scratch_shapes=exchange_scratch(count, ny, nx, parts),
         compiler_params=pltpu.CompilerParams(
             collective_id=collective_id, has_side_effects=True, vmem_limit_bytes=SMALL
         ),
@@ -276,18 +290,21 @@
         (n_row, row, lambda t: t, codes, codes_all),
     )
     sends = []
-    for i, (n, mine, name, src, dst) in enumerate(rings):
-        for d in range(1, n):
-            copy = pltpu.make_async_remote_copy(
-                src_ref=src,
-                dst_ref=dst.at[mine],
-                send_sem=send.at[i, d],
-                recv_sem=recv.at[i, d],
-                device_id={"row": name((mine + d) % n)},
-                device_id_type=MESH,
-            )
-            copy.start()
-            sends.append(copy)
+    order = [(2, d) for d in range(1, n_row)]
+    for d in range(1, max(nx, ny)):
+        order += [(i, (d, rings[i][0] - d)[i]) for i in range(2) if d < rings[i][0]]
+    for i, d in order:
+        n, mine, name, src, dst = rings[i]
+        copy = pltpu.make_async_remote_copy(
+            src_ref=src,
+            dst_ref=dst.at[mine],
+            send_sem=send.at[i, d],
+            recv_sem=recv.at[i, d],
+            device_id={"row": name((mine + d) % n)},
+            device_id_type=MESH,
+        )
+        copy.start()
+        sends.append(copy)
     codes_all[row] = codes[...]
     for i, (n, mine, _, _, dst) in enumerate(rings):
         for d in range(1, n):
@@ -313,7 +330,7 @@
     )(codes, early, late)
 
 
-def sum_kernel(n_sub, n_row, parts, out, by_row, by_sub, own_sem, send, recv):
+def sum_steps(n_sub, n_row, parts, out, by_row, by_sub, own_sem, send, recv):
     sub, row = lax.axis_index("sub"), lax.axis_index("row")
     barrier = pltpu.get_barrier_semaphore()
 
@@ -346,6 +363,7 @@
             to(d).start()
 
         own.start()
+        yield
 
         @pl.loop(1, n)
         def _(d):
@@ -361,16 +379,31 @@
             total = total + buffer[t]
         return total
 
-    phase(0, "row", row, n_row, lambda t: parts.at[t], lambda t: by_row.at[t])
+    yield from phase(0, "row", row, n_row, lambda t: parts.at[t], lambda t: by_row.at[t])
     by_row[n_row] = summed(by_row, n_row)
-    phase(1, "sub", sub, n_sub, lambda t: by_row.at[n_row], lambda t: by_sub.at[t])
+    yield from phase(1, "sub", sub, n_sub, lambda t: by_row.at[n_row], lambda t: by_sub.at[t])
     by_sub[n_sub] = summed(by_sub, n_sub)
-    phase(2, "row", row, n_row, lambda t: by_sub.at[n_sub], lambda t: out.at[t])
+    yield from phase(2, "row", row, n_row, lambda t: by_sub.at[n_sub], lambda t: out.at[t])
+
+
+def sum_kernel(*args):
+    for _ in sum_steps(*args):
+        pass
+
+
+def sum_scratch(n_sub, n_row, rows):
+    most = max(n_sub, n_row)
+    return [
+        pltpu.VMEM((n_row + 1, rows, LANES), F32),
+        pltpu.VMEM((n_sub + 1, rows, LANES), F32),
+        pltpu.SemaphoreType.DMA((3,)),
+        pltpu.SemaphoreType.DMA((3, most)),
+        pltpu.SemaphoreType.DMA((3, most)),
+    ]
 
 
 def sum_all(collective_id, n_sub, n_row, part):
     rows = part.shape[0] // n_row
-    most = max(n_sub, n_row)
     shape = (n_row, rows, LANES)
     total = pl.pallas_call(
         functools.partial(sum_kernel, n_sub, n_row),
@@ -378,18 +411,47 @@
         out_shape=jax.ShapeDtypeStruct(shape, F32),
         in_specs=[VMEM],
         out_specs=VMEM,
-        scratch_shapes=[
-            pltpu.VMEM((n_row + 1, rows, LANES), F32),
-            pltpu.VMEM((n_sub + 1, rows, LANES), F32),
-            pltpu.SemaphoreType.DMA((3,)),
-            pltpu.SemaphoreType.DMA((3, most)),
-            pltpu.SemaphoreType.DMA((3, most)),
-        ],
+        scratch_shapes=sum_scratch(n_sub, n_row, rows),
         compiler_params=pltpu.CompilerParams(
             collective_id=collective_id, has_side_effects=True, vmem_limit_bytes=SMALL
         ),
     )(part.reshape(shape))
     return total.reshape(part.shape)
+
+
+def sum_beside_exchange_kernel(ny, nx, n_sub, part, shard, bnd, parts, total, group, bnd_all, landed, *scratch):
+    summing = sum_steps(n_sub, ny * nx, part, total, *scratch[:5])
+    moving = exchange_steps(
+        False, 1, False, ny, nx, n_sub, shard, bnd, parts, group, bnd_all, landed, *scratch[5:]
+    )
+    for _ in range(3):
+        next(summing)
+        next(moving, None)
+    for _ in summing:
+        pass
+
+
+def sum_beside_exchange(collective_id, ny, nx, part, shard, bnd, parts):
+    n_row = ny * nx
+    n_sub = 2 * parts.shape[1]
+    rows = part.shape[0] // n_row
+    total, *moved = pl.pallas_call(
+        functools.partial(sum_beside_exchange_kernel, ny, nx, n_sub),
+        name=f"sum_beside_exchange_{collective_id}",
+        out_shape=[
+            shape(n_row, rows, LANES),
+            shape(n_row, *shard.shape),
+            shape(n_sub, *bnd.shape),
+            shape(*parts.shape[1:]),
+        ],
+        in_specs=[VMEM] * 4,
+        out_specs=[VMEM] * 4,
+        scratch_shapes=sum_scratch(n_sub, n_row, rows) + exchange_scratch(1, ny, nx, parts),
+        compiler_params=pltpu.CompilerParams(
+            collective_id=collective_id, has_side_effects=True, vmem_limit_bytes=SMALL
+        ),
+    )(part.reshape(n_row, rows, LANES), shard, bnd, parts)
+    return total.reshape(part.shape), *moved
 
 
 def select_kernel(ny, nx, codes, own_val, ring_x, ring_y, to_y, to_x, back_at, flat, goes, goes_at, sem):
@@ -564,26 +626,35 @@
     left_block = is_left((KB, LANES))
 
     def put_row(a, blocks):
-        image[block_at(a), :] = jnp.where(left_block, blocks[0], swap(blocks[1]))
-
-    apply_operator(2, False, col_at, rows_ref, own, group, bnd_all, terms, put_row)
+        image[block_at(a), :] = jnp.where(left_block, blocks[0], 0.0)
+
+    apply_operator(1, False, col_at, rows_ref, own, group, bnd_all, terms, put_row)
     for q in range(IFR):
-        one, two = landed_blocks(2, landed, q)
         at = block_at(bnd[0, 0, q])
-        image[at, :] = image[at, :] + jnp.where(left_block, one, swap(two))
+        image[at, :] = image[at, :] + jnp.where(left_block, landed_blocks(1, landed, q)[0], 0.0)
     both = basis[...]
     left = is_left(both.shape)
     gram[...] = hdot(both.T, jnp.where(left, both, swap(image[...])))
 
 
-def apply_kernel(
-    coarse, col_at, bnd, rows_ref, own, group, bnd_all, landed, current, image_x, basis, image_b, gram, terms, diagonal
-):
+def apply_kernel(coarse, col_at, bnd, rows_ref, own, group, bnd_all, landed, *refs):
+    *search, current, image_x, basis, image_b, gram, terms, diagonal = refs
     left_block = is_left((KB, LANES))
+    source = image_x
+    if search:
+        source = image_b
+
+        def put_search(a, blocks):
+            image_b[block_at(a), :] = swap(blocks[0])
+
+        apply_operator(1, False, col_at, rows_ref, *search[:3], terms, put_search)
+        for q in range(IFR):
+            at = block_at(bnd[0, 0, q])
+            image_b[at, :] = image_b[at, :] + jnp.where(left_block, 0.0, swap(landed_blocks(1, search[3], q)[0]))
 
     def put_row(a, blocks):
         at = block_at(a)
-        image_b[at, :] = jnp.where(left_block, blocks[0], image_x[at, :])
+        image_b[at, :] = jnp.where(left_block, blocks[0], source[at, :])
 
     apply_operator(1, coarse, col_at, rows_ref, own, group, bnd_all, terms, put_row)
     for q in range(IFR):
@@ -803,11 +874,11 @@
             shape(2, n_sub // 2, IFR, many * HALF, LANES),
         ]
 
-    current, shard, bnd, parts, weights = plain(
+    current, shard, bnd, parts, shard_p, bnd_p, parts_p, weights = plain(
         start_kernel,
         "start",
         [SMEM] * 3 + [VMEM] * 4,
-        [shape(rows_here, LANES), *sent(2), shape(rows_here, LANES)],
+        [shape(rows_here, LANES), *sent(1), *sent(1), shape(rows_here, LANES)],
         [],
         *faces,
         modes.T,
@@ -861,17 +932,17 @@
         "first_apply",
         [SMEM] * 2 + [VMEM] * 6,
         [shape(rows_here, LANES), shape(LANES, LANES)],
-        [pltpu.VMEM((blocks_all, HALF, 4 * LANES), BF16)],
+        [pltpu.VMEM((blocks_all, HALF, 2 * LANES), BF16)],
         col_at,
         bnd_rows,
         block_rows,
         shard,
-        group.reshape(n_row, LB, 2 * HALF, LANES),
+        group.reshape(n_row, LB, HALF, LANES),
         bnd_all,
         landed,
         current,
     )
-    metric = sum_all(1, n_sub, n_row, gram)
+    metric, group_p, bnd_p, landed_p = sum_beside_exchange(1, ny, nx, gram, shard_p.reshape(-1, LANES), bnd_p, parts_p)
     basis, packed, bnd, parts = plain(
         first_ritz_kernel,
         "first_ritz",
@@ -893,7 +964,7 @@
         image_b, gram = plain(
             functools.partial(apply_kernel, coarse),
             f"apply_{sweep}",
-            [SMEM] * 2 + [VMEM] * 8,
+            [SMEM] * 2 + [VMEM] * (12 if sweep == 0 else 8),
             [shape(rows_here, LANES), shape(3 * LANES, LANES)],
             [
                 pltpu.VMEM((blocks_all, HALF, LANES if coarse else 2 * LANES), BF16),
@@ -906,6 +977,7 @@
             group.reshape(n_row, LB, HALF, LANES),
             bnd_all,
             landed,
+            *((shard_p, group_p.reshape(n_row, LB, HALF, LANES), bnd_p, landed_p) if sweep == 0 else ()),
             current,
             image_x,
             basis,

time: 273 us -> 267 us (0.978)
  Pallas kernels: 267 us -> 261 us
    pallas_call x0 -> x1, Pallas kernels: none -> 32.7 us  [sum_beside_exchange(): pl.pallas_call(functools.partial(sum_beside_exchange_kernel, ny, nx, n_su...]
    pallas_call x3 -> x2, Pallas kernels: 67.2 us -> 47.1 us  [sum_all(): pl.pallas_call(functools.partial(sum_kernel, n_sub, n_row), name=f'sum_{c...]
    pallas_call x3, Pallas kernels: 115 us -> 94.6 us  [exchange(): pl.pallas_call(functools.partial(exchange_kernel, count, bool(handed), ny...]
where the time goes in v4:
time: 267 us
  Pallas kernels  261 us (98%)
  local copies, waits for them, and re-layouts  3.6 us (1%)
    pallas_call x3, Pallas kernels, exchange(): pl.pallas_call(functools.partial(exchange_kernel, count, bool(handed), ny...  94.6 us
    pallas_call x8, Pallas kernels, plain(): pl.pallas_call(kernel, name=name, out_shape=outs, in_specs=specs, out_spe...  55.7 us
    pallas_call x2, Pallas kernels, sum_all(): pl.pallas_call(functools.partial(sum_kernel, n_sub, n_row), name=f'sum_{c...  47.1 us
    pallas_call x1, Pallas kernels, sum_beside_exchange(): pl.pallas_call(functools.partial(sum_beside_exchange_kernel, ny, nx, n_su...  32.7 us
    pallas_call x1, Pallas kernels, ring_gather(): pl.pallas_call(functools.partial(rings_kernel, ny, nx), name=f'rings_{col...  25.9 us

profile of v4, /device:TPU:1, one launch (start us, length us, event | category | flops | bytes accessed | tf_op | source)
XLA Modules:
  0.0 267.3 jit_solution(3340386262096701480)
XLA Ops:
  0.6 0.7 fusion.5
  1.3 3.3 %copy.12 = bf16[1,1,96,64,64]{4,3,2,1,0:T(8,128)(2,1)S(1)} copy(bf16[1,1,96,64,64]{2,4,3,1,0:T(8,128)(2,1)} %param.15) | data formatting | bytes 1572864 | tf_op args[5]
  4.6 0.3 fusion.6
  4.9 0.2 fusion.1
  5.1 0.2 fusion
  5.3 0.4 pad_maximum_fusion.own_val
  5.7 25.9 %rings_6.1 = (s32[16,8,128]{2,1,0:T(8,128)S(1)}, bf16[4,1536,128]{2,1,0:T(8,128)(2,1)S(1)}, bf16[4,1152,128]{2,1,0:T(8,128)(2,1)S(1)}) custom-call(s32[8,128]{1,0:T(8,128)S(1)} %pad.4.codes, bf16[1536,128]{1,0:T(8,128)(2,1)S(1)} %bitcast.54, bf16[1152,128]{1,0:T(8,128)(2,1)S(1)} %bitcast.56), custom_call_target="tpu_custom_call" | custom-call | tf_op jit(solution)/shard_map/rings_6/pallas_call | solution.py:318
  31.7 0.0 copy-start
  31.7 0.0 copy-start.1
  31.7 0.0 copy-start.2
  31.7 0.0 copy-start.3
  31.7 0.0 copy-start.4
  31.7 0.0 copy-start.5
  31.7 0.0 copy-start.6
  31.7 2.0 select.2
  33.7 0.0 copy-done
  33.7 0.0 copy-done.1
  33.7 0.0 copy-done.2
  33.8 0.0 copy-done.3
  33.8 0.0 copy-done.4
  33.8 0.0 copy-done.5
  33.8 0.0 copy-done.6
  33.8 2.3 start.1
  36.1 0.0 copy-start.7
  36.1 0.0 copy-start.8
  36.1 46.9 %exchange_0.1 = (f32[16,384,128]{2,1,0:T(8,128)S(1)}, bf16[4,48,32,128]{3,2,1,0:T(8,128)(2,1)S(1)}, bf16[4,36,32,128]{3,2,1,0:T(8,128)(2,1)S(1)}, f32[16,3,32,128]{3,2,1,0:T(8,128)S(1)}, f32[8,3,32,128]{3,2,1,0:T(8,128)S(1)}) custom-call(f32[384,128]{1,0:T(8,128)S(1)} %bitcast.57, bf16[5,48,32,128]{3,2,1,0:T(8,128)(2,1)S(1)} %bitcast.45, ...), custom_call_target="tpu_custom_call" | custom-call | tf_op jit(solution)/shard_map/exchange_0/pallas_call | solution.py:265
  83.0 0.0 copy-done.7
  83.0 0.0 copy-done.8
  83.0 5.3 %build.1 = (bf16[12,128,512]{2,1,0:T(8,128)(2,1)S(1)}, s32[192]{0:T(256)S(1)}) custom-call(s32[1,1,96]{2,1,0:T(1,128)S(1)} %copy-done.7, s32[1,1,96]{2,1,0:T(1,128)S(1)} %copy-done.8, s32[16,128]{1,0:T(8,128)S(1)} %get-tuple-element.54.back_at, s32[1,1,12]{2,1,0:T(1,128)S(1)} %copy-done.4, s32[1,1,12]{2,1,0:T(1,128)S(1)} %copy-done.5, ...), custom_call_target="tpu_custom_call" | custom-call | tf_op jit(solution)/shard_map/build/pallas_call | solution.py:917
  88.3 3.4 %first_apply.1 = (f32[768,128]{1,0:T(8,128)S(1)}, f32[128,128]{1,0:T(8,128)S(1)}) custom-call(s32[192]{0:T(256)S(1)} %get-tuple-element.62.col_at, s32[1,1,3]{2,1,0:T(1,128)S(1)} %copy-done.3, bf16[12,128,512]{2,1,0:T(8,128)(2,1)S(1)} %get-tuple-element.63.rows_ref, f32[12,32,128]{2,1,0:T(8,128)S(1)} %get-tuple-element.57.own, ...), custom_call_target="tpu_custom_call" | custom-call | tf_op jit(solution)/shard_map/first_apply/pallas_call | solution.py:846
  91.8 32.7 %sum_beside_exchange_1.1 = (f32[16,8,128]{2,1,0:T(8,128)S(1)}, f32[16,384,128]{2,1,0:T(8,128)S(1)}, f32[16,3,32,128]{3,2,1,0:T(8,128)S(1)}, f32[8,3,32,128]{3,2,1,0:T(8,128)S(1)}) custom-call(f32[16,8,128]{2,1,0:T(8,128)S(1)} %bitcast.68, f32[384,128]{1,0:T(8,128)S(1)} %bitcast.60, f32[3,32,128]{2,1,0:T(8,128)S(1)} %get-tuple-element.70.bnd, ...), custom_call_target="tpu_custom_call" | custom-call | tf_op jit(solution)/shard_map/sum_beside_exchange_1/pallas_call | solution.py:438
  124.5 5.4 %first_ritz.1 = (f32[768,128]{1,0:T(8,128)S(1)}, f32[12,32,128]{2,1,0:T(8,128)S(1)}, f32[3,32,128]{2,1,0:T(8,128)S(1)}, f32[2,8,3,32,128]{4,3,2,1,0:T(8,128)S(1)}) custom-call(s32[1,1,3]{2,1,0:T(1,128)S(1)} %copy-done.3, s32[1,1,12]{2,1,0:T(1,128)S(1)} %copy-done.4, s32[1,1,12]{2,1,0:T(1,128)S(1)} %copy-done.5, f32[128,128]{1,0:T(8,128)S(1)} %bitcast.67, ...), custom_call_target="tpu_custom_call" | custom-call | tf_op jit(solution)/shard_map/first_ritz/pallas_call | solution.py:846
  129.9 28.8 %exchange_2.1 = (f32[16,384,128]{2,1,0:T(8,128)S(1)}, f32[16,3,32,128]{3,2,1,0:T(8,128)S(1)}, f32[8,3,32,128]{3,2,1,0:T(8,128)S(1)}) custom-call(f32[384,128]{1,0:T(8,128)S(1)} %bitcast.61, f32[3,32,128]{2,1,0:T(8,128)S(1)} %get-tuple-element.76.args_1_, f32[2,8,3,32,128]{4,3,2,1,0:T(8,128)S(1)} %get-tuple-element.77.args_2_), custom_call_target="tpu_custom_call" | custom-call | tf_op jit(solution)/shard_map/exchange_2/pallas_call | solution.py:265
  158.7 6.6 %apply_0.1 = (f32[768,128]{1,0:T(8,128)S(1)}, f32[384,128]{1,0:T(8,128)S(1)}) custom-call(s32[192]{0:T(256)S(1)} %get-tuple-element.62.col_at, s32[1,1,3]{2,1,0:T(1,128)S(1)} %copy-done.3, bf16[12,128,512]{2,1,0:T(8,128)(2,1)S(1)} %get-tuple-element.63.rows_ref, f32[12,32,128]{2,1,0:T(8,128)S(1)} %get-tuple-element.75.own, f32[16,12,32,128]{3,2,1,0:T(8,128)S(1)} %bitcast.51, ...), custom_call_target="tpu_custom_call" | custom-call | tf_op jit(solution)/shard_map/apply_0/pallas_call | solution.py:846
  165.3 23.2 %sum_3.1 = f32[16,24,128]{2,1,0:T(8,128)S(1)} custom-call(f32[16,24,128]{2,1,0:T(8,128)S(1)} %bitcast.63), custom_call_target="tpu_custom_call" | custom-call | tf_op jit(solution)/shard_map/sum_3/pallas_call | solution.py:408
  188.5 16.6 %step.1 = (f32[64,128]{1,0:T(8,128)S(1)}, f32[768,128]{1,0:T(8,128)S(1)}, f32[768,128]{1,0:T(8,128)S(1)}, f32[768,128]{1,0:T(8,128)S(1)}, bf16[12,32,128]{2,1,0:...) custom-call(s32[1,1,3]{2,1,0:T(1,128)S(1)} %copy-done.3, ...), custom_call_target="tpu_custom_call" | custom-call | tf_op jit(solution)/shard_map/step/pallas_call | solution.py:846
  205.1 18.9 %exchange_4.1 = (bf16[16,384,128]{2,1,0:T(8,128)(2,1)S(1)}, bf16[16,3,32,128]{3,2,1,0:T(8,128)(2,1)S(1)}, f32[8,3,32,128]{3,2,1,0:T(8,128)S(1)}) custom-call(bf16[384,128]{1,0:T(8,128)(2,1)S(1)} %bitcast.62, bf16[3,32,128]{2,1,0:T(8,128)(2,1)S(1)} %get-tuple-element.88.args_1_, f32[2,8,3,32,128]{4,3,2,1,0:T(8,128)S(1)} %get-tuple-element.89.args_2_), custom_call_target="tpu_custom_call" | custom-call | tf_op jit(solution)/shard_map/exchange_4/pallas_call | solution.py:265
  224.1 4.4 %apply_1.1 = (f32[768,128]{1,0:T(8,128)}, f32[384,128]{1,0:T(8,128)S(1)}) custom-call(s32[192]{0:T(256)S(1)} %get-tuple-element.62.col_at, s32[1,1,3]{2,1,0:T(1,128)S(1)} %copy-done.3, bf16[12,128,512]{2,1,0:T(8,128)(2,1)S(1)} %get-tuple-element.63.rows_ref, bf16[12,32,128]{2,1,0:T(8,128)(2,1)S(1)} %get-tuple-element.87.own, ...), custom_call_target="tpu_custom_call" | custom-call | tf_op jit(solution)/shard_map/apply_1/pallas_call | solution.py:846
  228.4 23.8 %sum_5.1 = f32[16,24,128]{2,1,0:T(8,128)S(1)} custom-call(f32[16,24,128]{2,1,0:T(8,128)S(1)} %bitcast.64), custom_call_target="tpu_custom_call" | custom-call | tf_op jit(solution)/shard_map/sum_5/pallas_call | solution.py:408
  252.3 15.1 %last.1 = (f32[64,768]{1,0:T(8,128)}, f32[64,768]{1,0:T(8,128)}) custom-call(f32[384,128]{1,0:T(8,128)S(1)} %bitcast.59, f32[64,128]{1,0:T(8,128)S(1)} %get-tuple-element.97.metric, f32[768,128]{1,0:T(8,128)S(1)} %get-tuple-element.93.refs_0_.current, f32[768,128]{1,0:T(8,128)S(1)} %get-tuple-element.95.refs_2_.basis), custom_call_target="tpu_custom_call" | custom-call | tf_op jit(solution)/shard_map/last/pallas_call | solution.py:846
  (2 shorter events, 0.0 us)
Async XLA Ops:
  31.7 2.1 copy-start
  31.7 2.1 copy-start.1
  31.7 2.1 copy-start.2
  31.7 2.1 copy-start.3
  31.7 2.1 copy-start.4
  31.7 2.1 copy-start.5
  31.7 2.1 copy-start.6
  36.1 46.9 %copy-start.7 = (s32[1,1,96]{2,1,0:T(1,128)S(1)}, s32[1,1,96]{2,1,0:T(1,128)}, u32[]{:S(2)}) copy-start(s32[1,1,96]{2,1,0:T(1,128)} %in_row.1) | copy-start | bytes 1156
  36.1 46.9 %copy-start.8 = (s32[1,1,96]{2,1,0:T(1,128)S(1)}, s32[1,1,96]{2,1,0:T(1,128)}, u32[]{:S(2)}) copy-start(s32[1,1,96]{2,1,0:T(1,128)} %in_col.1) | copy-start | bytes 1156

commit v5 on v4

--- a/solution.py
+++ b/solution.py
@@ -330,7 +330,7 @@
     )(codes, early, late)
 
 
-def sum_steps(n_sub, n_row, parts, out, by_row, by_sub, own_sem, send, recv):
+def sum_steps(n_sub, n_row, make, parts, out, by_row, by_sub, own_sem, send, recv):
     sub, row = lax.axis_index("sub"), lax.axis_index("row")
     barrier = pltpu.get_barrier_semaphore()
 
@@ -342,6 +342,7 @@
     def _(d):
         pl.semaphore_signal(barrier, inc=1, device_id={"sub": (sub + d) % n_sub}, device_id_type=MESH)
 
+    make()
     pl.semaphore_wait(barrier, n_row - 1 + n_sub - 1)
 
     def phase(index, axis, mine, n, source, target):
@@ -386,8 +387,31 @@
     yield from phase(2, "row", row, n_row, lambda t: by_sub.at[n_sub], lambda t: out.at[t])
 
 
-def sum_kernel(*args):
-    for _ in sum_steps(*args):
+def gram_of(current, image_x, basis, image_b, diagonal=None):
+    y = basis[...]
+    turned = y.T
+    left = is_left(y.shape)
+    if diagonal is None:
+        energy = hdot(turned, image_b[...])
+    else:
+        twice = jnp.where(left, y + (y - y.astype(BF16).astype(F32)), 0.0)
+        energy = hdot(turned, jnp.where(left, diagonal[...], image_x[...])) + hdot(
+            twice.T, jnp.where(left, image_b[...], 0.0)
+        )
+    driving = hdot(turned, jnp.where(left, image_x[...], swap(current[...])))
+    return jnp.concatenate([energy, driving, hdot(turned, y)], 0)
+
+
+def sum_kernel(count, n_sub, n_row, *refs):
+    images, out, parts, scratch = refs[:count], refs[count], refs[count + 1], refs[count + 2 :]
+    rows = parts.shape[1]
+
+    def make():
+        gram = gram_of(*images)
+        for t in range(n_row):
+            parts[t] = gram[t * rows : (t + 1) * rows]
+
+    for _ in sum_steps(n_sub, n_row, make, parts, out, *scratch):
         pass
 
 
@@ -402,25 +426,24 @@
     ]
 
 
-def sum_all(collective_id, n_sub, n_row, part):
-    rows = part.shape[0] // n_row
-    shape = (n_row, rows, LANES)
+def sum_grams(collective_id, n_sub, n_row, images):
+    rows = 3 * LANES // n_row
     total = pl.pallas_call(
-        functools.partial(sum_kernel, n_sub, n_row),
+        functools.partial(sum_kernel, len(images), n_sub, n_row),
         name=f"sum_{collective_id}",
-        out_shape=jax.ShapeDtypeStruct(shape, F32),
-        in_specs=[VMEM],
+        out_shape=shape(n_row, rows, LANES),
+        in_specs=[VMEM] * len(images),
         out_specs=VMEM,
-        scratch_shapes=sum_scratch(n_sub, n_row, rows),
+        scratch_shapes=[pltpu.VMEM((n_row, rows, LANES), F32)] + sum_scratch(n_sub, n_row, rows),
         compiler_params=pltpu.CompilerParams(
-            collective_id=collective_id, has_side_effects=True, vmem_limit_bytes=SMALL
+            collective_id=collective_id, has_side_effects=True, vmem_limit_bytes=LIMIT
         ),
-    )(part.reshape(shape))
-    return total.reshape(part.shape)
+    )(*images)
+    return total.reshape(-1, LANES)
 
 
 def sum_beside_exchange_kernel(ny, nx, n_sub, part, shard, bnd, parts, total, group, bnd_all, landed, *scratch):
-    summing = sum_steps(n_sub, ny * nx, part, total, *scratch[:5])
+    summing = sum_steps(n_sub, ny * nx, lambda: None, part, total, *scratch[:5])
     moving = exchange_steps(
         False, 1, False, ny, nx, n_sub, shard, bnd, parts, group, bnd_all, landed, *scratch[5:]
     )
@@ -638,7 +661,7 @@
 
 
 def apply_kernel(coarse, col_at, bnd, rows_ref, own, group, bnd_all, landed, *refs):
-    *search, current, image_x, basis, image_b, gram, terms, diagonal = refs
+    *search, image_x, basis, image_b, diagonal, terms = refs if coarse else (*refs[:-1], None, refs[-1])
     left_block = is_left((KB, LANES))
     source = image_x
     if search:
@@ -660,23 +683,12 @@
     for q in range(IFR):
         at = block_at(bnd[0, 0, q])
         image_b[at, :] = image_b[at, :] + jnp.where(left_block, landed_blocks(1, landed, q)[0], 0.0)
-    y = basis[...]
-    turned = y.T
-    left = is_left(y.shape)
     if coarse:
         for a in range(LB):
-            own_terms = jnp.concatenate(two_terms(pack(y[a * KB : (a + 1) * KB])), 1)
+            own_terms = jnp.concatenate(two_terms(pack(basis[a * KB : (a + 1) * KB, :])), 1)
             product = jnp.dot(rows_ref[a, :, :HALF], own_terms, preferred_element_type=F32)
             both = add_terms(False, product, 0)
             diagonal[a * KB : (a + 1) * KB] = both[:KB] + swap(both[KB:])
-        twice = jnp.where(left, y + (y - y.astype(BF16).astype(F32)), 0.0)
-        gram[0:LANES] = hdot(turned, jnp.where(left, diagonal[...], image_x[...])) + hdot(
-            twice.T, jnp.where(left, image_b[...], 0.0)
-        )
-    else:
-        gram[0:LANES] = hdot(turned, image_b[...])
-    gram[LANES : 2 * LANES] = hdot(turned, jnp.where(left, image_x[...], swap(current[...])))
-    gram[2 * LANES :] = hdot(turned, y)
 
 
 def eliminate(work, n, full):
@@ -961,15 +973,12 @@
     for sweep in range(ITERS):
         group, bnd_all, landed = exchange(2 + 2 * sweep, ny, nx, [packed.reshape(-1, LANES)], [], bnd, parts)
         coarse = sweep == ITERS - 1
-        image_b, gram = plain(
+        images = plain(
             functools.partial(apply_kernel, coarse),
             f"apply_{sweep}",
-            [SMEM] * 2 + [VMEM] * (12 if sweep == 0 else 8),
-            [shape(rows_here, LANES), shape(3 * LANES, LANES)],
-            [
-                pltpu.VMEM((blocks_all, HALF, LANES if coarse else 2 * LANES), BF16),
-                pltpu.VMEM((rows_here, LANES), F32),
-            ],
+            [SMEM] * 2 + [VMEM] * (11 if sweep == 0 else 7),
+            [shape(rows_here, LANES)] * (2 if coarse else 1),
+            [pltpu.VMEM((blocks_all, HALF, LANES if coarse else 2 * LANES), BF16)],
             col_at,
             bnd_rows,
             block_rows,
@@ -978,11 +987,11 @@
             bnd_all,
             landed,
             *((shard_p, group_p.reshape(n_row, LB, HALF, LANES), bnd_p, landed_p) if sweep == 0 else ()),
-            current,
             image_x,
             basis,
         )
-        gram = sum_all(3 + 2 * sweep, n_sub, n_row, gram)
+        image_b = images[0]
+        gram = sum_grams(3 + 2 * sweep, n_sub, n_row, [current, image_x, basis, *images])
         if sweep < ITERS - 1:
             metric, current, image_x, basis, packed, bnd, parts = plain(
                 functools.partial(step_kernel, total_rows),

time: 267 us -> 264 us (0.989)
  Pallas kernels: 261 us -> 258 us
    pallas_call x8, Pallas kernels: 55.7 us -> 52.7 us  [plain(): pl.pallas_call(kernel, name=name, out_shape=outs, in_specs=specs, out_spe...]
where the time goes in v5:
time: 264 us
  Pallas kernels  258 us (98%)
  local copies, waits for them, and re-layouts  3.6 us (1%)
    pallas_call x3, Pallas kernels, exchange(): pl.pallas_call(functools.partial(exchange_kernel, count, bool(handed), ny...  94.2 us
    pallas_call x8, Pallas kernels, plain(): pl.pallas_call(kernel, name=name, out_shape=outs, in_specs=specs, out_spe...  52.7 us
    pallas_call x2, Pallas kernels, sum_grams(): pl.pallas_call(functools.partial(sum_kernel, len(images), n_sub, n_row),...  47.5 us
    pallas_call x1, Pallas kernels, sum_beside_exchange(): pl.pallas_call(functools.partial(sum_beside_exchange_kernel, ny, nx, n_su...  32.7 us
    pallas_call x1, Pallas kernels, ring_gather(): pl.pallas_call(functools.partial(rings_kernel, ny, nx), name=f'rings_{col...  25.9 us
    pallas_call x1, Pallas kernels, local(): pl.pallas_call(functools.partial(build_kernel, ny, nx), name='build', out...  5.28 us

profile of v5, /device:TPU:1, one launch (start us, length us, event | category | flops | bytes accessed | tf_op | source)
XLA Modules:
  0.0 264.4 jit_solution(11810871804578497400)
XLA Ops:
  0.6 0.7 fusion.5
  1.3 3.3 %copy.12 = bf16[1,1,96,64,64]{4,3,2,1,0:T(8,128)(2,1)S(1)} copy(bf16[1,1,96,64,64]{2,4,3,1,0:T(8,128)(2,1)} %param.15) | data formatting | bytes 1572864 | tf_op args[5]
  4.6 0.3 fusion.6
  4.9 0.2 fusion.1
  5.1 0.2 fusion
  5.3 0.4 pad_maximum_fusion.own_val
  5.7 25.9 %rings_6.1 = (s32[16,8,128]{2,1,0:T(8,128)S(1)}, bf16[4,1536,128]{2,1,0:T(8,128)(2,1)S(1)}, bf16[4,1152,128]{2,1,0:T(8,128)(2,1)S(1)}) custom-call(s32[8,128]{1,0:T(8,128)S(1)} %pad.4.codes, bf16[1536,128]{1,0:T(8,128)(2,1)S(1)} %bitcast.52, bf16[1152,128]{1,0:T(8,128)(2,1)S(1)} %bitcast.54), custom_call_target="tpu_custom_call" | custom-call | tf_op jit(solution)/shard_map/rings_6/pallas_call | solution.py:318
  31.7 0.0 copy-start
  31.7 0.0 copy-start.1
  31.7 0.0 copy-start.2
  31.7 0.0 copy-start.3
  31.7 0.0 copy-start.4
  31.7 0.0 copy-start.5
  31.7 0.0 copy-start.6
  31.7 2.0 select.2
  33.7 0.0 copy-done
  33.7 0.0 copy-done.1
  33.7 0.0 copy-done.2
  33.8 0.0 copy-done.3
  33.8 0.0 copy-done.4
  33.8 0.0 copy-done.5
  33.8 0.0 copy-done.6
  33.8 2.3 start.1
  36.1 0.0 copy-start.7
  36.1 0.0 copy-start.8
  36.1 46.9 %exchange_0.1 = (f32[16,384,128]{2,1,0:T(8,128)S(1)}, bf16[4,48,32,128]{3,2,1,0:T(8,128)(2,1)S(1)}, bf16[4,36,32,128]{3,2,1,0:T(8,128)(2,1)S(1)}, f32[16,3,32,128]{3,2,1,0:T(8,128)S(1)}, f32[8,3,32,128]{3,2,1,0:T(8,128)S(1)}) custom-call(f32[384,128]{1,0:T(8,128)S(1)} %bitcast.55, bf16[5,48,32,128]{3,2,1,0:T(8,128)(2,1)S(1)} %bitcast.43, ...), custom_call_target="tpu_custom_call" | custom-call | tf_op jit(solution)/shard_map/exchange_0/pallas_call | solution.py:265
  83.0 0.0 copy-done.7
  83.0 0.0 copy-done.8
  83.0 5.3 %build.1 = (bf16[12,128,512]{2,1,0:T(8,128)(2,1)S(1)}, s32[192]{0:T(256)S(1)}) custom-call(s32[1,1,96]{2,1,0:T(1,128)S(1)} %copy-done.7, s32[1,1,96]{2,1,0:T(1,128)S(1)} %copy-done.8, s32[16,128]{1,0:T(8,128)S(1)} %get-tuple-element.54.back_at, s32[1,1,12]{2,1,0:T(1,128)S(1)} %copy-done.4, s32[1,1,12]{2,1,0:T(1,128)S(1)} %copy-done.5, ...), custom_call_target="tpu_custom_call" | custom-call | tf_op jit(solution)/shard_map/build/pallas_call | solution.py:929
  88.3 3.4 %first_apply.1 = (f32[768,128]{1,0:T(8,128)S(1)}, f32[128,128]{1,0:T(8,128)S(1)}) custom-call(s32[192]{0:T(256)S(1)} %get-tuple-element.62.col_at, s32[1,1,3]{2,1,0:T(1,128)S(1)} %copy-done.3, bf16[12,128,512]{2,1,0:T(8,128)(2,1)S(1)} %get-tuple-element.63.rows_ref, f32[12,32,128]{2,1,0:T(8,128)S(1)} %get-tuple-element.57.own, ...), custom_call_target="tpu_custom_call" | custom-call | tf_op jit(solution)/shard_map/first_apply/pallas_call | solution.py:858
  91.8 32.7 %sum_beside_exchange_1.1 = (f32[16,8,128]{2,1,0:T(8,128)S(1)}, f32[16,384,128]{2,1,0:T(8,128)S(1)}, f32[16,3,32,128]{3,2,1,0:T(8,128)S(1)}, f32[8,3,32,128]{3,2,1,0:T(8,128)S(1)}) custom-call(f32[16,8,128]{2,1,0:T(8,128)S(1)} %bitcast.64, f32[384,128]{1,0:T(8,128)S(1)} %bitcast.58, f32[3,32,128]{2,1,0:T(8,128)S(1)} %get-tuple-element.70.bnd, ...), custom_call_target="tpu_custom_call" | custom-call | tf_op jit(solution)/shard_map/sum_beside_exchange_1/pallas_call | solution.py:461
  124.5 5.4 %first_ritz.1 = (f32[768,128]{1,0:T(8,128)S(1)}, f32[12,32,128]{2,1,0:T(8,128)S(1)}, f32[3,32,128]{2,1,0:T(8,128)S(1)}, f32[2,8,3,32,128]{4,3,2,1,0:T(8,128)S(1)}) custom-call(s32[1,1,3]{2,1,0:T(1,128)S(1)} %copy-done.3, s32[1,1,12]{2,1,0:T(1,128)S(1)} %copy-done.4, s32[1,1,12]{2,1,0:T(1,128)S(1)} %copy-done.5, f32[128,128]{1,0:T(8,128)S(1)} %bitcast.63, ...), custom_call_target="tpu_custom_call" | custom-call | tf_op jit(solution)/shard_map/first_ritz/pallas_call | solution.py:858
  129.9 28.6 %exchange_2.1 = (f32[16,384,128]{2,1,0:T(8,128)S(1)}, f32[16,3,32,128]{3,2,1,0:T(8,128)S(1)}, f32[8,3,32,128]{3,2,1,0:T(8,128)S(1)}) custom-call(f32[384,128]{1,0:T(8,128)S(1)} %bitcast.59, f32[3,32,128]{2,1,0:T(8,128)S(1)} %get-tuple-element.76.args_1_, f32[2,8,3,32,128]{4,3,2,1,0:T(8,128)S(1)} %get-tuple-element.77.args_2_), custom_call_target="tpu_custom_call" | custom-call | tf_op jit(solution)/shard_map/exchange_2/pallas_call | solution.py:265
  158.5 5.4 %apply_0.1.refs_3_.image_b = f32[768,128]{1,0:T(8,128)S(1)} custom-call(s32[192]{0:T(256)S(1)} %get-tuple-element.62.col_at, s32[1,1,3]{2,1,0:T(1,128)S(1)} %copy-done.3, bf16[12,128,512]{2,1,0:T(8,128)(2,1)S(1)} %get-tuple-element.63.rows_ref, f32[12,32,128]{2,1,0:T(8,128)S(1)} %get-tuple-element.75.own, f32[16,12,32,128]{3,2,1,0:T(8,128)S(1)} %bitcast.49, ...), custom_call_target="tpu_custom_call" | custom-call | tf_op jit(solution)/shard_map/apply_0/pallas_call | solution.py:858
  164.0 23.3 %sum_3.1 = f32[16,24,128]{2,1,0:T(8,128)S(1)} custom-call(f32[768,128]{1,0:T(8,128)S(1)} %get-tuple-element.50.basis.current.refs_0_, f32[768,128]{1,0:T(8,128)S(1)} %get-tuple-element.67.image_x.refs_4_.refs_1_, f32[768,128]{1,0:T(8,128)S(1)} %get-tuple-element.74.refs_5_.refs_2_.basis, f32[768,128]{1,0:T(8,128)S(1)} %apply_0.1.refs_3_.image_b), custom_call_target="tpu_custom_call" | custom-call | tf_op jit(solution)/shard_map/sum_3/pallas_call | solution.py:431
  187.2 16.6 %step.1 = (f32[64,128]{1,0:T(8,128)S(1)}, f32[768,128]{1,0:T(8,128)S(1)}, f32[768,128]{1,0:T(8,128)S(1)}, f32[768,128]{1,0:T(8,128)S(1)}, bf16[12,32,128]{2,1,0:...) custom-call(s32[1,1,3]{2,1,0:T(1,128)S(1)} %copy-done.3, ...), custom_call_target="tpu_custom_call" | custom-call | tf_op jit(solution)/shard_map/step/pallas_call | solution.py:858
  203.8 18.7 %exchange_4.1 = (bf16[16,384,128]{2,1,0:T(8,128)(2,1)S(1)}, bf16[16,3,32,128]{3,2,1,0:T(8,128)(2,1)S(1)}, f32[8,3,32,128]{3,2,1,0:T(8,128)S(1)}) custom-call(bf16[384,128]{1,0:T(8,128)(2,1)S(1)} %bitcast.60, bf16[3,32,128]{2,1,0:T(8,128)(2,1)S(1)} %get-tuple-element.88.args_1_, f32[2,8,3,32,128]{4,3,2,1,0:T(8,128)S(1)} %get-tuple-element.89.args_2_), custom_call_target="tpu_custom_call" | custom-call | tf_op jit(solution)/shard_map/exchange_4/pallas_call | solution.py:265
  222.5 2.6 apply_1.1
  225.1 24.2 %sum_5.1 = f32[16,24,128]{2,1,0:T(8,128)S(1)} custom-call(f32[768,128]{1,0:T(8,128)S(1)} %get-tuple-element.84.refs_0_.current, f32[768,128]{1,0:T(8,128)S(1)} %get-tuple-element.85.refs_0_.refs_1_, f32[768,128]{1,0:T(8,128)S(1)} %get-tuple-element.86.refs_1_.refs_2_.basis, f32[768,128]{1,0:T(8,128)S(1)} %get-tuple-element.93.refs_3_, ...), custom_call_target="tpu_custom_call" | custom-call | tf_op jit(solution)/shard_map/sum_5/pallas_call | solution.py:431
  249.3 15.1 %last.1 = (f32[64,768]{1,0:T(8,128)}, f32[64,768]{1,0:T(8,128)}) custom-call(f32[384,128]{1,0:T(8,128)S(1)} %bitcast.57, f32[64,128]{1,0:T(8,128)S(1)} %get-tuple-element.95.metric, f32[768,128]{1,0:T(8,128)S(1)} %get-tuple-element.84.refs_0_.current, f32[768,128]{1,0:T(8,128)S(1)} %get-tuple-element.86.refs_1_.refs_2_.basis), custom_call_target="tpu_custom_call" | custom-call | tf_op jit(solution)/shard_map/last/pallas_call | solution.py:858
  (2 shorter events, 0.0 us)
Async XLA Ops:
  31.7 2.1 copy-start
  31.7 2.1 copy-start.1
  31.7 2.1 copy-start.2
  31.7 2.1 copy-start.3
  31.7 2.1 copy-start.4
  31.7 2.1 copy-start.5
  31.7 2.1 copy-start.6
  36.1 46.9 %copy-start.7 = (s32[1,1,96]{2,1,0:T(1,128)S(1)}, s32[1,1,96]{2,1,0:T(1,128)}, u32[]{:S(2)}) copy-start(s32[1,1,96]{2,1,0:T(1,128)} %in_row.1) | copy-start | bytes 1156
  36.1 46.9 %copy-start.8 = (s32[1,1,96]{2,1,0:T(1,128)S(1)}, s32[1,1,96]{2,1,0:T(1,128)}, u32[]{:S(2)}) copy-start(s32[1,1,96]{2,1,0:T(1,128)} %in_col.1) | copy-start | bytes 1156
